TPU v7x, 32 devices: a whole 2x2x4 slice. The times are simulated.
32 devices in a mesh: tm: 8 (over z, y), site: 4 (over x, core).
Axes of the slice: x: 2, y: 2, z: 4, core: 2. Of those that a mesh axis runs over, the one named last changes fastest.
Arguments:
- obs_rows: bfloat16 [16384, 256], P(('tm', 'site')), may hold values from -2 to 2
- obs_values: bfloat16 [16384], P(('tm', 'site')), may hold values from -6 to 6
- obs_hours: int32 [16384], P(('tm', 'site')), may hold values from 0 to 3
- prior_precision: float32 [256, 256], replicated, may hold values from -1 to 3, as said below
- transition: float32 [256, 256], replicated, may hold values from -1 to 1
- site_basis: bfloat16 [131072, 256], P(('tm', 'site')), may hold values from -0.375 to 0.375
Outputs:
- prediction: bfloat16 [32, 131072], P(None, ('tm', 'site'))
Inputs may be any that keep to these rules, and one draw needn't show every extreme that they name: `prior_precision`: symmetric and positive definite.
All inputs are finite; a program needn't handle non-finite values. Where the computation divides by a largest or mean magnitude, that divisor is 1e-20 or more.
Results may differ from a plain program's by a relative error of at most 0.0049.
Values may be sent and summed in bfloat16 or wider, within the bound.
No kernel may reach another device: no remote copies, remote signals or barrier semaphores. Data moves between devices by JAX's collectives and lax.ppermute only.
A program may use at most 64 MiB of HBM per device.

v0:
```python
import jax
import jax.numpy as jnp
from jax import lax
from jax.sharding import PartitionSpec as P

NS_ITERS = 8


def entering(part, axis, combine, identity):
    place = lax.axis_index(axis)
    gathered = jax.tree.map(lambda a: lax.all_gather(a, axis), part)
    state = jax.tree.map(lambda a, e: jnp.zeros_like(a) + jnp.asarray(e, a.dtype), part, identity)

    def one(turn, state):
        return combine(
            state, jax.tree.map(lambda a: lax.dynamic_index_in_dim(a, turn, 0, False), gathered)
        )

    return lax.fori_loop(0, place, one, state)


def approx_inverse(precisions):
    states = precisions.shape[-1]
    bounds = jnp.max(jnp.sum(jnp.abs(precisions), axis=2), axis=1)
    identity = jnp.eye(states, dtype=jnp.float32)
    inverse = identity[None] / bounds[:, None, None]
    for iteration in range(NS_ITERS):
        product = jnp.einsum("hij,hjk->hik", precisions, inverse, precision=lax.Precision.HIGHEST)
        inverse = jnp.einsum(
            "hij,hjk->hik", inverse, 2.0 * identity - product, precision=lax.Precision.HIGHEST
        )
    return inverse


def compose(earlier, latter):
    joined_map = jnp.dot(latter[0], earlier[0], precision=lax.Precision.HIGHEST)
    joined_shift = jnp.dot(latter[0], earlier[1], precision=lax.Precision.HIGHEST) + latter[1]
    return (joined_map, joined_shift)


def hour_elements(summed_grams, drives, prior_precision, coupled):
    inverse = approx_inverse(prior_precision[None] + summed_grams)
    hour_maps = jnp.einsum("hij,jk->hik", inverse, coupled, precision=lax.Precision.HIGHEST)
    offsets = jnp.einsum("hij,hj->hi", inverse, drives, precision=lax.Precision.HIGHEST)
    return (hour_maps, offsets)


def body(obs_rows, obs_values, obs_hours, prior_precision, transition, site_basis):
    blocks = lax.axis_size("site")
    own_hour = lax.axis_index("site")
    hour_codes = obs_hours.astype(jnp.bfloat16)
    block_feats, block_values, block_codes = (
        lax.all_gather(obs_rows, "site", axis=0, tiled=True),
        lax.all_gather(obs_values, "site", axis=0, tiled=True),
        lax.all_gather(hour_codes, "site", axis=0, tiled=True),
    )
    mine = block_codes == own_hour.astype(jnp.bfloat16)
    masked = jnp.where(mine[:, None], block_feats, jnp.zeros((), jnp.bfloat16))
    summed_grams = jnp.einsum("rs,rt->st", masked, block_feats, preferred_element_type=jnp.float32)[
        None
    ]
    weighted = jnp.where(mine, block_values, jnp.zeros((), jnp.bfloat16))
    drives = jnp.einsum("r,rs->s", weighted, block_feats, preferred_element_type=jnp.float32)[None]
    coupled = jnp.dot(prior_precision, transition, precision=lax.Precision.HIGHEST)
    states = transition.shape[0]
    identity = jnp.eye(states, dtype=jnp.float32)
    zero_state = jnp.zeros((states,), jnp.float32)
    hour_maps, offsets = hour_elements(summed_grams, drives, prior_precision, coupled)
    block_maps, block_offsets = (
        lax.all_gather(hour_maps, "site", axis=0, tiled=True),
        lax.all_gather(offsets, "site", axis=0, tiled=True),
    )
    joined = (block_maps[0], block_offsets[0])
    for position in range(1, blocks):
        joined = compose(joined, (block_maps[position], block_offsets[position]))
    before = entering(joined, "tm", compose, (identity, zero_state))
    state_mean = before[1]
    results = []
    for position in range(blocks):
        state_mean = (
            jnp.dot(block_maps[position], state_mean, precision=lax.Precision.HIGHEST)
            + block_offsets[position]
        )
        results.append(state_mean)
    rounded = jnp.stack(results).astype(jnp.bfloat16)
    return jnp.einsum(
        "hs,ns->hn",
        lax.all_gather(rounded, "tm", axis=0, tiled=True),
        site_basis,
        preferred_element_type=jnp.float32,
    ).astype(jnp.bfloat16)


def solution(mesh):
    in_specs = (
        P(("tm", "site"), None),
        P(("tm", "site")),
        P(("tm", "site")),
        P(),
        P(),
        P(("tm", "site"), None),
    )
    out_specs = P(None, ("tm", "site"))
    return jax.shard_map(body, mesh=mesh, in_specs=in_specs, out_specs=out_specs, check_vma=False)
```

profile of v0, /device:TPU:0, one launch (start us, length us, event | category | flops | bytes accessed | tf_op | source)
XLA Modules:
  0.0 154.3 jit_solution(9217139668701592832)
XLA Ops:
  6.5 0.0 copy-start
  6.5 0.0 all-gather.13.cloned.1.call-start
  6.5 0.7 all-gather.13.cloned.1.call-update
  7.3 0.0 all-gather.15.cloned.1.call-start
  7.3 0.7 convert_element_type.15
  8.0 6.1 %all-gather.4 = bf16[4,1,512]{2,1,0:T(2,128)(2,1)S(1)} all-gather(bf16[1,1,512]{2,1,0:T(2,128)(2,1)S(1)} %reshape.126), channel_id=1, replica_groups=mesh['tm'=8,'site'=4] {'site'}, dimensions={0}, use_global_device_ids=true | all-gather | bytes 5120 | tf_op jit(solution)/shard_map/all_gather | solution.py:55
  14.2 1.1 copy.9
  15.2 1.4 fusion.55
  16.7 11.7 %all-gather.13.cloned.1.call-done = bf16[2048,256]{1,0:T(8,128)(2,1)} async-done(((bf16[512,256]{1,0:T(8,128)(2,1)}), bf16[2048,256]{1,0:T(8,128)(2,1)}) %all-gather.13.cloned.1.call-update) | async-done | bytes 1048592 | tf_op jit(solution)/shard_map/all_gather | solution.py:53
  28.4 2.4 %abs_reduce_fusion = (f32[256]{0:T(256)S(1)}, f32[256,256]{0,1:T(8,128)S(1)}) fusion(f32[256,256]{0,1:T(8,128)S(1)} %copy.9, bf16[2048,256]{1,0:T(8,128)(2,1)} %all-gather.13.cloned.1.call-done, pred[2048]{0:T(1024)(128)(4,1)S(1)} %bitcast.119), kind=kOutput, calls=%fused_computation.24 | convolution fusion | flops 269156096 | bytes 1575936 | tf_op jit(solution)/shard_map/rs,rt->st/dot_general | solution.py:59
  30.8 0.6 reduce_max.9
  32.1 0.6 convolution_subtract_fusion.7
  32.7 0.4 fusion.11
  33.1 0.6 convolution_subtract_fusion.6
  33.7 0.4 fusion.48
  34.1 0.6 convolution_subtract_fusion.5
  34.7 0.4 fusion.49
  35.0 0.6 convolution_subtract_fusion.4
  35.7 0.4 fusion.50
  36.0 0.6 convolution_subtract_fusion.3
  36.6 0.4 fusion.51
  37.0 0.6 convolution_subtract_fusion.2
  37.6 0.4 fusion.52
  38.0 0.6 convolution_subtract_fusion.1
  38.6 0.4 fusion.53
  39.0 0.6 convolution_subtract_fusion
  39.6 0.0 copy-start.2
  39.6 0.4 fusion.54
  40.0 1.1 fusion.56
  41.1 0.0 all-gather.15.cloned.1.call-update
  41.1 0.0 all-gather.17.cloned.1.call-start
  41.2 16.8 %all-gather.15.cloned.1.call-done = f32[1024,256]{1,0:T(8,128)} async-done(((f32[256,256]{1,0:T(8,128)}), f32[1024,256]{1,0:T(8,128)}) %all-gather.15.cloned.1.call-update) | async-done | bytes 1048592 | tf_op jit(solution)/shard_map/all_gather | solution.py:70
  58.0 0.0 copy-start.1
  58.0 1.5 fusion.14
  59.5 1.3 fusion.25
  60.9 2.0 %fusion.31 = f32[256,256]{1,0:T(8,128)} fusion(f32[256,256]{1,0:T(8,128)S(1)} %fusion.25, f32[1024,256]{1,0:T(8,128)} %all-gather.15.cloned.1.call-done), kind=kOutput, calls=%fused_computation.43 | convolution fusion | flops 201326592 | bytes 786432 | tf_op jit(solution)/shard_map/dot_general | solution.py:36
  62.9 0.0 all-gather.17.cloned.1.call-update
  62.9 0.0 copy-done.2
  62.9 5.2 %all-gather.5 = bf16[4,1,512]{2,1,0:T(2,128)(2,1)S(1)} all-gather(bf16[1,1,512]{2,1,0:T(2,128)(2,1)S(1)} %reshape.128), channel_id=1, replica_groups=mesh['tm'=8,'site'=4] {'site'}, dimensions={0}, use_global_device_ids=true | all-gather | bytes 5120 | tf_op jit(solution)/shard_map/all_gather | solution.py:54
  68.2 1.5 convolution_bitcast_fusion
  69.7 0.3 convolution_bitcast_fusion.1
  69.9 5.1 %all-gather.6 = f32[4,1,256]{2,1,0:T(1,128)S(1)} all-gather(f32[1,1,256]{2,1,0:T(1,128)S(1)} %convolution_bitcast_fusion.1), channel_id=4, replica_groups=mesh['tm'=8,'site'=4] {'site'}, dimensions={0}, use_global_device_ids=true | all-gather | bytes 5120 | tf_op jit(solution)/shard_map/all_gather | solution.py:71
  75.0 0.0 copy-done.1
  75.0 0.3 fusion.18
  75.3 0.3 fusion.23
  75.7 0.3 fusion.29
  76.0 20.6 %all-gather.7 = f32[8,1,256]{2,1,0:T(1,128)S(1)} all-gather(f32[1,1,256]{2,1,0:T(1,128)S(1)} %bitcast.134), channel_id=5, replica_groups=mesh['tm'=8,'site'=4] {'tm'}, dimensions={0}, use_global_device_ids=true | all-gather | bytes 9216 | tf_op jit(solution)/shard_map/all_gather | solution.py:11
  96.6 15.8 %all-gather.17.cloned.1.call-done = f32[2048,256]{1,0:T(8,128)} async-done(((f32[256,256]{1,0:T(8,128)}), f32[2048,256]{1,0:T(8,128)}) %all-gather.17.cloned.1.call-update) | async-done | bytes 2097168 | tf_op jit(solution)/shard_map/all_gather | solution.py:11
  112.4 0.3 fusion.16
  112.7 0.3 fusion.21
  113.1 0.3 fusion.27
  113.4 0.3 fusion.33
  113.8 32.5 %all-gather.8 = bf16[8,4,256]{2,1,0:T(4,128)(2,1)S(1)} all-gather(bf16[1,4,256]{2,1,0:T(4,128)(2,1)S(1)} %maximum_bitcast_fusion), channel_id=1, replica_groups=mesh['tm'=8,'site'=4] {'tm'}, dimensions={0}, use_global_device_ids=true | all-gather | bytes 18432 | tf_op jit(solution)/shard_map/all_gather | solution.py:88
  146.3 0.0 copy-done
  146.3 1.4 convolution_convert_fusion
  (25 shorter events, 0.2 us)
Async XLA Ops:
  6.5 139.8 %copy-start = (bf16[4096,256]{1,0:T(8,128)(2,1)S(1)}, bf16[4096,256]{1,0:T(8,128)(2,1)}, u32[]{:S(2)}) copy-start(bf16[4096,256]{1,0:T(8,128)(2,1)} %param.13) | copy-start | bytes 6291460
  6.5 21.8 %all-gather.13.cloned.1.call-start = ((), (), s32[]{:S(2)}) async-start(), calls=%async_computation | async-start | bytes 1310720 | tf_op jit(solution)/shard_map/all_gather | solution.py:53
  7.3 50.8 %all-gather.15.cloned.1.call-start = ((), (), s32[]{:S(2)}) async-start(), calls=%async_computation.1 | async-start | bytes 1310720 | tf_op jit(solution)/shard_map/all_gather | solution.py:70
  39.6 23.3 %copy-start.2 = (bf16[512]{0:T(512)(128)(2,1)S(1)}, bf16[512]{0:T(512)(128)(2,1)}, u32[]{:S(2)}) copy-start(bf16[512]{0:T(512)(128)(2,1)} %param.9) | copy-start | bytes 3076
  41.1 71.3 %all-gather.17.cloned.1.call-start = ((), (), s32[]{:S(2)}) async-start(), calls=%async_computation.2 | async-start | bytes 2359296 | tf_op jit(solution)/shard_map/all_gather | solution.py:11
  58.0 17.0 %copy-start.1 = (f32[1024,256]{1,0:T(8,128)S(1)}, f32[1024,256]{1,0:T(8,128)}, u32[]{:S(2)}) copy-start(f32[1024,256]{1,0:T(8,128)} %all-gather.15.cloned.1.call-done) | copy-start | bytes 3145732
Sparse Core Ops, SparseCore 0:
  8.9 19.4 all-gather.12
  41.3 16.7 all-gather.14
  63.0 49.3 all-gather.16
where the time goes:
time: 155 us; the launch traced here: 154 us
  blocking collectives  69.4 us (45%)
  waiting for transfers between devices  45.1 us (29%)
  matrix products  22.8 us (15%)
  between operations  14.3 us (9%)
    all_gather x1, blocking collectives, body(): lax.all_gather(rounded, 'tm', axis=0, tiled=True)  32.5 us
    all_gather x1, blocking collectives, entering(): gathered = jax.tree.map(lambda a: lax.all_gather(a, axis), part)  20.6 us
    all_gather x1, waiting for transfers between devices, body(): lax.all_gather(hour_maps, 'site', axis=0, tiled=True)  16.8 us
    all_gather x1, waiting for transfers between devices, entering(): gathered = jax.tree.map(lambda a: lax.all_gather(a, axis), part)  15.8 us
    all_gather x1, waiting for transfers between devices, body(): lax.all_gather(obs_rows, 'site', axis=0, tiled=True)  11.7 us
    all_gather x1, blocking collectives, body(): lax.all_gather(hour_codes, 'site', axis=0, tiled=True)  6.1 us
    all_gather x1, blocking collectives, body(): lax.all_gather(obs_values, 'site', axis=0, tiled=True)  5.17 us
    all_gather x1, blocking collectives, body(): lax.all_gather(offsets, 'site', axis=0, tiled=True)  5.12 us
  transfers between devices with their start and end apart: 3, of which 3 were waited for; matrix products, arithmetic and copies ran while one was open for 4% of the time, Pallas kernels for 0%

commit v1 on v0

v1 whole, which is shorter than its diff:
```python
import functools

import jax
import jax.numpy as jnp
from jax import lax
from jax.experimental import pallas as pl
from jax.experimental.pallas import tpu as pltpu
from jax.sharding import PartitionSpec as P

NS_ITERS = 8
TAIL = 8
BF16 = jnp.bfloat16
F32 = jnp.float32
VMEM_LIMIT = 40 * 2**20


def whole():
    return pl.BlockSpec(memory_space=pltpu.VMEM)


def call(kernel, outs, args, name, scratch=()):
    return pl.pallas_call(
        kernel,
        out_shape=outs,
        in_specs=[whole()] * len(args),
        out_specs=jax.tree.map(lambda _: whole(), outs),
        scratch_shapes=scratch,
        compiler_params=pltpu.CompilerParams(vmem_limit_bytes=VMEM_LIMIT),
        name=name,
    )(*args)


def dot(a, b):
    return jnp.dot(a, b, preferred_element_type=F32)


def split(x):
    high = x.astype(BF16)
    return high, (x - high.astype(F32)).astype(BF16)


def dot_wide(a, b):
    a_high, a_low = split(a)
    b_high, b_low = split(b)
    return dot(
        jnp.concatenate([a_high, a_low, a_high], axis=1),
        jnp.concatenate([b_high, b_high, b_low], axis=0),
    )


def thirds(row):
    first = row.astype(BF16).astype(F32)
    second = (row - first).astype(BF16).astype(F32)
    third = row - first - second
    zeros = jnp.zeros((13, row.shape[1]), F32)
    return jnp.concatenate([first, second, third, zeros], axis=0).astype(BF16)


def row_times(row, *weights):
    rows = thirds(row)
    total = dot(rows, weights[0])
    for w in weights[1:]:
        total += dot(rows, w)
    return jnp.sum(total, axis=0, keepdims=True)


def own_half(hours):
    return lax.rem(lax.axis_index("site"), 2) * (hours // 2)


def local_grams(hours, rows_ref, values_ref, codes_ref, keep_ref, send_ref):
    half = hours // 2
    states = rows_ref.shape[1]
    start = own_half(hours)
    rows = rows_ref[...]
    turned = rows.T
    codes = codes_ref[...]
    values = values_ref[...].astype(F32)
    slots = []
    for slot in range(hours):
        hour = lax.rem(start + slot, hours)
        slots.append((codes == hour).astype(F32))
    masked = jnp.concatenate([turned * s.astype(BF16) for s in slots], axis=0)
    grams = dot(masked, rows)
    weighted = jnp.concatenate([s * values for s in slots], axis=0)
    pad = jnp.zeros((16 - hours, weighted.shape[1]), F32)
    drives = dot(jnp.concatenate([weighted, pad], axis=0).astype(BF16), rows)
    row_id = lax.broadcasted_iota(jnp.int32, (states, states), 0)
    column_id = lax.broadcasted_iota(jnp.int32, (states, states), 1)
    for out_ref, base in ((keep_ref, 0), (send_ref, half)):
        for pair in range(half // 2):
            first = base + 2 * pair
            a = grams[first * states : (first + 1) * states]
            b = grams[(first + 1) * states : (first + 2) * states]
            diagonal = jnp.sum(jnp.where(row_id == column_id, b, 0.0), axis=0, keepdims=True)
            out_ref[pair, :states, :] = jnp.where(row_id <= column_id, a, b)
            out_ref[pair, states:, :] = jnp.concatenate(
                [diagonal, drives[first : first + 2], jnp.zeros((TAIL - 3, states), F32)], axis=0
            )


def add_and_round(keep_ref, received_ref, sum_ref, send_ref):
    states = keep_ref.shape[2]
    for pair in range(keep_ref.shape[0]):
        total = keep_ref[pair] + received_ref[pair]
        sum_ref[pair] = total
        send_ref[pair, :states, :] = total[:states].astype(BF16)
        tail = total[states:]
        high = tail.astype(BF16).astype(F32)
        send_ref[pair, states:, :] = jnp.concatenate([high, tail - high], axis=0).astype(BF16)


def add_received(sum_ref, received_ref, out_ref):
    states = sum_ref.shape[2]
    for pair in range(sum_ref.shape[0]):
        out_ref[pair] = sum_of(sum_ref, received_ref, pair, states)


def sum_of(sum_ref, received_ref, pair, states):
    received = received_ref[pair].astype(F32)
    tail = received[states : states + TAIL] + received[states + TAIL :]
    return sum_ref[pair] + jnp.concatenate([received[:states], tail], axis=0)


def hour_maps(sum_ref, received_ref, prior_ref, turned_ref, out_ref):
    states = prior_ref.shape[0]
    prior = prior_ref[...]
    turned = turned_ref[...]
    row_id = lax.broadcasted_iota(jnp.int32, (states, states), 0)
    column_id = lax.broadcasted_iota(jnp.int32, (states, states), 1)
    running = []
    for pair in range(sum_ref.shape[0]):
        total = sum_of(sum_ref, received_ref, pair, states)
        square = total[:states]
        flipped = square.T
        upper, lower = row_id <= column_id, row_id > column_id
        gram_a = jnp.where(upper, square, flipped)
        gram_b = jnp.where(lower, square, flipped)
        gram_b = jnp.where(row_id == column_id, total[states : states + 1], gram_b)
        for gram, place in ((gram_a, states + 1), (gram_b, states + 2)):
            precision = prior + gram
            bound = jnp.max(jnp.sum(jnp.abs(precision), axis=0, keepdims=True), axis=1, keepdims=True)
            scale = 1.0 / bound
            offset = jnp.concatenate(
                [total[place : place + 1], jnp.zeros((15, states), F32)], axis=0
            )
            running.append((precision * scale, turned * scale, offset * scale))
    stacked = tuple(jnp.concatenate(parts, axis=0) for parts in running)

    def step(_, state):
        return tuple(2.0 * z - dot_wide(z, z[:states]) for z in state)

    stacked = lax.fori_loop(0, NS_ITERS - 1, step, stacked)
    maps = []
    for z in stacked:
        v = z[states:]
        maps.append(2.0 * v - dot_wide(v, z[:states]))
    joined = maps[0]
    out_ref[0] = joined
    for position in range(1, len(maps)):
        joined = append(joined, maps[position])
        out_ref[position] = joined


def append(earlier, latter):
    states = latter.shape[1]
    product = dot_wide(earlier, latter[:states])
    return jnp.concatenate([product[:states], product[states:] + latter[states:]], axis=0)


def in_order(half, own_ref, received_ref):
    first = own_half(2 * half) == 0
    early = [jnp.where(first, own_ref[i], received_ref[i]) for i in range(half)]
    late = [jnp.where(first, received_ref[i], own_ref[i]) for i in range(half)]
    return early, late


def block_map(own_ref, received_ref, out_ref):
    half, rows, states = own_ref.shape
    early, late = in_order(half, own_ref, received_ref)
    joined = append(early[-1], late[-1])
    out_ref[:states, :] = joined[:states].astype(BF16)
    out_ref[states:, :] = thirds(joined[states : states + 1])


def shift_of(block):
    states = block.shape[1]
    return jnp.sum(block[states:].astype(F32), axis=0, keepdims=True)


def pick(refs, slot):
    value = refs[0][...]
    for i in range(1, len(refs)):
        value = jnp.where(slot == i, refs[i][...], value)
    return value


def apply(block, mean):
    return row_times(mean, block[: block.shape[1]]) + shift_of(block)


def follow(earlier, latter):
    states = latter.shape[1]
    product = dot(earlier[:states], latter[:states]).astype(BF16)
    return jnp.concatenate([product, thirds(apply(latter, shift_of(earlier)))], axis=0)


def group_shift(*refs):
    gathered, out_ref = refs[:-1], refs[-1]
    place = lax.rem(lax.axis_index("tm"), len(gathered))
    mean = shift_of(pick(gathered, place))
    for i in range(1, len(gathered)):
        mean = apply(pick(gathered, place ^ i), mean)
    out_ref[...] = jnp.broadcast_to(mean, out_ref.shape)


def group_map(*refs):
    gathered, out_ref = refs[:-1], refs[-1]
    place = lax.rem(lax.axis_index("tm"), len(gathered))
    joined = pick(gathered, place)
    for i in range(1, len(gathered)):
        joined = follow(joined, pick(gathered, place ^ i))
    out_ref[...] = joined


def pair_map(distance, own_ref, received_ref, out_ref):
    upper = is_upper(distance)
    first = jnp.where(upper, received_ref[...], own_ref[...])
    second = jnp.where(upper, own_ref[...], received_ref[...])
    out_ref[...] = follow(first, second)


def is_upper(distance):
    return lax.rem(lax.axis_index("tm") // distance, 2) == 1


def block_means(distances, *refs):
    out_ref, own_ref, other_ref = refs[-1], refs[0], refs[1]
    levels, gathered = refs[2 : 2 + len(distances)], refs[2 + len(distances) : -1]
    half, rows, states = own_ref.shape
    mean = jnp.zeros((1, states), F32)
    for level in reversed(range(len(distances))):
        if level == len(distances) - 1:
            entered = levels[level][0:1, :]
        else:
            entered = apply(levels[level][...], mean)
        mean = jnp.where(is_upper(distances[level]), entered, mean)
    place = lax.rem(lax.axis_index("tm"), len(gathered))
    for i in range(len(gathered) - 1):
        mean = jnp.where(i < place, apply(pick(gathered, place ^ i), mean), mean)
    early, late = in_order(half, own_ref, other_ref)
    results = []
    for maps in (early, late):
        start = mean
        for each in maps:
            mean = row_times(start, *split(each[:states])) + each[states : states + 1]
            results.append(mean)
    results = jnp.concatenate(results, axis=0).astype(BF16)
    for copy in range(out_ref.shape[0]):
        out_ref[copy] = results


def swaps(size, distance):
    return [(i, i ^ distance) for i in range(size)]


def body(obs_rows, obs_values, obs_hours, prior_precision, transition, site_basis):
    hours = lax.axis_size("site")
    blocks = lax.axis_size("tm")
    count, states = obs_rows.shape
    half = hours // 2
    pairs = half // 2
    sds = jax.ShapeDtypeStruct
    turned = jnp.dot(transition.T, prior_precision.T, precision=lax.Precision.HIGHEST)
    packed = sds((pairs, states + TAIL, states), F32)
    keep, send = call(
        functools.partial(local_grams, hours),
        (packed, packed),
        (obs_rows, obs_values.reshape(1, count), obs_hours.reshape(1, count)),
        "local_grams",
    )
    received = lax.ppermute(send, "site", swaps(hours, 1))
    rounded = sds((pairs, states + 2 * TAIL, states), BF16)
    distance = 2
    while distance < hours:
        total, send = call(add_and_round, (packed, rounded), (keep, received), "add_and_round")
        received = lax.ppermute(send, "site", swaps(hours, distance))
        distance *= 2
        if distance < hours:
            keep = call(add_received, packed, (total, received), "add_received")
            received = jnp.zeros_like(keep)
    maps = call(
        hour_maps,
        sds((half, states + 16, states), F32),
        (total, received, prior_precision, turned),
        "hour_maps",
    )
    other = lax.ppermute(maps, "site", swaps(hours, 1))
    own = call(block_map, sds((states + 16, states), BF16), (maps, other), "block_map")
    radix = min(4, blocks)
    gathered = [own] + [lax.ppermute(own, "tm", swaps(blocks, d)) for d in range(1, radix)]
    distances, levels = [], []
    distance = radix
    if 2 * distance < blocks:
        joined = call(group_map, sds(own.shape, BF16), gathered, "group_map")
    while distance < blocks:
        if 2 * distance == blocks:
            if levels:
                shift = joined[states:].astype(F32).sum(axis=0, keepdims=True)
                shift = jnp.broadcast_to(shift, (8, states))
            else:
                shift = call(group_shift, sds((8, states), F32), gathered, "group_shift")
            received = lax.ppermute(shift, "tm", swaps(blocks, distance))
        else:
            received = lax.ppermute(joined, "tm", swaps(blocks, distance))
            joined = call(
                functools.partial(pair_map, distance),
                sds(own.shape, BF16),
                (joined, received),
                "pair_map",
            )
        distances.append(distance)
        levels.append(received)
        distance *= 2
    means = call(
        functools.partial(block_means, tuple(distances)),
        sds((blocks, hours, states), BF16),
        [maps, other] + levels + gathered,
        "block_means",
    )
    means = lax.all_to_all(means, "tm", 0, 0, tiled=True).reshape(blocks * hours, states)
    return jnp.einsum("hs,ns->hn", means, site_basis, preferred_element_type=F32).astype(BF16)


def solution(mesh):
    in_specs = (
        P(("tm", "site"), None),
        P(("tm", "site")),
        P(("tm", "site")),
        P(),
        P(),
        P(("tm", "site"), None),
    )
    out_specs = P(None, ("tm", "site"))
    return jax.shard_map(body, mesh=mesh, in_specs=in_specs, out_specs=out_specs, check_vma=False)
```

time: 155 us -> 50.8 us (0.33)
  blocking collectives: 69.4 us -> 12.1 us
  waiting for transfers between devices: 45.1 us -> 13.9 us
  matrix products: 22.8 us -> 3.04 us
  between operations: 14.3 us -> 0.07 us
  starting transfers between devices: 0.08 us -> 9.72 us
  Pallas kernels: 0 us -> 8.28 us
  local copies, waits for them, and re-layouts: 1.17 us -> 3.43 us
    all_gather x5 -> x0, blocking collectives: 69.4 us -> none  [the longest x1 32.5 us: body(): lax.all_gather(rounded, 'tm', axis=0, tiled=True)]
    all_gather x3 -> x0, waiting for transfers between devices: 44.4 us -> none  [the longest x1 16.8 us: body(): lax.all_gather(hour_maps, 'site', axis=0, tiled=True)]
    dot_general x32 -> x2, matrix products: 22.8 us -> 3.04 us  [the longest x1 1.62 us: body(): jnp.dot(transition.T, prior_precision.T, precision=lax.Precision.HIGHEST)]
    ppermute x0 -> x7, waiting for transfers between devices: none -> 13.9 us  [the longest x3 6.44 us: body(): lax.ppermute(own, 'tm', swaps(blocks, d))]
    all_to_all x0 -> x1, blocking collectives: none -> 12.1 us  [body(): lax.all_to_all(means, 'tm', 0, 0, tiled=True)]
    ppermute x0 -> x7, starting transfers between devices: none -> 9.72 us  [the longest x3 3.55 us: body(): lax.ppermute(own, 'tm', swaps(blocks, d))]
    pallas_call x0 -> x6, Pallas kernels: none -> 8.28 us  [call(): pl.pallas_call(kernel, out_shape=outs, in_specs=[whole()] * len(args), ou...]
  transfers between devices with their start and end apart: 3 -> 7, of which waited for: 3 -> 6; matrix products, arithmetic and copies ran while one was open for 4% -> 3% of each run, Pallas kernels for 0% -> 0%
where the time goes in v1:
time: 50.8 us; the launch traced here: 50.5 us
  waiting for transfers between devices  13.9 us (27%)
  blocking collectives  12.1 us (24%)
  starting transfers between devices  9.72 us (19%)
  Pallas kernels  8.28 us (16%)
  local copies, waits for them, and re-layouts  3.43 us (7%)
  matrix products  3.04 us (6%)
    all_to_all x1, blocking collectives, body(): lax.all_to_all(means, 'tm', 0, 0, tiled=True)  12.1 us
    pallas_call x6, Pallas kernels, call(): pl.pallas_call(kernel, out_shape=outs, in_specs=[whole()] * len(args), ou...  8.28 us
    ppermute x3, waiting for transfers between devices, body(): lax.ppermute(own, 'tm', swaps(blocks, d))  6.44 us
    ppermute x3, starting transfers between devices, body(): lax.ppermute(own, 'tm', swaps(blocks, d))  3.55 us
    ppermute x1, starting transfers between devices, body(): received = lax.ppermute(send, 'site', swaps(hours, distance))  2.93 us
    ppermute x1, starting transfers between devices, body(): received = lax.ppermute(shift, 'tm', swaps(blocks, distance))  2.65 us
    unnamed x8, local copies, waits for them, and re-layouts  2.58 us
    ppermute x1, waiting for transfers between devices, body(): received = lax.ppermute(send, 'site', swaps(hours, distance))  2.35 us
  transfers between devices with their start and end apart: 7, of which 6 were waited for; matrix products, arithmetic and copies ran while one was open for 3% of the time, Pallas kernels for 0%

profile of v1, /device:TPU:0, one launch (start us, length us, event | category | flops | bytes accessed | tf_op | source)
XLA Modules:
  0.0 50.5 jit_solution(10593393470648661617)
XLA Ops:
  0.0 0.0 copy-start
  0.0 0.8 %reshape.9.values_ref = bf16[1,512]{1,0:T(2,128)(2,1)S(1)} reshape(bf16[512]{0:T(512)(128)(2,1)} %param.7) | data formatting | bytes 2048 | tf_op jit(solution)/shard_map/reshape | solution.py:279
  0.8 0.0 copy-start.2
  0.8 0.9 %copy-done.2 = bf16[512,256]{1,0:T(8,128)(2,1)S(1)} copy-done((bf16[512,256]{1,0:T(8,128)(2,1)S(1)}, bf16[512,256]{1,0:T(8,128)(2,1)}, u32[]{:S(2)}) %copy-start.2) | copy-done | bytes 262168
  1.8 0.0 copy-start.3
  1.8 0.7 %copy-done.3 = s32[512]{0:T(512)S(1)} copy-done((s32[512]{0:T(512)S(1)}, s32[512]{0:T(512)}, u32[]{:S(2)}) %copy-start.3) | copy-done | bytes 2072
  2.5 0.5 local_grams.1
  3.0 0.5 %collective-permute-start = (f32[1,264,256]{2,1,0:T(8,128)S(1)}, f32[1,264,256]{2,1,0:T(8,128)S(1)}, u32[]{:S(2)}, u32[]{:S(2)}) collective-permute-start(f32[1,264,256]{2,1,0:T(8,128)S(1)} %get-tuple-element.10), channel_id=1, source_target_pairs={{0,1},{1,0},{2,3},{3,2},{4,5},{5,4},{6,7},{7,6},{8,9},{9,8},{10,11... | collective-permute-start | bytes 811016 | tf_op jit(solution)/shard_map/ppermute | solution.py:282
  3.5 1.2 %collective-permute-done.received_ref = f32[1,264,256]{2,1,0:T(8,128)S(1)} collective-permute-done((f32[1,264,256]{2,1,0:T(8,128)S(1)}, f32[1,264,256]{2,1,0:T(8,128)S(1)}, u32[]{:S(2)}, u32[]{:S(2)}) %collective-permute-start) | collective-permute-done | bytes 270368 | tf_op jit(solution)/shard_map/ppermute | solution.py:282
  4.7 2.9 %collective-permute-start.1 = (bf16[1,272,256]{2,1,0:T(8,128)(2,1)S(1)}, bf16[1,272,256]{2,1,0:T(8,128)(2,1)S(1)}, u32[]{:S(2)}, u32[]{:S(2)}) collective-permute-start(bf16[1,272,256]{2,1,0:T(8,128)(2,1)S(1)} %get-tuple-element.12), channel_id=1, source_target_pairs={{0,2},{1,3},{2,0},{3,1},{4,6},{5,7},{6,4},{7,5},{8,10},{9,11},{10,... | collective-permute-start | bytes 417800 | tf_op jit(solution)/shard_map/ppermute | solution.py:287
  7.6 1.6 %fusion.turned_ref = f32[256,256]{1,0:T(8,128)S(1)} fusion(f32[256,256]{1,0:T(8,128)} %param.10, f32[256,256]{1,0:T(8,128)} %prior_ref.1), kind=kOutput, calls=%fused_computation.1 | convolution fusion | flops 201326592 | bytes 786432 | tf_op jit(solution)/shard_map/dot_general | solution.py:274
  9.3 2.3 %collective-permute-done.1.received_ref = bf16[1,272,256]{2,1,0:T(8,128)(2,1)S(1)} collective-permute-done((bf16[1,272,256]{2,1,0:T(8,128)(2,1)S(1)}, bf16[1,272,256]{2,1,0:T(8,128)(2,1)S(1)}, u32[]{:S(2)}, u32[]{:S(2)}) %collective-permute-start.1) | collective-permute-done | bytes 139296 | tf_op jit(solution)/shard_map/ppermute | solution.py:287
  11.6 0.0 copy-start.1
  11.6 0.9 %copy-done.1 = f32[256,256]{1,0:T(8,128)S(1)} copy-done((f32[256,256]{1,0:T(8,128)S(1)}, f32[256,256]{1,0:T(8,128)}, u32[]{:S(2)}) %copy-start.1) | copy-done | bytes 262168
  12.6 6.2 %hour_maps.1.own_ref.refs_0_ = f32[2,272,256]{2,1,0:T(8,128)S(1)} custom-call(f32[1,264,256]{2,1,0:T(8,128)S(1)} %get-tuple-element.11.sum_ref, bf16[1,272,256]{2,1,0:T(8,128)(2,1)S(1)} %collective-permute-done.1.received_ref, f32[256,256]{1,0:T(8,128)S(1)} %copy-done.1, f32[256,256]{1,0:T(8,128)S(1)} %fusion.turned_ref), custom_call_target="tpu_custom_call" | custom-call | tf_op jit(solution)/shard_map/hour_maps/pallas_call | solution.py:22
  18.7 0.1 collective-permute-start.2
  18.8 1.9 %collective-permute-done.2.received_ref.refs_1_ = f32[2,272,256]{2,1,0:T(8,128)S(1)} collective-permute-done((f32[2,272,256]{2,1,0:T(8,128)S(1)}, f32[2,272,256]{2,1,0:T(8,128)S(1)}, u32[]{:S(2)}, u32[]{:S(2)}) %collective-permute-start.2) | collective-permute-done | bytes 557088 | tf_op jit(solution)/shard_map/ppermute | solution.py:298
  20.8 0.3 block_map.1.refs_0_.refs_3_
  21.1 2.9 %collective-permute-start.5 = (bf16[272,256]{1,0:T(8,128)(2,1)S(1)}, bf16[272,256]{1,0:T(8,128)(2,1)S(1)}, u32[]{:S(2)}, u32[]{:S(2)}) collective-permute-start(bf16[272,256]{1,0:T(8,128)(2,1)S(1)} %block_map.1.refs_0_.refs_3_), channel_id=1, source_target_pairs={{0,12},{4,8},{8,4},{12,0},{16,28},{20,24},{24,20},{28,16},{1,13},{... | collective-permute-start | bytes 417800 | tf_op jit(solution)/shard_map/ppermute | solution.py:301
  23.9 0.4 collective-permute-start.4
  24.4 0.3 collective-permute-start.3
  24.7 3.9 %collective-permute-done.5.refs_3_.refs_6_ = bf16[272,256]{1,0:T(8,128)(2,1)S(1)} collective-permute-done((bf16[272,256]{1,0:T(8,128)(2,1)S(1)}, bf16[272,256]{1,0:T(8,128)(2,1)S(1)}, u32[]{:S(2)}, u32[]{:S(2)}) %collective-permute-start.5) | collective-permute-done | bytes 139296 | tf_op jit(solution)/shard_map/ppermute | solution.py:301
  28.6 2.5 %collective-permute-done.4.refs_2_.refs_5_ = bf16[272,256]{1,0:T(8,128)(2,1)S(1)} collective-permute-done((bf16[272,256]{1,0:T(8,128)(2,1)S(1)}, bf16[272,256]{1,0:T(8,128)(2,1)S(1)}, u32[]{:S(2)}, u32[]{:S(2)}) %collective-permute-start.4) | collective-permute-done | bytes 139296 | tf_op jit(solution)/shard_map/ppermute | solution.py:301
  31.1 0.0 collective-permute-done.3.refs_1_.refs_4_
  31.1 0.4 group_shift.1
  31.5 2.6 %collective-permute-start.6 = (f32[8,256]{1,0:T(8,128)S(1)}, f32[8,256]{1,0:T(8,128)S(1)}, u32[]{:S(2)}, u32[]{:S(2)}) collective-permute-start(f32[8,256]{1,0:T(8,128)S(1)} %group_shift.1), channel_id=1, source_target_pairs={{0,16},{4,20},{8,24},{12,28},{16,0},{20,4},{24,8},{28,12},{1,17},{... | collective-permute-start | bytes 24584 | tf_op jit(solution)/shard_map/ppermute | solution.py:313
  34.2 2.0 %collective-permute-done.6.refs_2_ = f32[8,256]{1,0:T(8,128)S(1)} collective-permute-done((f32[8,256]{1,0:T(8,128)S(1)}, f32[8,256]{1,0:T(8,128)S(1)}, u32[]{:S(2)}, u32[]{:S(2)}) %collective-permute-start.6) | collective-permute-done | bytes 8224 | tf_op jit(solution)/shard_map/ppermute | solution.py:313
  36.2 0.8 %block_means.1 = bf16[8,4,256]{2,1,0:T(4,128)(2,1)S(1)} custom-call(f32[2,272,256]{2,1,0:T(8,128)S(1)} %hour_maps.1.own_ref.refs_0_, f32[2,272,256]{2,1,0:T(8,128)S(1)} %collective-permute-done.2.received_ref.refs_1_, f32[8,256]{1,0:T(8,128)S(1)} %collective-permute-done.6.refs_2_, bf16[272,256]{1,0:T(8,128)(2,1)S(1)} %block_map.1.refs_0_.refs_3_, ...), custom_call_target="tpu_custom_call" | custom-call | tf_op jit(solution)/shard_map/block_means/pallas_call | solution.py:22
  37.0 12.1 %all_to_all.5 = bf16[8,4,256]{2,1,0:T(4,128)(2,1)S(1)} all-to-all(bf16[8,4,256]{2,1,0:T(4,128)(2,1)S(1)} %block_means.1), channel_id=1, replica_groups=mesh['tm'=8,'site'=4] {'tm'}, dimensions={0} | all-to-all | bytes 32768 | tf_op jit(solution)/shard_map/all_to_all | solution.py:331
  49.1 0.0 copy-done
  49.1 1.4 %convolution_convert_fusion = bf16[32,4096]{1,0:T(8,128)(2,1)} fusion(bf16[32,256]{1,0:T(8,128)(2,1)S(1)} %reshape.11, bf16[4096,256]{1,0:T(8,128)(2,1)S(1)} %copy-done), kind=kOutput, calls=%fused_computation | convolution fusion | flops 67239936 | bytes 2375680 | tf_op jit(solution)/shard_map/hs,ns->hn/dot_general | solution.py:332
  (2 shorter events, 0.0 us)
Async XLA Ops:
  0.0 49.1 %copy-start = (bf16[4096,256]{1,0:T(8,128)(2,1)S(1)}, bf16[4096,256]{1,0:T(8,128)(2,1)}, u32[]{:S(2)}) copy-start(bf16[4096,256]{1,0:T(8,128)(2,1)} %param.11) | copy-start | bytes 6291460
  0.8 0.9 %copy-start.2 = (bf16[512,256]{1,0:T(8,128)(2,1)S(1)}, bf16[512,256]{1,0:T(8,128)(2,1)}, u32[]{:S(2)}) copy-start(bf16[512,256]{1,0:T(8,128)(2,1)} %rows_ref.1) | copy-start | bytes 786436
  1.8 0.7 %copy-start.3 = (s32[512]{0:T(512)S(1)}, s32[512]{0:T(512)}, u32[]{:S(2)}) copy-start(s32[512]{0:T(512)} %param.8) | copy-start | bytes 6148
  3.0 1.7 %collective-permute-start = (f32[1,264,256]{2,1,0:T(8,128)S(1)}, f32[1,264,256]{2,1,0:T(8,128)S(1)}, u32[]{:S(2)}, u32[]{:S(2)}) collective-permute-start(f32[1,264,256]{2,1,0:T(8,128)S(1)} %get-tuple-element.10), channel_id=1, source_target_pairs={{0,1},{1,0},{2,3},{3,2},{4,5},{5,4},{6,7},{7,6},{8,9},{9,8},{10,11... | collective-permute-start | bytes 811016 | tf_op jit(solution)/shard_map/ppermute | solution.py:282
  4.7 6.9 %collective-permute-start.1 = (bf16[1,272,256]{2,1,0:T(8,128)(2,1)S(1)}, bf16[1,272,256]{2,1,0:T(8,128)(2,1)S(1)}, u32[]{:S(2)}, u32[]{:S(2)}) collective-permute-start(bf16[1,272,256]{2,1,0:T(8,128)(2,1)S(1)} %get-tuple-element.12), channel_id=1, source_target_pairs={{0,2},{1,3},{2,0},{3,1},{4,6},{5,7},{6,4},{7,5},{8,10},{9,11},{10,... | collective-permute-start | bytes 417800 | tf_op jit(solution)/shard_map/ppermute | solution.py:287
  11.6 1.0 %copy-start.1 = (f32[256,256]{1,0:T(8,128)S(1)}, f32[256,256]{1,0:T(8,128)}, u32[]{:S(2)}) copy-start(f32[256,256]{1,0:T(8,128)} %prior_ref.1) | copy-start | bytes 786436
  18.7 2.0 %collective-permute-start.2 = (f32[2,272,256]{2,1,0:T(8,128)S(1)}, f32[2,272,256]{2,1,0:T(8,128)S(1)}, u32[]{:S(2)}, u32[]{:S(2)}) collective-permute-start(f32[2,272,256]{2,1,0:T(8,128)S(1)} %hour_maps.1.own_ref.refs_0_), channel_id=1, source_target_pairs={{0,1},{1,0},{2,3},{3,2},{4,5},{5,4},{6,7},{7,6},{8,9},{9,8},{10,11... | collective-permute-start | bytes 1671176 | tf_op jit(solution)/shard_map/ppermute | solution.py:298
  21.1 7.5 %collective-permute-start.5 = (bf16[272,256]{1,0:T(8,128)(2,1)S(1)}, bf16[272,256]{1,0:T(8,128)(2,1)S(1)}, u32[]{:S(2)}, u32[]{:S(2)}) collective-permute-start(bf16[272,256]{1,0:T(8,128)(2,1)S(1)} %block_map.1.refs_0_.refs_3_), channel_id=1, source_target_pairs={{0,12},{4,8},{8,4},{12,0},{16,28},{20,24},{24,20},{28,16},{1,13},{... | collective-permute-start | bytes 417800 | tf_op jit(solution)/shard_map/ppermute | solution.py:301
  23.9 7.1 %collective-permute-start.4 = (bf16[272,256]{1,0:T(8,128)(2,1)S(1)}, bf16[272,256]{1,0:T(8,128)(2,1)S(1)}, u32[]{:S(2)}, u32[]{:S(2)}) collective-permute-start(bf16[272,256]{1,0:T(8,128)(2,1)S(1)} %block_map.1.refs_0_.refs_3_), channel_id=1, source_target_pairs={{0,8},{4,12},{8,0},{12,4},{16,24},{20,28},{24,16},{28,20},{1,9},{5... | collective-permute-start | bytes 417800 | tf_op jit(solution)/shard_map/ppermute | solution.py:301
  24.4 6.7 %collective-permute-start.3 = (bf16[272,256]{1,0:T(8,128)(2,1)S(1)}, bf16[272,256]{1,0:T(8,128)(2,1)S(1)}, u32[]{:S(2)}, u32[]{:S(2)}) collective-permute-start(bf16[272,256]{1,0:T(8,128)(2,1)S(1)} %block_map.1.refs_0_.refs_3_), channel_id=1, source_target_pairs={{0,4},{4,0},{8,12},{12,8},{16,20},{20,16},{24,28},{28,24},{1,5},{5... | collective-permute-start | bytes 417800 | tf_op jit(solution)/shard_map/ppermute | solution.py:301
  31.5 4.6 %collective-permute-start.6 = (f32[8,256]{1,0:T(8,128)S(1)}, f32[8,256]{1,0:T(8,128)S(1)}, u32[]{:S(2)}, u32[]{:S(2)}) collective-permute-start(f32[8,256]{1,0:T(8,128)S(1)} %group_shift.1), channel_id=1, source_target_pairs={{0,16},{4,20},{8,24},{12,28},{16,0},{20,4},{24,8},{28,12},{1,17},{... | collective-permute-start | bytes 24584 | tf_op jit(solution)/shard_map/ppermute | solution.py:313

commit v2 on v1

--- a/solution.py
+++ b/solution.py
@@ -18,11 +18,13 @@
     return pl.BlockSpec(memory_space=pltpu.VMEM)
 
 
-def call(kernel, outs, args, name, scratch=()):
+def call(kernel, outs, args, name, scratch=(), in_hbm=False):
+    if in_hbm:
+        args = [pltpu.with_memory_space_constraint(arg, pltpu.HBM) for arg in args]
     return pl.pallas_call(
         kernel,
         out_shape=outs,
-        in_specs=[whole()] * len(args),
+        in_specs=[pl.BlockSpec(memory_space=pltpu.HBM) if in_hbm else whole()] * len(args),
         out_specs=jax.tree.map(lambda _: whole(), outs),
         scratch_shapes=scratch,
         compiler_params=pltpu.CompilerParams(vmem_limit_bytes=VMEM_LIMIT),
@@ -68,14 +70,34 @@
     return lax.rem(lax.axis_index("site"), 2) * (hours // 2)
 
 
-def local_grams(hours, rows_ref, values_ref, codes_ref, keep_ref, send_ref):
+def local_grams(
+    hours,
+    rows_hbm,
+    values_hbm,
+    codes_hbm,
+    keep_ref,
+    send_ref,
+    rows_ref,
+    values_ref,
+    codes_ref,
+    sems,
+):
     half = hours // 2
-    states = rows_ref.shape[1]
+    states = rows_hbm.shape[1]
     start = own_half(hours)
+    copies = [
+        pltpu.make_async_copy(rows_hbm, rows_ref, sems.at[0]),
+        pltpu.make_async_copy(values_hbm, values_ref, sems.at[1]),
+        pltpu.make_async_copy(codes_hbm, codes_ref, sems.at[2]),
+    ]
+    for copy in copies:
+        copy.start()
+    for copy in copies:
+        copy.wait()
     rows = rows_ref[...]
     turned = rows.T
-    codes = codes_ref[...]
-    values = values_ref[...].astype(F32)
+    codes = codes_ref[...].reshape(1, rows.shape[0])
+    values = values_ref[...].astype(F32).reshape(1, rows.shape[0])
     slots = []
     for slot in range(hours):
         hour = lax.rem(start + slot, hours)
@@ -97,6 +119,12 @@
             out_ref[pair, states:, :] = jnp.concatenate(
                 [diagonal, drives[first : first + 2], jnp.zeros((TAIL - 3, states), F32)], axis=0
             )
+
+
+def coupled_turned(prior_ref, transition_ref, prior_out_ref, turned_ref):
+    prior = prior_ref[...]
+    prior_out_ref[...] = prior
+    turned_ref[...] = dot_wide(transition_ref[...].T, prior)
 
 
 def add_and_round(keep_ref, received_ref, sum_ref, send_ref):
@@ -145,16 +173,17 @@
                 [total[place : place + 1], jnp.zeros((15, states), F32)], axis=0
             )
             running.append((precision * scale, turned * scale, offset * scale))
-    stacked = tuple(jnp.concatenate(parts, axis=0) for parts in running)
-
-    def step(_, state):
-        return tuple(2.0 * z - dot_wide(z, z[:states]) for z in state)
-
-    stacked = lax.fori_loop(0, NS_ITERS - 1, step, stacked)
+    stacked = [jnp.concatenate(parts, axis=0) for parts in running]
+
+    for _ in range(NS_ITERS - 2):
+        stacked = [2.0 * z - dot_wide(z, z[:states]) for z in stacked]
     maps = []
     for z in stacked:
+        power = (jnp.where(row_id == column_id, 1.0, 0.0) - z[:states]).astype(BF16)
         v = z[states:]
-        maps.append(2.0 * v - dot_wide(v, z[:states]))
+        product = dot(jnp.concatenate([power, v.astype(BF16)], axis=0), power)
+        v = v + product[states:]
+        maps.append(v + dot(v.astype(BF16), product[:states].astype(BF16)))
     joined = maps[0]
     out_ref[0] = joined
     for position in range(1, len(maps)):
@@ -175,12 +204,25 @@
     return early, late
 
 
-def block_map(own_ref, received_ref, out_ref):
+def block_map(own_ref, received_ref, out_ref, part_ref):
     half, rows, states = own_ref.shape
     early, late = in_order(half, own_ref, received_ref)
     joined = append(early[-1], late[-1])
     out_ref[:states, :] = joined[:states].astype(BF16)
     out_ref[states:, :] = thirds(joined[states : states + 1])
+    height = part_ref.shape[0]
+    first = own_half(2 * half) == 0
+    part_ref[...] = jnp.where(first, out_ref[:height, :], out_ref[rows - height :, :])
+
+
+def group_blocks(own_ref, near_ref, part_ref, other_near_ref, other_part_ref, *out_refs):
+    first = lax.rem(lax.axis_index("site"), 2) == 0
+    rows, height = own_ref.shape[0], part_ref.shape[0]
+    out_refs[0][...] = jnp.where(first, near_ref[...], other_near_ref[...])
+    out_refs[1][...] = jnp.where(first, other_near_ref[...], near_ref[...])
+    out_refs[2][:height, :] = jnp.where(first, part_ref[...], other_part_ref[...])
+    low = jnp.where(first, other_part_ref[...], part_ref[...])
+    out_refs[2][height:, :] = low[2 * height - rows :]
 
 
 def shift_of(block):
@@ -271,13 +313,25 @@
     half = hours // 2
     pairs = half // 2
     sds = jax.ShapeDtypeStruct
-    turned = jnp.dot(transition.T, prior_precision.T, precision=lax.Precision.HIGHEST)
+    prior, turned = call(
+        coupled_turned,
+        (sds((states, states), F32), sds((states, states), F32)),
+        (prior_precision, transition),
+        "coupled_turned",
+    )
     packed = sds((pairs, states + TAIL, states), F32)
     keep, send = call(
         functools.partial(local_grams, hours),
         (packed, packed),
-        (obs_rows, obs_values.reshape(1, count), obs_hours.reshape(1, count)),
+        (obs_rows, obs_values, obs_hours),
         "local_grams",
+        [
+            pltpu.VMEM(obs_rows.shape, BF16),
+            pltpu.VMEM(obs_values.shape, BF16),
+            pltpu.VMEM(obs_hours.shape, jnp.int32),
+            pltpu.SemaphoreType.DMA((3,)),
+        ],
+        in_hbm=True,
     )
     received = lax.ppermute(send, "site", swaps(hours, 1))
     rounded = sds((pairs, states + 2 * TAIL, states), BF16)
@@ -292,13 +346,30 @@
     maps = call(
         hour_maps,
         sds((half, states + 16, states), F32),
-        (total, received, prior_precision, turned),
+        (total, received, prior, turned),
         "hour_maps",
     )
     other = lax.ppermute(maps, "site", swaps(hours, 1))
-    own = call(block_map, sds((states + 16, states), BF16), (maps, other), "block_map")
-    radix = min(4, blocks)
-    gathered = [own] + [lax.ppermute(own, "tm", swaps(blocks, d)) for d in range(1, radix)]
+    rows = states + 16
+    height = (rows // 2 + 15) // 16 * 16
+    own, part = call(
+        block_map,
+        (sds((rows, states), BF16), sds((height, states), BF16)),
+        (maps, other),
+        "block_map",
+    )
+    radix = 4
+    devices = [(t, d) for t in range(blocks) for d in range(hours)]
+    near_swap = [(t * hours + d, (t ^ (1 + d % 2)) * hours + d) for t, d in devices]
+    far_swap = [(t * hours + d, (t ^ 3) * hours + d) for t, d in devices]
+    near = lax.ppermute(own, ("tm", "site"), near_swap)
+    far = lax.ppermute(part, ("tm", "site"), far_swap)
+    other_near = lax.ppermute(near, "site", swaps(hours, 1))
+    other_far = lax.ppermute(far, "site", swaps(hours, 1))
+    block = sds(own.shape, BF16)
+    gathered = (own,) + call(
+        group_blocks, (block,) * 3, (own, near, far, other_near, other_far), "group_blocks"
+    )
     distances, levels = [], []
     distance = radix
     if 2 * distance < blocks:
@@ -325,7 +396,7 @@
     means = call(
         functools.partial(block_means, tuple(distances)),
         sds((blocks, hours, states), BF16),
-        [maps, other] + levels + gathered,
+        [maps, other] + levels + list(gathered),
         "block_means",
     )
     means = lax.all_to_all(means, "tm", 0, 0, tiled=True).reshape(blocks * hours, states)

time: 50.8 us -> 44.9 us (0.88)
  waiting for transfers between devices: 13.9 us -> 11.8 us
  matrix products: 3.04 us -> 1.43 us
  local copies, waits for them, and re-layouts: 3.43 us -> 1.91 us
  Pallas kernels: 8.28 us -> 7.61 us
    dot_general x1 -> x0, matrix products: 1.62 us -> none  [body(): jnp.dot(transition.T, prior_precision.T, precision=lax.Precision.HIGHEST)]
    ppermute x3 -> x4, waiting for transfers between devices: 6.44 us -> 5 us  [the longest x1 2.68 us: body(): near = lax.ppermute(own, ('tm', 'site'), near_swap)]
    reshape x1 -> x0, local copies, waits for them, and re-layouts: 0.83 us -> none  [body(): obs_values.reshape(1, count)]
    unnamed x8 -> x6, local copies, waits for them, and re-layouts: 2.58 us -> 1.9 us
    pallas_call x6 -> x8, Pallas kernels: 8.28 us -> 7.61 us  [call(): pl.pallas_call(kernel, out_shape=outs, in_specs=[pl.BlockSpec(memory_spac...]
    ppermute x1, waiting for transfers between devices: 2.35 us -> 1.76 us  [body(): received = lax.ppermute(send, 'site', swaps(hours, distance))]
    ppermute x3 -> x4, starting transfers between devices: 3.55 us -> 3.35 us  [the longest x1 1.84 us: body(): near = lax.ppermute(own, ('tm', 'site'), near_swap)]
  transfers between devices with their start and end apart: 7 -> 8, of which waited for: 6 -> 7; matrix products, arithmetic and copies ran while one was open for 3% -> 0% of each run, Pallas kernels for 0% -> 1%
where the time goes in v2:
time: 44.9 us; the launch traced here: 44.7 us
  blocking collectives  12.3 us (27%)
  waiting for transfers between devices  11.8 us (26%)
  starting transfers between devices  9.51 us (21%)
  Pallas kernels  7.61 us (17%)
  local copies, waits for them, and re-layouts  1.91 us (4%)
  matrix products  1.43 us (3%)
    all_to_all x1, blocking collectives, body(): lax.all_to_all(means, 'tm', 0, 0, tiled=True)  12.3 us
    pallas_call x8, Pallas kernels, call(): pl.pallas_call(kernel, out_shape=outs, in_specs=[pl.BlockSpec(memory_spac...  7.61 us
    ppermute x1, starting transfers between devices, body(): received = lax.ppermute(send, 'site', swaps(hours, distance))  2.92 us
    ppermute x1, waiting for transfers between devices, body(): near = lax.ppermute(own, ('tm', 'site'), near_swap)  2.68 us
    ppermute x1, starting transfers between devices, body(): received = lax.ppermute(shift, 'tm', swaps(blocks, distance))  2.65 us
    ppermute x1, waiting for transfers between devices, body(): received = lax.ppermute(shift, 'tm', swaps(blocks, distance))  1.97 us
    ppermute x1, waiting for transfers between devices, body(): other = lax.ppermute(maps, 'site', swaps(hours, 1))  1.94 us
    unnamed x6, local copies, waits for them, and re-layouts  1.9 us
  transfers between devices with their start and end apart: 8, of which 7 were waited for; matrix products, arithmetic and copies ran while one was open for 0% of the time, Pallas kernels for 1%

profile of v2, /device:TPU:0, one launch (start us, length us, event | category | flops | bytes accessed | tf_op | source)
XLA Modules:
  0.0 44.7 jit_solution(10850069602535865226)
XLA Ops:
  0.0 0.0 copy-start
  0.0 1.6 %local_grams.1 = (f32[1,264,256]{2,1,0:T(8,128)S(1)}, f32[1,264,256]{2,1,0:T(8,128)S(1)}) custom-call(bf16[512,256]{1,0:T(8,128)(2,1)} %rows_hbm.1, bf16[512]{0:T(512)(128)(2,1)} %values_hbm.1, s32[512]{0:T(512)} %codes_hbm.1), custom_call_target="tpu_custom_call" | custom-call | tf_op jit(solution)/shard_map/local_grams/pallas_call | solution.py:24
  1.6 0.5 %collective-permute-start = (f32[1,264,256]{2,1,0:T(8,128)S(1)}, f32[1,264,256]{2,1,0:T(8,128)S(1)}, u32[]{:S(2)}, u32[]{:S(2)}) collective-permute-start(f32[1,264,256]{2,1,0:T(8,128)S(1)} %get-tuple-element.17), channel_id=1, source_target_pairs={{0,1},{1,0},{2,3},{3,2},{4,5},{5,4},{6,7},{7,6},{8,9},{9,8},{10,11... | collective-permute-start | bytes 811016 | tf_op jit(solution)/shard_map/ppermute | solution.py:336
  2.2 1.2 %collective-permute-done.received_ref = f32[1,264,256]{2,1,0:T(8,128)S(1)} collective-permute-done((f32[1,264,256]{2,1,0:T(8,128)S(1)}, f32[1,264,256]{2,1,0:T(8,128)S(1)}, u32[]{:S(2)}, u32[]{:S(2)}) %collective-permute-start) | collective-permute-done | bytes 270368 | tf_op jit(solution)/shard_map/ppermute | solution.py:336
  3.4 2.9 %collective-permute-start.1 = (bf16[1,272,256]{2,1,0:T(8,128)(2,1)S(1)}, bf16[1,272,256]{2,1,0:T(8,128)(2,1)S(1)}, u32[]{:S(2)}, u32[]{:S(2)}) collective-permute-start(bf16[1,272,256]{2,1,0:T(8,128)(2,1)S(1)} %get-tuple-element.19), channel_id=1, source_target_pairs={{0,2},{1,3},{2,0},{3,1},{4,6},{5,7},{6,4},{7,5},{8,10},{9,11},{10,... | collective-permute-start | bytes 417800 | tf_op jit(solution)/shard_map/ppermute | solution.py:341
  6.3 0.0 copy-start.1
  6.3 0.9 %copy-done.1 = f32[256,256]{1,0:T(8,128)S(1)} copy-done((f32[256,256]{1,0:T(8,128)S(1)}, f32[256,256]{1,0:T(8,128)}, u32[]{:S(2)}) %copy-start.1) | copy-done | bytes 262168
  7.2 0.0 copy-start.2
  7.3 0.9 %copy-done.2 = f32[256,256]{1,0:T(8,128)S(1)} copy-done((f32[256,256]{1,0:T(8,128)S(1)}, f32[256,256]{1,0:T(8,128)}, u32[]{:S(2)}) %copy-start.2) | copy-done | bytes 262168
  8.2 0.3 coupled_turned.1
  8.5 1.8 %collective-permute-done.1.received_ref = bf16[1,272,256]{2,1,0:T(8,128)(2,1)S(1)} collective-permute-done((bf16[1,272,256]{2,1,0:T(8,128)(2,1)S(1)}, bf16[1,272,256]{2,1,0:T(8,128)(2,1)S(1)}, u32[]{:S(2)}, u32[]{:S(2)}) %collective-permute-start.1) | collective-permute-done | bytes 139296 | tf_op jit(solution)/shard_map/ppermute | solution.py:341
  10.3 4.0 %hour_maps.1.own_ref.refs_0_ = f32[2,272,256]{2,1,0:T(8,128)S(1)} custom-call(f32[1,264,256]{2,1,0:T(8,128)S(1)} %get-tuple-element.18.sum_ref, bf16[1,272,256]{2,1,0:T(8,128)(2,1)S(1)} %collective-permute-done.1.received_ref, f32[256,256]{1,0:T(8,128)S(1)} %get-tuple-element.20.prior_ref, f32[256,256]{1,0:T(8,128)S(1)} %get-tuple-element.21.turned_ref), custom_call_target="tpu_custom_call" | custom-call | tf_op jit(solution)/shard_map/hour_maps/pallas_call | solution.py:24
  14.3 0.1 collective-permute-start.2
  14.4 1.9 %collective-permute-done.2.received_ref.refs_1_ = f32[2,272,256]{2,1,0:T(8,128)S(1)} collective-permute-done((f32[2,272,256]{2,1,0:T(8,128)S(1)}, f32[2,272,256]{2,1,0:T(8,128)S(1)}, u32[]{:S(2)}, u32[]{:S(2)}) %collective-permute-start.2) | collective-permute-done | bytes 557088 | tf_op jit(solution)/shard_map/ppermute | solution.py:352
  16.3 0.3 block_map.1
  16.7 1.8 %collective-permute-start.3 = (bf16[272,256]{1,0:T(8,128)(2,1)S(1)}, bf16[272,256]{1,0:T(8,128)(2,1)S(1)}, u32[]{:S(2)}, u32[]{:S(2)}) collective-permute-start(bf16[272,256]{1,0:T(8,128)(2,1)S(1)} %get-tuple-element.22.own_ref.refs_0_.refs_3_), channel_id=1, source_target_pairs={{0,4},{1,9},{2,6},{3,11},{4,0},{5,13},{6,2},{7,15},{8,12},{9,1},{1... | collective-permute-start | bytes 417800 | tf_op jit(solution)/shard_map/ppermute | solution.py:365
  18.5 1.5 %collective-permute-start.4 = (bf16[144,256]{1,0:T(8,128)(2,1)S(1)}, bf16[144,256]{1,0:T(8,128)(2,1)S(1)}, u32[]{:S(2)}, u32[]{:S(2)}) collective-permute-start(bf16[144,256]{1,0:T(8,128)(2,1)S(1)} %get-tuple-element.23), channel_id=1, source_target_pairs={{0,12},{1,13},{2,14},{3,15},{4,8},{5,9},{6,10},{7,11},{8,4},{9,5},... | collective-permute-start | bytes 221192 | tf_op jit(solution)/shard_map/ppermute | solution.py:366
  20.0 2.7 %collective-permute-done.3.near_ref = bf16[272,256]{1,0:T(8,128)(2,1)S(1)} collective-permute-done((bf16[272,256]{1,0:T(8,128)(2,1)S(1)}, bf16[272,256]{1,0:T(8,128)(2,1)S(1)}, u32[]{:S(2)}, u32[]{:S(2)}) %collective-permute-start.3) | collective-permute-done | bytes 139296 | tf_op jit(solution)/shard_map/ppermute | solution.py:365
  22.7 0.0 collective-permute-start.5
  22.7 1.1 %collective-permute-done.4.part_ref = bf16[144,256]{1,0:T(8,128)(2,1)S(1)} collective-permute-done((bf16[144,256]{1,0:T(8,128)(2,1)S(1)}, bf16[144,256]{1,0:T(8,128)(2,1)S(1)}, u32[]{:S(2)}, u32[]{:S(2)}) %collective-permute-start.4) | collective-permute-done | bytes 73760 | tf_op jit(solution)/shard_map/ppermute | solution.py:366
  23.8 0.0 collective-permute-start.6
  23.8 1.3 %collective-permute-done.6.other_part_ref = bf16[144,256]{1,0:T(8,128)(2,1)S(1)} collective-permute-done((bf16[144,256]{1,0:T(8,128)(2,1)S(1)}, bf16[144,256]{1,0:T(8,128)(2,1)S(1)}, u32[]{:S(2)}, u32[]{:S(2)}) %collective-permute-start.6) | collective-permute-done | bytes 73760 | tf_op jit(solution)/shard_map/ppermute | solution.py:368
  25.0 0.0 collective-permute-done.5.other_near_ref
  25.1 0.4 %group_shift.1 = f32[8,256]{1,0:T(8,128)S(1)} custom-call(bf16[272,256]{1,0:T(8,128)(2,1)S(1)} %get-tuple-element.22.own_ref.refs_0_.refs_3_, bf16[272,256]{1,0:T(8,128)(2,1)S(1)} %get-tuple-element.24.refs_1_.refs_4_, bf16[272,256]{1,0:T(8,128)(2,1)S(1)} %get-tuple-element.25.refs_2_.refs_5_, bf16[272,256]{1,0:T(8,128)(2,1)S(1)} %get-tuple-element.26.refs_3_.refs_6_), custom_call_target="tpu_custom_call" | custom-call | tf_op jit(solution)/shard_map/group_shift/pallas_call | solution.py:24
  25.5 2.6 %collective-permute-start.7 = (f32[8,256]{1,0:T(8,128)S(1)}, f32[8,256]{1,0:T(8,128)S(1)}, u32[]{:S(2)}, u32[]{:S(2)}) collective-permute-start(f32[8,256]{1,0:T(8,128)S(1)} %group_shift.1), channel_id=1, source_target_pairs={{0,16},{4,20},{8,24},{12,28},{16,0},{20,4},{24,8},{28,12},{1,17},{... | collective-permute-start | bytes 24584 | tf_op jit(solution)/shard_map/ppermute | solution.py:384
  28.2 2.0 %collective-permute-done.7.refs_2_ = f32[8,256]{1,0:T(8,128)S(1)} collective-permute-done((f32[8,256]{1,0:T(8,128)S(1)}, f32[8,256]{1,0:T(8,128)S(1)}, u32[]{:S(2)}, u32[]{:S(2)}) %collective-permute-start.7) | collective-permute-done | bytes 8224 | tf_op jit(solution)/shard_map/ppermute | solution.py:384
  30.1 0.8 %block_means.1 = bf16[8,4,256]{2,1,0:T(4,128)(2,1)S(1)} custom-call(f32[2,272,256]{2,1,0:T(8,128)S(1)} %hour_maps.1.own_ref.refs_0_, f32[2,272,256]{2,1,0:T(8,128)S(1)} %collective-permute-done.2.received_ref.refs_1_, f32[8,256]{1,0:T(8,128)S(1)} %collective-permute-done.7.refs_2_, bf16[272,256]{1,0:T(8,128)(2,1)S(1)} %get-tuple-element.22.own_ref.refs_0_.refs_3_, ...), custom_call_target="tpu_custom_call" | custom-call | tf_op jit(solution)/shard_map/block_means/pallas_call | solution.py:24
  30.9 12.3 %all_to_all.5 = bf16[8,4,256]{2,1,0:T(4,128)(2,1)S(1)} all-to-all(bf16[8,4,256]{2,1,0:T(4,128)(2,1)S(1)} %block_means.1), channel_id=1, replica_groups=mesh['tm'=8,'site'=4] {'tm'}, dimensions={0} | all-to-all | bytes 32768 | tf_op jit(solution)/shard_map/all_to_all | solution.py:402
  43.2 0.0 copy-done
  43.2 1.4 %convolution_convert_fusion = bf16[32,4096]{1,0:T(8,128)(2,1)} fusion(bf16[32,256]{1,0:T(8,128)(2,1)S(1)} %reshape.3, bf16[4096,256]{1,0:T(8,128)(2,1)S(1)} %copy-done), kind=kOutput, calls=%fused_computation | convolution fusion | flops 67239936 | bytes 2375680 | tf_op jit(solution)/shard_map/hs,ns->hn/dot_general | solution.py:403
  (3 shorter events, 0.1 us)
Async XLA Ops:
  0.0 43.2 %copy-start = (bf16[4096,256]{1,0:T(8,128)(2,1)S(1)}, bf16[4096,256]{1,0:T(8,128)(2,1)}, u32[]{:S(2)}) copy-start(bf16[4096,256]{1,0:T(8,128)(2,1)} %param.11) | copy-start | bytes 6291460
  1.6 1.7 %collective-permute-start = (f32[1,264,256]{2,1,0:T(8,128)S(1)}, f32[1,264,256]{2,1,0:T(8,128)S(1)}, u32[]{:S(2)}, u32[]{:S(2)}) collective-permute-start(f32[1,264,256]{2,1,0:T(8,128)S(1)} %get-tuple-element.17), channel_id=1, source_target_pairs={{0,1},{1,0},{2,3},{3,2},{4,5},{5,4},{6,7},{7,6},{8,9},{9,8},{10,11... | collective-permute-start | bytes 811016 | tf_op jit(solution)/shard_map/ppermute | solution.py:336
  3.4 6.9 %collective-permute-start.1 = (bf16[1,272,256]{2,1,0:T(8,128)(2,1)S(1)}, bf16[1,272,256]{2,1,0:T(8,128)(2,1)S(1)}, u32[]{:S(2)}, u32[]{:S(2)}) collective-permute-start(bf16[1,272,256]{2,1,0:T(8,128)(2,1)S(1)} %get-tuple-element.19), channel_id=1, source_target_pairs={{0,2},{1,3},{2,0},{3,1},{4,6},{5,7},{6,4},{7,5},{8,10},{9,11},{10,... | collective-permute-start | bytes 417800 | tf_op jit(solution)/shard_map/ppermute | solution.py:341
  6.3 0.9 %copy-start.1 = (f32[256,256]{1,0:T(8,128)S(1)}, f32[256,256]{1,0:T(8,128)}, u32[]{:S(2)}) copy-start(f32[256,256]{1,0:T(8,128)} %prior_ref.1) | copy-start | bytes 786436
  7.2 0.9 %copy-start.2 = (f32[256,256]{1,0:T(8,128)S(1)}, f32[256,256]{1,0:T(8,128)}, u32[]{:S(2)}) copy-start(f32[256,256]{1,0:T(8,128)} %transition_ref.1) | copy-start | bytes 786436
  14.3 2.0 %collective-permute-start.2 = (f32[2,272,256]{2,1,0:T(8,128)S(1)}, f32[2,272,256]{2,1,0:T(8,128)S(1)}, u32[]{:S(2)}, u32[]{:S(2)}) collective-permute-start(f32[2,272,256]{2,1,0:T(8,128)S(1)} %hour_maps.1.own_ref.refs_0_), channel_id=1, source_target_pairs={{0,1},{1,0},{2,3},{3,2},{4,5},{5,4},{6,7},{7,6},{8,9},{9,8},{10,11... | collective-permute-start | bytes 1671176 | tf_op jit(solution)/shard_map/ppermute | solution.py:352
  16.7 6.0 %collective-permute-start.3 = (bf16[272,256]{1,0:T(8,128)(2,1)S(1)}, bf16[272,256]{1,0:T(8,128)(2,1)S(1)}, u32[]{:S(2)}, u32[]{:S(2)}) collective-permute-start(bf16[272,256]{1,0:T(8,128)(2,1)S(1)} %get-tuple-element.22.own_ref.refs_0_.refs_3_), channel_id=1, source_target_pairs={{0,4},{1,9},{2,6},{3,11},{4,0},{5,13},{6,2},{7,15},{8,12},{9,1},{1... | collective-permute-start | bytes 417800 | tf_op jit(solution)/shard_map/ppermute | solution.py:365
  18.5 5.3 %collective-permute-start.4 = (bf16[144,256]{1,0:T(8,128)(2,1)S(1)}, bf16[144,256]{1,0:T(8,128)(2,1)S(1)}, u32[]{:S(2)}, u32[]{:S(2)}) collective-permute-start(bf16[144,256]{1,0:T(8,128)(2,1)S(1)} %get-tuple-element.23), channel_id=1, source_target_pairs={{0,12},{1,13},{2,14},{3,15},{4,8},{5,9},{6,10},{7,11},{8,4},{9,5},... | collective-permute-start | bytes 221192 | tf_op jit(solution)/shard_map/ppermute | solution.py:366
  22.7 2.3 %collective-permute-start.5 = (bf16[272,256]{1,0:T(8,128)(2,1)S(1)}, bf16[272,256]{1,0:T(8,128)(2,1)S(1)}, u32[]{:S(2)}, u32[]{:S(2)}) collective-permute-start(bf16[272,256]{1,0:T(8,128)(2,1)S(1)} %collective-permute-done.3.near_ref), channel_id=1, source_target_pairs={{0,1},{1,0},{2,3},{3,2},{4,5},{5,4},{6,7},{7,6},{8,9},{9,8},{10,11... | collective-permute-start | bytes 417800 | tf_op jit(solution)/shard_map/ppermute | solution.py:367
  23.8 1.3 %collective-permute-start.6 = (bf16[144,256]{1,0:T(8,128)(2,1)S(1)}, bf16[144,256]{1,0:T(8,128)(2,1)S(1)}, u32[]{:S(2)}, u32[]{:S(2)}) collective-permute-start(bf16[144,256]{1,0:T(8,128)(2,1)S(1)} %collective-permute-done.4.part_ref), channel_id=1, source_target_pairs={{0,1},{1,0},{2,3},{3,2},{4,5},{5,4},{6,7},{7,6},{8,9},{9,8},{10,11... | collective-permute-start | bytes 221192 | tf_op jit(solution)/shard_map/ppermute | solution.py:368
  25.5 4.6 %collective-permute-start.7 = (f32[8,256]{1,0:T(8,128)S(1)}, f32[8,256]{1,0:T(8,128)S(1)}, u32[]{:S(2)}, u32[]{:S(2)}) collective-permute-start(f32[8,256]{1,0:T(8,128)S(1)} %group_shift.1), channel_id=1, source_target_pairs={{0,16},{4,20},{8,24},{12,28},{16,0},{20,4},{24,8},{28,12},{1,17},{... | collective-permute-start | bytes 24584 | tf_op jit(solution)/shard_map/ppermute | solution.py:384

commit v3 on v2

--- a/solution.py
+++ b/solution.py
@@ -9,6 +9,7 @@
 
 NS_ITERS = 8
 TAIL = 8
+CHUNKS = 4
 BF16 = jnp.bfloat16
 F32 = jnp.float32
 VMEM_LIMIT = 40 * 2**20
@@ -121,7 +122,8 @@
             )
 
 
-def coupled_turned(prior_ref, transition_ref, prior_out_ref, turned_ref):
+def prepare(prior_ref, transition_ref, basis_ref, prior_out_ref, turned_ref, basis_out_ref):
+    basis_out_ref[...] = basis_ref[...].T
     prior = prior_ref[...]
     prior_out_ref[...] = prior
     turned_ref[...] = dot_wide(transition_ref[...].T, prior)
@@ -150,7 +152,7 @@
     return sum_ref[pair] + jnp.concatenate([received[:states], tail], axis=0)
 
 
-def hour_maps(sum_ref, received_ref, prior_ref, turned_ref, out_ref):
+def hour_maps(sum_ref, received_ref, prior_ref, turned_ref, out_ref, last_ref, firsts_ref):
     states = prior_ref.shape[0]
     prior = prior_ref[...]
     turned = turned_ref[...]
@@ -184,11 +186,17 @@
         product = dot(jnp.concatenate([power, v.astype(BF16)], axis=0), power)
         v = v + product[states:]
         maps.append(v + dot(v.astype(BF16), product[:states].astype(BF16)))
-    joined = maps[0]
-    out_ref[0] = joined
-    for position in range(1, len(maps)):
-        joined = append(joined, maps[position])
+    for position in range(len(maps)):
+        joined = maps[0] if position == 0 else append(joined, maps[position])
         out_ref[position] = joined
+        if position < len(maps) - 1:
+            firsts_ref[position] = rounded(joined)
+    last_ref[...] = rounded(joined)
+
+
+def rounded(affine):
+    states = affine.shape[1]
+    return jnp.concatenate([affine[:states].astype(BF16), thirds(affine[states : states + 1])], axis=0)
 
 
 def append(earlier, latter):
@@ -197,32 +205,38 @@
     return jnp.concatenate([product[:states], product[states:] + latter[states:]], axis=0)
 
 
-def in_order(half, own_ref, received_ref):
-    first = own_half(2 * half) == 0
-    early = [jnp.where(first, own_ref[i], received_ref[i]) for i in range(half)]
-    late = [jnp.where(first, received_ref[i], own_ref[i]) for i in range(half)]
+def in_order(own_ref, received_ref):
+    first = lax.rem(lax.axis_index("site"), 2) == 0
+    count = len(own_ref) if isinstance(own_ref, list) else own_ref.shape[0]
+    early = [jnp.where(first, own_ref[i], received_ref[i]) for i in range(count)]
+    late = [jnp.where(first, received_ref[i], own_ref[i]) for i in range(count)]
     return early, late
 
 
 def block_map(own_ref, received_ref, out_ref, part_ref):
     half, rows, states = own_ref.shape
-    early, late = in_order(half, own_ref, received_ref)
-    joined = append(early[-1], late[-1])
-    out_ref[:states, :] = joined[:states].astype(BF16)
-    out_ref[states:, :] = thirds(joined[states : states + 1])
+    early, late = in_order(own_ref, received_ref)
+    out_ref[...] = rounded(append(early[-1], late[-1]))
     height = part_ref.shape[0]
     first = own_half(2 * half) == 0
     part_ref[...] = jnp.where(first, out_ref[:height, :], out_ref[rows - height :, :])
 
 
-def group_blocks(own_ref, near_ref, part_ref, other_near_ref, other_part_ref, *out_refs):
+def merge(last_ref, near_ref, far_ref, out_ref):
+    out_ref[...] = jnp.concatenate([last_ref[...], near_ref[...], far_ref[...]], axis=0)
+
+
+def group_blocks(merged_ref, other_ref, *out_refs):
     first = lax.rem(lax.axis_index("site"), 2) == 0
-    rows, height = own_ref.shape[0], part_ref.shape[0]
-    out_refs[0][...] = jnp.where(first, near_ref[...], other_near_ref[...])
-    out_refs[1][...] = jnp.where(first, other_near_ref[...], near_ref[...])
-    out_refs[2][:height, :] = jnp.where(first, part_ref[...], other_part_ref[...])
-    low = jnp.where(first, other_part_ref[...], part_ref[...])
-    out_refs[2][height:, :] = low[2 * height - rows :]
+    rows = out_refs[0].shape[0]
+    height = (merged_ref.shape[0] - rows) // 2
+    own, other = merged_ref[:rows, :], other_ref[:rows, :]
+    out_refs[0][...] = follow(jnp.where(first, own, other), jnp.where(first, other, own))
+    for place in range(2):
+        start = rows + place * height
+        part, other = merged_ref[start : start + height, :], other_ref[start : start + height, :]
+        low = jnp.where(first, other, part)[2 * height - rows :]
+        out_refs[1 + place][...] = jnp.concatenate([jnp.where(first, part, other), low], axis=0)
 
 
 def shift_of(block):
@@ -276,9 +290,14 @@
     return lax.rem(lax.axis_index("tm") // distance, 2) == 1
 
 
-def block_means(distances, *refs):
-    out_ref, own_ref, other_ref = refs[-1], refs[0], refs[1]
-    levels, gathered = refs[2 : 2 + len(distances)], refs[2 + len(distances) : -1]
+def hold(maps_ref, received_ref, out_ref):
+    out_ref[...] = maps_ref[...]
+
+
+def pair_means(distances, *refs):
+    out_ref = refs[-1]
+    own_ref, other_ref, last_ref, other_last_ref = refs[:4]
+    levels, gathered = refs[4 : 4 + len(distances)], refs[4 + len(distances) : -1]
     half, rows, states = own_ref.shape
     mean = jnp.zeros((1, states), F32)
     for level in reversed(range(len(distances))):
@@ -288,18 +307,66 @@
             entered = apply(levels[level][...], mean)
         mean = jnp.where(is_upper(distances[level]), entered, mean)
     place = lax.rem(lax.axis_index("tm"), len(gathered))
-    for i in range(len(gathered) - 1):
-        mean = jnp.where(i < place, apply(pick(gathered, place ^ i), mean), mean)
-    early, late = in_order(half, own_ref, other_ref)
-    results = []
-    for maps in (early, late):
-        start = mean
+    for i in range(2):
+        mean = jnp.where(place >= 2, apply(pick(gathered, place ^ i), mean), mean)
+    odd = lax.rem(place, 2) == 1
+    between = apply(pick(gathered, place & 1), mean)
+    own_start = jnp.where(odd, between, mean)
+    own = []
+    for maps in in_order(own_ref, other_ref):
+        start = own_start if not own else own[-1]
         for each in maps:
-            mean = row_times(start, *split(each[:states])) + each[states : states + 1]
-            results.append(mean)
-    results = jnp.concatenate(results, axis=0).astype(BF16)
+            own.append(row_times(start, *split(each[:states])) + each[states : states + 1])
+    state = jnp.where(odd, mean, own[-1])
+    partner = []
+    for maps in in_order([last_ref[:rows, :]], [other_last_ref[:rows, :]]):
+        partner += [state] * (half - 1)
+        state = apply(maps[0], state)
+        partner.append(state)
+    own, partner = jnp.concatenate(own, axis=0), jnp.concatenate(partner, axis=0)
+    out_ref[: 2 * half, :] = jnp.where(odd, partner, own)
+    out_ref[2 * half :, :] = jnp.where(odd, own, partner)
+
+
+def rest_of_means(means_ref, firsts_ref, other_ref, out_ref):
+    count = firsts_ref.shape[0]
+    hours = 2 * (count + 1)
+    odd = lax.rem(lax.axis_index("tm"), 2) == 1
+    out_ref[...] = means_ref[...]
+    partner = jnp.where(odd, means_ref[:hours, :], means_ref[hours:, :])
+    for side, maps in enumerate(in_order(firsts_ref, other_ref)):
+        for i in range(count):
+            hour = side * (count + 1) + i
+            mean = apply(maps[i], partner[hour : hour + 1])
+            out_ref[pl.ds(jnp.where(odd, hour, hours + hour), 1), :] = mean
+
+
+def own_means(means_ref, out_ref):
+    hours = out_ref.shape[1]
+    odd = lax.rem(lax.axis_index("tm"), 2) == 1
+    means = jnp.where(odd, means_ref[hours:, :], means_ref[:hours, :]).astype(BF16)
     for copy in range(out_ref.shape[0]):
-        out_ref[copy] = results
+        out_ref[copy] = means
+
+
+def predict(*refs):
+    means_refs, basis_ref, out_hbm, held_ref, sems = refs[:-4], *refs[-4:]
+    if len(means_refs) > 1:
+        place = lax.axis_index("tm") // 2
+        means = [pick(means_refs, place ^ i) for i in range(len(means_refs))]
+        means = jnp.concatenate(means, axis=0).astype(BF16)
+    else:
+        means = means_refs[0][...]
+    width = held_ref.shape[2]
+    copies = []
+    for chunk in range(CHUNKS):
+        columns = pl.ds(chunk * width, width)
+        held_ref[chunk] = dot(means, basis_ref[:, columns]).astype(BF16)
+        copy = pltpu.make_async_copy(held_ref.at[chunk], out_hbm.at[:, columns], sems.at[chunk])
+        copy.start()
+        copies.append(copy)
+    for copy in copies:
+        copy.wait()
 
 
 def swaps(size, distance):
@@ -313,11 +380,12 @@
     half = hours // 2
     pairs = half // 2
     sds = jax.ShapeDtypeStruct
-    prior, turned = call(
-        coupled_turned,
-        (sds((states, states), F32), sds((states, states), F32)),
-        (prior_precision, transition),
-        "coupled_turned",
+    square = sds((states, states), F32)
+    prior, turned, basis = call(
+        prepare,
+        (square, square, sds(site_basis.shape[::-1], BF16)),
+        (prior_precision, transition, site_basis),
+        "prepare",
     )
     packed = sds((pairs, states + TAIL, states), F32)
     keep, send = call(
@@ -343,33 +411,29 @@
         if distance < hours:
             keep = call(add_received, packed, (total, received), "add_received")
             received = jnp.zeros_like(keep)
-    maps = call(
+    rows = states + 16
+    block, height = sds((rows, states), BF16), (rows // 2 + 15) // 16 * 16
+    firsts = sds((half - 1, rows, states), BF16)
+    maps, last, first_maps = call(
         hour_maps,
-        sds((half, states + 16, states), F32),
+        (sds((half, rows, states), F32), block, firsts),
         (total, received, prior, turned),
         "hour_maps",
     )
     other = lax.ppermute(maps, "site", swaps(hours, 1))
-    rows = states + 16
-    height = (rows // 2 + 15) // 16 * 16
+    last = lax.ppermute(last, "tm", swaps(blocks, 1))
+    first_maps = lax.ppermute(first_maps, "tm", swaps(blocks, 1))
     own, part = call(
-        block_map,
-        (sds((rows, states), BF16), sds((height, states), BF16)),
-        (maps, other),
-        "block_map",
-    )
+        block_map, (block, sds((height, states), BF16)), (maps, other), "block_map"
+    )
+    near = lax.ppermute(part, "tm", swaps(blocks, 2))
+    far = lax.ppermute(part, "tm", swaps(blocks, 3))
+    merged = call(merge, sds((rows + 2 * height, states), BF16), (last, near, far), "merge")
+    other_merged = lax.ppermute(merged, "site", swaps(hours, 1))
     radix = 4
-    devices = [(t, d) for t in range(blocks) for d in range(hours)]
-    near_swap = [(t * hours + d, (t ^ (1 + d % 2)) * hours + d) for t, d in devices]
-    far_swap = [(t * hours + d, (t ^ 3) * hours + d) for t, d in devices]
-    near = lax.ppermute(own, ("tm", "site"), near_swap)
-    far = lax.ppermute(part, ("tm", "site"), far_swap)
-    other_near = lax.ppermute(near, "site", swaps(hours, 1))
-    other_far = lax.ppermute(far, "site", swaps(hours, 1))
-    block = sds(own.shape, BF16)
-    gathered = (own,) + call(
-        group_blocks, (block,) * 3, (own, near, far, other_near, other_far), "group_blocks"
-    )
+    gathered = (own,) + tuple(call(
+        group_blocks, (block,) * 3, (merged, other_merged), "group_blocks"
+    ))
     distances, levels = [], []
     distance = radix
     if 2 * distance < blocks:
@@ -394,13 +458,37 @@
         levels.append(received)
         distance *= 2
     means = call(
-        functools.partial(block_means, tuple(distances)),
-        sds((blocks, hours, states), BF16),
-        [maps, other] + levels + list(gathered),
-        "block_means",
-    )
-    means = lax.all_to_all(means, "tm", 0, 0, tiled=True).reshape(blocks * hours, states)
-    return jnp.einsum("hs,ns->hn", means, site_basis, preferred_element_type=F32).astype(BF16)
+        functools.partial(pair_means, tuple(distances)),
+        sds((2 * hours, states), F32),
+        [maps, other, merged, other_merged] + levels + list(gathered),
+        "pair_means",
+    )
+    first_maps = call(hold, firsts, (first_maps, levels[-1]), "hold")
+    other_firsts = lax.ppermute(first_maps, "site", swaps(hours, 1))
+    means = call(
+        rest_of_means,
+        sds(means.shape, F32),
+        (means, first_maps, other_firsts),
+        "rest_of_means",
+    )
+    if blocks <= 8:
+        means = [means] + [lax.ppermute(means, "tm", swaps(blocks, d)) for d in range(2, blocks, 2)]
+    else:
+        means = call(own_means, sds((blocks, hours, states), BF16), (means,), "own_means")
+        means = [lax.all_to_all(means, "tm", 0, 0, tiled=True).reshape(blocks * hours, states)]
+    sites = site_basis.shape[0]
+    return pl.pallas_call(
+        predict,
+        out_shape=sds((blocks * hours, sites), BF16),
+        in_specs=[whole()] * (len(means) + 1),
+        out_specs=pl.BlockSpec(memory_space=pltpu.HBM),
+        scratch_shapes=[
+            pltpu.VMEM((CHUNKS, blocks * hours, sites // CHUNKS), BF16),
+            pltpu.SemaphoreType.DMA((CHUNKS,)),
+        ],
+        compiler_params=pltpu.CompilerParams(vmem_limit_bytes=VMEM_LIMIT),
+        name="predict",
+    )(*means, basis)
 
 
 def solution(mesh):

time: 44.9 us -> 41.9 us (0.933)
  blocking collectives: 12.3 us -> 0 us
  starting transfers between devices: 9.51 us -> 16 us
  Pallas kernels: 7.61 us -> 9.73 us
  local copies, waits for them, and re-layouts: 1.91 us -> 3.49 us
  matrix products: 1.43 us -> 0 us
  waiting for transfers between devices: 11.8 us -> 12.4 us
    all_to_all x1 -> x0, blocking collectives: 12.3 us -> none  [body(): lax.all_to_all(means, 'tm', 0, 0, tiled=True)]
    ppermute x4 -> x9, starting transfers between devices: 3.35 us -> 9.8 us  [the longest x3 4.45 us: body(): lax.ppermute(means, 'tm', swaps(blocks, d))]
    ppermute x4 -> x9, waiting for transfers between devices: 5 us -> 10.1 us  [the longest x3 3.74 us: body(): lax.ppermute(means, 'tm', swaps(blocks, d))]
    ppermute x1, waiting for transfers between devices: 1.76 us -> 0.01 us  [body(): received = lax.ppermute(send, 'site', swaps(hours, distance))]
    unnamed x6, local copies, waits for them, and re-layouts: 1.9 us -> 3.49 us
    ppermute x1, waiting for transfers between devices: 1.94 us -> 0.36 us  [body(): other = lax.ppermute(maps, 'site', swaps(hours, 1))]
    dot_general x1 -> x0, matrix products: 1.43 us -> none  [body(): jnp.einsum('hs,ns->hn', means, site_basis, preferred_element_type=F32)]
    ppermute x1, waiting for transfers between devices: 1.97 us -> 0.77 us  [body(): received = lax.ppermute(shift, 'tm', swaps(blocks, distance))]
  transfers between devices with their start and end apart: 8 -> 13, of which waited for: 7 -> 11; matrix products, arithmetic and copies ran while one was open for 0% -> 0% of each run, Pallas kernels for 1% -> 7%
where the time goes in v3:
time: 41.9 us; the launch traced here: 41.7 us
  starting transfers between devices  16 us (38%)
  waiting for transfers between devices  12.4 us (30%)
  Pallas kernels  9.73 us (23%)
  local copies, waits for them, and re-layouts  3.49 us (8%)
    pallas_call x11, Pallas kernels, call(): pl.pallas_call(kernel, out_shape=outs, in_specs=[pl.BlockSpec(memory_spac...  8.59 us
    ppermute x3, starting transfers between devices, body(): lax.ppermute(means, 'tm', swaps(blocks, d))  4.45 us
    ppermute x3, waiting for transfers between devices, body(): lax.ppermute(means, 'tm', swaps(blocks, d))  3.74 us
    unnamed x6, local copies, waits for them, and re-layouts  3.49 us
    ppermute x1, starting transfers between devices, body(): received = lax.ppermute(send, 'site', swaps(hours, distance))  2.92 us
    ppermute x1, starting transfers between devices, body(): received = lax.ppermute(shift, 'tm', swaps(blocks, distance))  2.66 us
    ppermute x1, starting transfers between devices, body(): far = lax.ppermute(part, 'tm', swaps(blocks, 3))  2.6 us
    ppermute x1, waiting for transfers between devices, body(): last = lax.ppermute(last, 'tm', swaps(blocks, 1))  2.02 us
  transfers between devices with their start and end apart: 13, of which 11 were waited for; matrix products, arithmetic and copies ran while one was open for 0% of the time, Pallas kernels for 7%

profile of v3, /device:TPU:0, one launch (start us, length us, event | category | flops | bytes accessed | tf_op | source)
XLA Modules:
  0.0 41.7 jit_solution(5822396610516057771)
XLA Ops:
  0.0 1.5 %local_grams.1 = (f32[1,264,256]{2,1,0:T(8,128)S(1)}, f32[1,264,256]{2,1,0:T(8,128)S(1)}) custom-call(bf16[512,256]{1,0:T(8,128)(2,1)} %rows_hbm.1, bf16[512]{0:T(512)(128)(2,1)} %values_hbm.1, s32[512]{0:T(512)} %codes_hbm.1), custom_call_target="tpu_custom_call" | custom-call | tf_op jit(solution)/shard_map/local_grams/pallas_call | solution.py:25
  1.5 0.5 %collective-permute-start = (f32[1,264,256]{2,1,0:T(8,128)S(1)}, f32[1,264,256]{2,1,0:T(8,128)S(1)}, u32[]{:S(2)}, u32[]{:S(2)}) collective-permute-start(f32[1,264,256]{2,1,0:T(8,128)S(1)} %get-tuple-element.21), channel_id=1, source_target_pairs={{0,1},{1,0},{2,3},{3,2},{4,5},{5,4},{6,7},{7,6},{8,9},{9,8},{10,11... | collective-permute-start | bytes 811016 | tf_op jit(solution)/shard_map/ppermute | solution.py:404
  2.0 1.2 %collective-permute-done.received_ref = f32[1,264,256]{2,1,0:T(8,128)S(1)} collective-permute-done((f32[1,264,256]{2,1,0:T(8,128)S(1)}, f32[1,264,256]{2,1,0:T(8,128)S(1)}, u32[]{:S(2)}, u32[]{:S(2)}) %collective-permute-start) | collective-permute-done | bytes 270368 | tf_op jit(solution)/shard_map/ppermute | solution.py:404
  3.2 2.9 %collective-permute-start.1 = (bf16[1,272,256]{2,1,0:T(8,128)(2,1)S(1)}, bf16[1,272,256]{2,1,0:T(8,128)(2,1)S(1)}, u32[]{:S(2)}, u32[]{:S(2)}) collective-permute-start(bf16[1,272,256]{2,1,0:T(8,128)(2,1)S(1)} %get-tuple-element.23), channel_id=1, source_target_pairs={{0,2},{1,3},{2,0},{3,1},{4,6},{5,7},{6,4},{7,5},{8,10},{9,11},{10,... | collective-permute-start | bytes 417800 | tf_op jit(solution)/shard_map/ppermute | solution.py:409
  6.1 0.0 copy-start
  6.1 1.6 %copy-done = bf16[4096,256]{1,0:T(8,128)(2,1)S(1)} copy-done((bf16[4096,256]{1,0:T(8,128)(2,1)S(1)}, bf16[4096,256]{1,0:T(8,128)(2,1)}, u32[]{:S(2)}) %copy-start) | copy-done | bytes 2097176
  7.7 0.0 copy-start.1
  7.7 0.9 %copy-done.1 = f32[256,256]{1,0:T(8,128)S(1)} copy-done((f32[256,256]{1,0:T(8,128)S(1)}, f32[256,256]{1,0:T(8,128)}, u32[]{:S(2)}) %copy-start.1) | copy-done | bytes 262168
  8.7 0.0 copy-start.2
  8.7 0.9 %copy-done.2 = f32[256,256]{1,0:T(8,128)S(1)} copy-done((f32[256,256]{1,0:T(8,128)S(1)}, f32[256,256]{1,0:T(8,128)}, u32[]{:S(2)}) %copy-start.2) | copy-done | bytes 262168
  9.6 0.8 %prepare.1 = (f32[256,256]{1,0:T(8,128)S(1)}, f32[256,256]{1,0:T(8,128)S(1)}, bf16[256,4096]{1,0:T(8,128)(2,1)S(1)}) custom-call(f32[256,256]{1,0:T(8,128)S(1)} %copy-done.1, f32[256,256]{1,0:T(8,128)S(1)} %copy-done.2, bf16[4096,256]{1,0:T(8,128)(2,1)S(1)} %copy-done), custom_call_target="tpu_custom_call" | custom-call | tf_op jit(solution)/shard_map/prepare/pallas_call | solution.py:25
  10.4 0.0 collective-permute-done.1.received_ref
  10.4 4.0 %hour_maps.1 = (f32[2,272,256]{2,1,0:T(8,128)S(1)}, bf16[272,256]{1,0:T(8,128)(2,1)S(1)}, bf16[1,272,256]{2,1,0:T(8,128)(2,1)S(1)}) custom-call(f32[1,264,256]{2,1,0:T(8,128)S(1)} %get-tuple-element.22.sum_ref, bf16[1,272,256]{2,1,0:T(8,128)(2,1)S(1)} %collective-permute-done.1.received_ref, f32[256,256]{1,0:T(8,128)S(1)} %get-tuple-element.24.prior_ref, ...), custom_call_target="tpu_custom_call" | custom-call | tf_op jit(solution)/shard_map/hour_maps/pallas_call | solution.py:25
  14.5 0.1 collective-permute-start.2
  14.6 1.6 %collective-permute-start.3 = (bf16[272,256]{1,0:T(8,128)(2,1)S(1)}, bf16[272,256]{1,0:T(8,128)(2,1)S(1)}, u32[]{:S(2)}, u32[]{:S(2)}) collective-permute-start(bf16[272,256]{1,0:T(8,128)(2,1)S(1)} %get-tuple-element.27), channel_id=1, source_target_pairs={{0,4},{4,0},{8,12},{12,8},{16,20},{20,16},{24,28},{28,24},{1,5},{5... | collective-permute-start | bytes 417800 | tf_op jit(solution)/shard_map/ppermute | solution.py:424
  16.1 0.4 collective-permute-done.2.received_ref.refs_1_
  16.5 0.3 block_map.1
  16.8 2.6 %collective-permute-start.5 = (bf16[144,256]{1,0:T(8,128)(2,1)S(1)}, bf16[144,256]{1,0:T(8,128)(2,1)S(1)}, u32[]{:S(2)}, u32[]{:S(2)}) collective-permute-start(bf16[144,256]{1,0:T(8,128)(2,1)S(1)} %get-tuple-element.28), channel_id=1, source_target_pairs={{0,12},{4,8},{8,4},{12,0},{16,28},{20,24},{24,20},{28,16},{1,13},{... | collective-permute-start | bytes 221192 | tf_op jit(solution)/shard_map/ppermute | solution.py:430
  19.4 0.4 %collective-permute-start.4 = (bf16[144,256]{1,0:T(8,128)(2,1)S(1)}, bf16[144,256]{1,0:T(8,128)(2,1)S(1)}, u32[]{:S(2)}, u32[]{:S(2)}) collective-permute-start(bf16[144,256]{1,0:T(8,128)(2,1)S(1)} %get-tuple-element.28), channel_id=1, source_target_pairs={{0,8},{4,12},{8,0},{12,4},{16,24},{20,28},{24,16},{28,20},{1,9},{5... | collective-permute-start | bytes 221192 | tf_op jit(solution)/shard_map/ppermute | solution.py:429
  19.9 2.0 %collective-permute-done.3.last_ref = bf16[272,256]{1,0:T(8,128)(2,1)S(1)} collective-permute-done((bf16[272,256]{1,0:T(8,128)(2,1)S(1)}, bf16[272,256]{1,0:T(8,128)(2,1)S(1)}, u32[]{:S(2)}, u32[]{:S(2)}) %collective-permute-start.3) | collective-permute-done | bytes 139296 | tf_op jit(solution)/shard_map/ppermute | solution.py:424
  21.9 0.7 %collective-permute-done.5.far_ref = bf16[144,256]{1,0:T(8,128)(2,1)S(1)} collective-permute-done((bf16[144,256]{1,0:T(8,128)(2,1)S(1)}, bf16[144,256]{1,0:T(8,128)(2,1)S(1)}, u32[]{:S(2)}, u32[]{:S(2)}) %collective-permute-start.5) | collective-permute-done | bytes 73760 | tf_op jit(solution)/shard_map/ppermute | solution.py:430
  22.6 1.2 %collective-permute-done.4.near_ref = bf16[144,256]{1,0:T(8,128)(2,1)S(1)} collective-permute-done((bf16[144,256]{1,0:T(8,128)(2,1)S(1)}, bf16[144,256]{1,0:T(8,128)(2,1)S(1)}, u32[]{:S(2)}, u32[]{:S(2)}) %collective-permute-start.4) | collective-permute-done | bytes 73760 | tf_op jit(solution)/shard_map/ppermute | solution.py:429
  23.8 0.1 collective-permute-start.6
  23.9 0.6 %collective-permute-start.8 = (bf16[1,272,256]{2,1,0:T(8,128)(2,1)S(1)}, bf16[1,272,256]{2,1,0:T(8,128)(2,1)S(1)}, u32[]{:S(2)}, u32[]{:S(2)}) collective-permute-start(bf16[1,272,256]{2,1,0:T(8,128)(2,1)S(1)} %get-tuple-element.33), channel_id=1, source_target_pairs={{0,4},{4,0},{8,12},{12,8},{16,20},{20,16},{24,28},{28,24},{1,5},{5... | collective-permute-start | bytes 417800 | tf_op jit(solution)/shard_map/ppermute | solution.py:425
  24.5 1.0 %collective-permute-done.6.other_ref.refs_3_ = bf16[560,256]{1,0:T(8,128)(2,1)S(1)} collective-permute-done((bf16[560,256]{1,0:T(8,128)(2,1)S(1)}, bf16[560,256]{1,0:T(8,128)(2,1)S(1)}, u32[]{:S(2)}, u32[]{:S(2)}) %collective-permute-start.6) | collective-permute-done | bytes 286752 | tf_op jit(solution)/shard_map/ppermute | solution.py:432
  25.4 0.2 group_blocks.1
  25.7 0.4 %group_shift.1 = f32[8,256]{1,0:T(8,128)S(1)} custom-call(bf16[272,256]{1,0:T(8,128)(2,1)S(1)} %get-tuple-element.29.refs_0_.refs_5_, bf16[272,256]{1,0:T(8,128)(2,1)S(1)} %get-tuple-element.30.refs_1_.refs_6_, bf16[272,256]{1,0:T(8,128)(2,1)S(1)} %get-tuple-element.31.refs_2_.refs_7_, bf16[272,256]{1,0:T(8,128)(2,1)S(1)} %get-tuple-element.32.refs_3_.refs_8_), custom_call_target="tpu_custom_call" | custom-call | tf_op jit(solution)/shard_map/group_shift/pallas_call | solution.py:25
  26.1 2.7 %collective-permute-start.7 = (f32[8,256]{1,0:T(8,128)S(1)}, f32[8,256]{1,0:T(8,128)S(1)}, u32[]{:S(2)}, u32[]{:S(2)}) collective-permute-start(f32[8,256]{1,0:T(8,128)S(1)} %group_shift.1), channel_id=1, source_target_pairs={{0,16},{4,20},{8,24},{12,28},{16,0},{20,4},{24,8},{28,12},{1,17},{... | collective-permute-start | bytes 24584 | tf_op jit(solution)/shard_map/ppermute | solution.py:448
  28.8 1.2 %collective-permute-done.8.maps_ref = bf16[1,272,256]{2,1,0:T(8,128)(2,1)S(1)} collective-permute-done((bf16[1,272,256]{2,1,0:T(8,128)(2,1)S(1)}, bf16[1,272,256]{2,1,0:T(8,128)(2,1)S(1)}, u32[]{:S(2)}, u32[]{:S(2)}) %collective-permute-start.8) | collective-permute-done | bytes 139296 | tf_op jit(solution)/shard_map/ppermute | solution.py:425
  30.0 0.8 %collective-permute-done.7.refs_4_.received_ref = f32[8,256]{1,0:T(8,128)S(1)} collective-permute-done((f32[8,256]{1,0:T(8,128)S(1)}, f32[8,256]{1,0:T(8,128)S(1)}, u32[]{:S(2)}, u32[]{:S(2)}) %collective-permute-start.7) | collective-permute-done | bytes 8224 | tf_op jit(solution)/shard_map/ppermute | solution.py:448
  30.8 0.1 collective-permute-start.9
  30.8 1.1 %pair_means.1.means_ref = f32[8,256]{1,0:T(8,128)S(1)} custom-call(f32[2,272,256]{2,1,0:T(8,128)S(1)} %get-tuple-element.26.own_ref.refs_0_, f32[2,272,256]{2,1,0:T(8,128)S(1)} %collective-permute-done.2.received_ref.refs_1_, bf16[560,256]{1,0:T(8,128)(2,1)S(1)} %merge.1.merged_ref.refs_2_, bf16[560,256]{1,0:T(8,128)(2,1)S(1)} %collective-permute-done.6.other_ref.refs_3_, ...), custom_call_target="tpu_custom_call" | custom-call | tf_op jit(solution)/shard_map/pair_means/pallas_call | solution.py:25
  31.9 0.3 collective-permute-done.9.other_ref
  32.2 0.2 rest_of_means.1.refs_0_
  32.4 3.6 %collective-permute-start.12 = (f32[8,256]{1,0:T(8,128)S(1)}, f32[8,256]{1,0:T(8,128)S(1)}, u32[]{:S(2)}, u32[]{:S(2)}) collective-permute-start(f32[8,256]{1,0:T(8,128)S(1)} %rest_of_means.1.refs_0_), channel_id=1, source_target_pairs={{0,24},{4,28},{8,16},{12,20},{16,8},{20,12},{24,0},{28,4},{1,25},{... | collective-permute-start | bytes 24584 | tf_op jit(solution)/shard_map/ppermute | solution.py:475
  36.0 0.0 collective-permute-start.11
  36.0 0.8 %collective-permute-start.10 = (f32[8,256]{1,0:T(8,128)S(1)}, f32[8,256]{1,0:T(8,128)S(1)}, u32[]{:S(2)}, u32[]{:S(2)}) collective-permute-start(f32[8,256]{1,0:T(8,128)S(1)} %rest_of_means.1.refs_0_), channel_id=1, source_target_pairs={{0,8},{4,12},{8,0},{12,4},{16,24},{20,28},{24,16},{28,20},{1,9},{5... | collective-permute-start | bytes 24584 | tf_op jit(solution)/shard_map/ppermute | solution.py:475
  36.8 1.1 %collective-permute-done.12.refs_3_ = f32[8,256]{1,0:T(8,128)S(1)} collective-permute-done((f32[8,256]{1,0:T(8,128)S(1)}, f32[8,256]{1,0:T(8,128)S(1)}, u32[]{:S(2)}, u32[]{:S(2)}) %collective-permute-start.12) | collective-permute-done | bytes 8224 | tf_op jit(solution)/shard_map/ppermute | solution.py:475
  37.9 2.7 %collective-permute-done.11.refs_2_ = f32[8,256]{1,0:T(8,128)S(1)} collective-permute-done((f32[8,256]{1,0:T(8,128)S(1)}, f32[8,256]{1,0:T(8,128)S(1)}, u32[]{:S(2)}, u32[]{:S(2)}) %collective-permute-start.11) | collective-permute-done | bytes 8224 | tf_op jit(solution)/shard_map/ppermute | solution.py:475
  40.6 0.0 collective-permute-done.10.refs_1_
  40.6 1.1 %predict.1 = bf16[32,4096]{1,0:T(8,128)(2,1)} custom-call(f32[8,256]{1,0:T(8,128)S(1)} %rest_of_means.1.refs_0_, f32[8,256]{1,0:T(8,128)S(1)} %collective-permute-done.10.refs_1_, f32[8,256]{1,0:T(8,128)S(1)} %collective-permute-done.11.refs_2_, f32[8,256]{1,0:T(8,128)S(1)} %collective-permute-done.12.refs_3_, bf16[256,4096]{1,0:T(8,128)(2,1)S(1)} %get-tuple-element.34.refs_4_), custom_call_target="tpu_custom_call" | custom-call | tf_op jit(solution)/shard_map/predict/pallas_call | solution.py:480
  (3 shorter events, 0.1 us)
Async XLA Ops:
  1.5 1.7 %collective-permute-start = (f32[1,264,256]{2,1,0:T(8,128)S(1)}, f32[1,264,256]{2,1,0:T(8,128)S(1)}, u32[]{:S(2)}, u32[]{:S(2)}) collective-permute-start(f32[1,264,256]{2,1,0:T(8,128)S(1)} %get-tuple-element.21), channel_id=1, source_target_pairs={{0,1},{1,0},{2,3},{3,2},{4,5},{5,4},{6,7},{7,6},{8,9},{9,8},{10,11... | collective-permute-start | bytes 811016 | tf_op jit(solution)/shard_map/ppermute | solution.py:404
  3.2 7.2 %collective-permute-start.1 = (bf16[1,272,256]{2,1,0:T(8,128)(2,1)S(1)}, bf16[1,272,256]{2,1,0:T(8,128)(2,1)S(1)}, u32[]{:S(2)}, u32[]{:S(2)}) collective-permute-start(bf16[1,272,256]{2,1,0:T(8,128)(2,1)S(1)} %get-tuple-element.23), channel_id=1, source_target_pairs={{0,2},{1,3},{2,0},{3,1},{4,6},{5,7},{6,4},{7,5},{8,10},{9,11},{10,... | collective-permute-start | bytes 417800 | tf_op jit(solution)/shard_map/ppermute | solution.py:409
  6.1 1.6 %copy-start = (bf16[4096,256]{1,0:T(8,128)(2,1)S(1)}, bf16[4096,256]{1,0:T(8,128)(2,1)}, u32[]{:S(2)}) copy-start(bf16[4096,256]{1,0:T(8,128)(2,1)} %basis_ref.1) | copy-start | bytes 6291460
  7.7 0.9 %copy-start.1 = (f32[256,256]{1,0:T(8,128)S(1)}, f32[256,256]{1,0:T(8,128)}, u32[]{:S(2)}) copy-start(f32[256,256]{1,0:T(8,128)} %prior_ref.1) | copy-start | bytes 786436
  8.7 0.9 %copy-start.2 = (f32[256,256]{1,0:T(8,128)S(1)}, f32[256,256]{1,0:T(8,128)}, u32[]{:S(2)}) copy-start(f32[256,256]{1,0:T(8,128)} %transition_ref.1) | copy-start | bytes 786436
  14.5 2.0 %collective-permute-start.2 = (f32[2,272,256]{2,1,0:T(8,128)S(1)}, f32[2,272,256]{2,1,0:T(8,128)S(1)}, u32[]{:S(2)}, u32[]{:S(2)}) collective-permute-start(f32[2,272,256]{2,1,0:T(8,128)S(1)} %get-tuple-element.26.own_ref.refs_0_), channel_id=1, source_target_pairs={{0,1},{1,0},{2,3},{3,2},{4,5},{5,4},{6,7},{7,6},{8,9},{9,8},{10,11... | collective-permute-start | bytes 1671176 | tf_op jit(solution)/shard_map/ppermute | solution.py:423
  14.6 7.3 %collective-permute-start.3 = (bf16[272,256]{1,0:T(8,128)(2,1)S(1)}, bf16[272,256]{1,0:T(8,128)(2,1)S(1)}, u32[]{:S(2)}, u32[]{:S(2)}) collective-permute-start(bf16[272,256]{1,0:T(8,128)(2,1)S(1)} %get-tuple-element.27), channel_id=1, source_target_pairs={{0,4},{4,0},{8,12},{12,8},{16,20},{20,16},{24,28},{28,24},{1,5},{5... | collective-permute-start | bytes 417800 | tf_op jit(solution)/shard_map/ppermute | solution.py:424
  16.8 5.7 %collective-permute-start.5 = (bf16[144,256]{1,0:T(8,128)(2,1)S(1)}, bf16[144,256]{1,0:T(8,128)(2,1)S(1)}, u32[]{:S(2)}, u32[]{:S(2)}) collective-permute-start(bf16[144,256]{1,0:T(8,128)(2,1)S(1)} %get-tuple-element.28), channel_id=1, source_target_pairs={{0,12},{4,8},{8,4},{12,0},{16,28},{20,24},{24,20},{28,16},{1,13},{... | collective-permute-start | bytes 221192 | tf_op jit(solution)/shard_map/ppermute | solution.py:430
  19.4 4.4 %collective-permute-start.4 = (bf16[144,256]{1,0:T(8,128)(2,1)S(1)}, bf16[144,256]{1,0:T(8,128)(2,1)S(1)}, u32[]{:S(2)}, u32[]{:S(2)}) collective-permute-start(bf16[144,256]{1,0:T(8,128)(2,1)S(1)} %get-tuple-element.28), channel_id=1, source_target_pairs={{0,8},{4,12},{8,0},{12,4},{16,24},{20,28},{24,16},{28,20},{1,9},{5... | collective-permute-start | bytes 221192 | tf_op jit(solution)/shard_map/ppermute | solution.py:429
  23.8 1.6 %collective-permute-start.6 = (bf16[560,256]{1,0:T(8,128)(2,1)S(1)}, bf16[560,256]{1,0:T(8,128)(2,1)S(1)}, u32[]{:S(2)}, u32[]{:S(2)}) collective-permute-start(bf16[560,256]{1,0:T(8,128)(2,1)S(1)} %merge.1.merged_ref.refs_2_), channel_id=1, source_target_pairs={{0,1},{1,0},{2,3},{3,2},{4,5},{5,4},{6,7},{7,6},{8,9},{9,8},{10,11... | collective-permute-start | bytes 860168 | tf_op jit(solution)/shard_map/ppermute | solution.py:432
  23.9 6.1 %collective-permute-start.8 = (bf16[1,272,256]{2,1,0:T(8,128)(2,1)S(1)}, bf16[1,272,256]{2,1,0:T(8,128)(2,1)S(1)}, u32[]{:S(2)}, u32[]{:S(2)}) collective-permute-start(bf16[1,272,256]{2,1,0:T(8,128)(2,1)S(1)} %get-tuple-element.33), channel_id=1, source_target_pairs={{0,4},{4,0},{8,12},{12,8},{16,20},{20,16},{24,28},{28,24},{1,5},{5... | collective-permute-start | bytes 417800 | tf_op jit(solution)/shard_map/ppermute | solution.py:425
  26.1 4.6 %collective-permute-start.7 = (f32[8,256]{1,0:T(8,128)S(1)}, f32[8,256]{1,0:T(8,128)S(1)}, u32[]{:S(2)}, u32[]{:S(2)}) collective-permute-start(f32[8,256]{1,0:T(8,128)S(1)} %group_shift.1), channel_id=1, source_target_pairs={{0,16},{4,20},{8,24},{12,28},{16,0},{20,4},{24,8},{28,12},{1,17},{... | collective-permute-start | bytes 24584 | tf_op jit(solution)/shard_map/ppermute | solution.py:448
  30.8 1.4 %collective-permute-start.9 = (bf16[1,272,256]{2,1,0:T(8,128)(2,1)S(1)}, bf16[1,272,256]{2,1,0:T(8,128)(2,1)S(1)}, u32[]{:S(2)}, u32[]{:S(2)}) collective-permute-start(bf16[1,272,256]{2,1,0:T(8,128)(2,1)S(1)} %hold.1.firsts_ref), channel_id=1, source_target_pairs={{0,1},{1,0},{2,3},{3,2},{4,5},{5,4},{6,7},{7,6},{8,9},{9,8},{10,11... | collective-permute-start | bytes 417800 | tf_op jit(solution)/shard_map/ppermute | solution.py:467
  32.4 5.5 %collective-permute-start.12 = (f32[8,256]{1,0:T(8,128)S(1)}, f32[8,256]{1,0:T(8,128)S(1)}, u32[]{:S(2)}, u32[]{:S(2)}) collective-permute-start(f32[8,256]{1,0:T(8,128)S(1)} %rest_of_means.1.refs_0_), channel_id=1, source_target_pairs={{0,24},{4,28},{8,16},{12,20},{16,8},{20,12},{24,0},{28,4},{1,25},{... | collective-permute-start | bytes 24584 | tf_op jit(solution)/shard_map/ppermute | solution.py:475
  36.0 4.5 %collective-permute-start.11 = (f32[8,256]{1,0:T(8,128)S(1)}, f32[8,256]{1,0:T(8,128)S(1)}, u32[]{:S(2)}, u32[]{:S(2)}) collective-permute-start(f32[8,256]{1,0:T(8,128)S(1)} %rest_of_means.1.refs_0_), channel_id=1, source_target_pairs={{0,16},{4,20},{8,24},{12,28},{16,0},{20,4},{24,8},{28,12},{1,17},{... | collective-permute-start | bytes 24584 | tf_op jit(solution)/shard_map/ppermute | solution.py:475
  36.0 4.5 %collective-permute-start.10 = (f32[8,256]{1,0:T(8,128)S(1)}, f32[8,256]{1,0:T(8,128)S(1)}, u32[]{:S(2)}, u32[]{:S(2)}) collective-permute-start(f32[8,256]{1,0:T(8,128)S(1)} %rest_of_means.1.refs_0_), channel_id=1, source_target_pairs={{0,8},{4,12},{8,0},{12,4},{16,24},{20,28},{24,16},{28,20},{1,9},{5... | collective-permute-start | bytes 24584 | tf_op jit(solution)/shard_map/ppermute | solution.py:475

commit v4 on v3

--- a/solution.py
+++ b/solution.py
@@ -122,11 +122,30 @@
             )
 
 
-def prepare(prior_ref, transition_ref, basis_ref, prior_out_ref, turned_ref, basis_out_ref):
+def prepare(
+    prior_hbm,
+    transition_hbm,
+    basis_hbm,
+    prior_out_ref,
+    turned_ref,
+    basis_out_ref,
+    transition_ref,
+    basis_ref,
+    sems,
+):
+    copies = [
+        pltpu.make_async_copy(prior_hbm, prior_out_ref, sems.at[0]),
+        pltpu.make_async_copy(transition_hbm, transition_ref, sems.at[1]),
+        pltpu.make_async_copy(basis_hbm, basis_ref, sems.at[2]),
+    ]
+    for copy in copies:
+        copy.start()
+    copies[0].wait()
+    copies[1].wait()
+    prior = prior_out_ref[...]
+    turned_ref[...] = dot_wide(transition_ref[...].T, prior)
+    copies[2].wait()
     basis_out_ref[...] = basis_ref[...].T
-    prior = prior_ref[...]
-    prior_out_ref[...] = prior
-    turned_ref[...] = dot_wide(transition_ref[...].T, prior)
 
 
 def add_and_round(keep_ref, received_ref, sum_ref, send_ref):
@@ -152,7 +171,16 @@
     return sum_ref[pair] + jnp.concatenate([received[:states], tail], axis=0)
 
 
-def hour_maps(sum_ref, received_ref, prior_ref, turned_ref, out_ref, last_ref, firsts_ref):
+def hour_maps(
+    sum_ref,
+    received_ref,
+    prior_ref,
+    turned_ref,
+    last_ref,
+    firsts_ref,
+    rounded_last_ref,
+    rounded_firsts_ref,
+):
     states = prior_ref.shape[0]
     prior = prior_ref[...]
     turned = turned_ref[...]
@@ -188,10 +216,11 @@
         maps.append(v + dot(v.astype(BF16), product[:states].astype(BF16)))
     for position in range(len(maps)):
         joined = maps[0] if position == 0 else append(joined, maps[position])
-        out_ref[position] = joined
         if position < len(maps) - 1:
-            firsts_ref[position] = rounded(joined)
-    last_ref[...] = rounded(joined)
+            firsts_ref[position] = joined
+            rounded_firsts_ref[position] = rounded(joined)
+    last_ref[...] = joined
+    rounded_last_ref[...] = rounded(joined)
 
 
 def rounded(affine):
@@ -213,30 +242,24 @@
     return early, late
 
 
-def block_map(own_ref, received_ref, out_ref, part_ref):
-    half, rows, states = own_ref.shape
-    early, late = in_order(own_ref, received_ref)
-    out_ref[...] = rounded(append(early[-1], late[-1]))
-    height = part_ref.shape[0]
-    first = own_half(2 * half) == 0
-    part_ref[...] = jnp.where(first, out_ref[:height, :], out_ref[rows - height :, :])
-
-
-def merge(last_ref, near_ref, far_ref, out_ref):
-    out_ref[...] = jnp.concatenate([last_ref[...], near_ref[...], far_ref[...]], axis=0)
-
-
-def group_blocks(merged_ref, other_ref, *out_refs):
-    first = lax.rem(lax.axis_index("site"), 2) == 0
-    rows = out_refs[0].shape[0]
-    height = (merged_ref.shape[0] - rows) // 2
-    own, other = merged_ref[:rows, :], other_ref[:rows, :]
-    out_refs[0][...] = follow(jnp.where(first, own, other), jnp.where(first, other, own))
-    for place in range(2):
-        start = rows + place * height
-        part, other = merged_ref[start : start + height, :], other_ref[start : start + height, :]
-        low = jnp.where(first, other, part)[2 * height - rows :]
-        out_refs[1 + place][...] = jnp.concatenate([jnp.where(first, part, other), low], axis=0)
+def block_map(own_ref, received_ref, out_ref):
+    (early,), (late,) = in_order([own_ref[...]], [received_ref[...]])
+    out_ref[...] = rounded(append(early, late))
+
+
+def merge(last_ref, far_ref, out_ref):
+    out_ref[0] = last_ref[...]
+    out_ref[1] = far_ref[...]
+
+
+def group_blocks(own_ref, merged_ref, other_ref, *out_refs):
+    shift_ref, out_refs = out_refs[-1], out_refs[:-1]
+    (early,), (late,) = in_order([merged_ref[0]], [other_ref[0]])
+    out_refs[0][...] = follow(early, late)
+    (near,), (far,) = in_order([merged_ref[1]], [other_ref[1]])
+    out_refs[1][...] = near
+    out_refs[2][...] = far
+    group_shift(own_ref, *out_refs, shift_ref)
 
 
 def shift_of(block):
@@ -244,11 +267,15 @@
     return jnp.sum(block[states:].astype(F32), axis=0, keepdims=True)
 
 
+def choose(values, slot):
+    value = values[0]
+    for i in range(1, len(values)):
+        value = jnp.where(slot == i, values[i], value)
+    return value
+
+
 def pick(refs, slot):
-    value = refs[0][...]
-    for i in range(1, len(refs)):
-        value = jnp.where(slot == i, refs[i][...], value)
-    return value
+    return choose([ref[...] for ref in refs], slot)
 
 
 def apply(block, mean):
@@ -296,9 +323,10 @@
 
 def pair_means(distances, *refs):
     out_ref = refs[-1]
-    own_ref, other_ref, last_ref, other_last_ref = refs[:4]
-    levels, gathered = refs[4 : 4 + len(distances)], refs[4 + len(distances) : -1]
-    half, rows, states = own_ref.shape
+    own_last_ref, own_other_ref, own_firsts_ref, other_firsts_ref, merged_ref, other_merged_ref = refs[:6]
+    levels, gathered = refs[6 : 6 + len(distances)], refs[6 + len(distances) : -1]
+    rows, states = own_last_ref.shape
+    half = own_firsts_ref.shape[0] + 1
     mean = jnp.zeros((1, states), F32)
     for level in reversed(range(len(distances))):
         if level == len(distances) - 1:
@@ -313,13 +341,17 @@
     between = apply(pick(gathered, place & 1), mean)
     own_start = jnp.where(odd, between, mean)
     own = []
-    for maps in in_order(own_ref, other_ref):
+    sides = [
+        [firsts[i] for i in range(half - 1)] + [last[...]]
+        for firsts, last in ((own_firsts_ref, own_last_ref), (other_firsts_ref, own_other_ref))
+    ]
+    for maps in in_order(*sides):
         start = own_start if not own else own[-1]
         for each in maps:
             own.append(row_times(start, *split(each[:states])) + each[states : states + 1])
     state = jnp.where(odd, mean, own[-1])
     partner = []
-    for maps in in_order([last_ref[:rows, :]], [other_last_ref[:rows, :]]):
+    for maps in in_order([merged_ref[0]], [other_merged_ref[0]]):
         partner += [state] * (half - 1)
         state = apply(maps[0], state)
         partner.append(state)
@@ -353,8 +385,11 @@
     means_refs, basis_ref, out_hbm, held_ref, sems = refs[:-4], *refs[-4:]
     if len(means_refs) > 1:
         place = lax.axis_index("tm") // 2
-        means = [pick(means_refs, place ^ i) for i in range(len(means_refs))]
-        means = jnp.concatenate(means, axis=0).astype(BF16)
+        own, near, far, other_far = [ref[...] for ref in means_refs]
+        (third,), (fourth,) = in_order([far], [other_far])
+        by_distance = [own, near, third, fourth]
+        means = jnp.concatenate([choose(by_distance, place ^ i) for i in range(4)], axis=0)
+        means = means.astype(BF16)
     else:
         means = means_refs[0][...]
     width = held_ref.shape[2]
@@ -367,6 +402,13 @@
         copies.append(copy)
     for copy in copies:
         copy.wait()
+
+
+def core_swaps(blocks, hours, first, second):
+    distances = [first, second] * (hours // 2)
+    return [
+        (t * hours + d, (t ^ distances[d]) * hours + d) for t in range(blocks) for d in range(hours)
+    ]
 
 
 def swaps(size, distance):
@@ -386,6 +428,12 @@
         (square, square, sds(site_basis.shape[::-1], BF16)),
         (prior_precision, transition, site_basis),
         "prepare",
+        [
+            pltpu.VMEM(transition.shape, F32),
+            pltpu.VMEM(site_basis.shape, BF16),
+            pltpu.SemaphoreType.DMA((3,)),
+        ],
+        in_hbm=True,
     )
     packed = sds((pairs, states + TAIL, states), F32)
     keep, send = call(
@@ -412,28 +460,29 @@
             keep = call(add_received, packed, (total, received), "add_received")
             received = jnp.zeros_like(keep)
     rows = states + 16
-    block, height = sds((rows, states), BF16), (rows // 2 + 15) // 16 * 16
+    block = sds((rows, states), BF16)
     firsts = sds((half - 1, rows, states), BF16)
-    maps, last, first_maps = call(
+    own_last, own_firsts, last, first_maps = call(
         hour_maps,
-        (sds((half, rows, states), F32), block, firsts),
+        (sds((rows, states), F32), sds((half - 1, rows, states), F32), block, firsts),
         (total, received, prior, turned),
         "hour_maps",
     )
-    other = lax.ppermute(maps, "site", swaps(hours, 1))
+    other_last = lax.ppermute(own_last, "site", swaps(hours, 1))
     last = lax.ppermute(last, "tm", swaps(blocks, 1))
     first_maps = lax.ppermute(first_maps, "tm", swaps(blocks, 1))
-    own, part = call(
-        block_map, (block, sds((height, states), BF16)), (maps, other), "block_map"
-    )
-    near = lax.ppermute(part, "tm", swaps(blocks, 2))
-    far = lax.ppermute(part, "tm", swaps(blocks, 3))
-    merged = call(merge, sds((rows + 2 * height, states), BF16), (last, near, far), "merge")
+    own = call(block_map, block, (own_last, other_last), "block_map")
+    far = lax.ppermute(own, ("tm", "site"), core_swaps(blocks, hours, 2, 3))
+    merged = call(merge, sds((2, rows, states), BF16), (last, far), "merge")
     other_merged = lax.ppermute(merged, "site", swaps(hours, 1))
     radix = 4
-    gathered = (own,) + tuple(call(
-        group_blocks, (block,) * 3, (merged, other_merged), "group_blocks"
-    ))
+    *gathered, shift = call(
+        group_blocks,
+        (block,) * 3 + (sds((8, states), F32),),
+        (own, merged, other_merged),
+        "group_blocks",
+    )
+    gathered = (own, *gathered)
     distances, levels = [], []
     distance = radix
     if 2 * distance < blocks:
@@ -443,8 +492,6 @@
             if levels:
                 shift = joined[states:].astype(F32).sum(axis=0, keepdims=True)
                 shift = jnp.broadcast_to(shift, (8, states))
-            else:
-                shift = call(group_shift, sds((8, states), F32), gathered, "group_shift")
             received = lax.ppermute(shift, "tm", swaps(blocks, distance))
         else:
             received = lax.ppermute(joined, "tm", swaps(blocks, distance))
@@ -457,10 +504,13 @@
         distances.append(distance)
         levels.append(received)
         distance *= 2
+    other_firsts = lax.ppermute(own_firsts, "site", swaps(hours, 1))
     means = call(
         functools.partial(pair_means, tuple(distances)),
         sds((2 * hours, states), F32),
-        [maps, other, merged, other_merged] + levels + list(gathered),
+        [own_last, other_last, own_firsts, other_firsts, merged, other_merged]
+        + levels
+        + list(gathered),
         "pair_means",
     )
     first_maps = call(hold, firsts, (first_maps, levels[-1]), "hold")
@@ -471,8 +521,11 @@
         (means, first_maps, other_firsts),
         "rest_of_means",
     )
-    if blocks <= 8:
-        means = [means] + [lax.ppermute(means, "tm", swaps(blocks, d)) for d in range(2, blocks, 2)]
+    if blocks == 2 * radix:
+        far = lax.ppermute(means, ("tm", "site"), core_swaps(blocks, hours, 4, 6))
+        near = lax.ppermute(means, "tm", swaps(blocks, 2))
+        other_far = lax.ppermute(far, "site", swaps(hours, 1))
+        means = [means, near, far, other_far]
     else:
         means = call(own_means, sds((blocks, hours, states), BF16), (means,), "own_means")
         means = [lax.all_to_all(means, "tm", 0, 0, tiled=True).reshape(blocks * hours, states)]

time: 41.9 us -> 39.2 us (0.936)
  local copies, waits for them, and re-layouts: 3.49 us -> 0 us
  Pallas kernels: 9.73 us -> 11.3 us
  starting transfers between devices: 16 us -> 15.5 us
    unnamed x6 -> x0, local copies, waits for them, and re-layouts: 3.49 us -> none
    ppermute x6, waiting for transfers between devices: 5.99 us -> 3.73 us  [the longest x1 1.73 us: body(): near = lax.ppermute(means, 'tm', swaps(blocks, 2))]
    pallas_call x11 -> x10, Pallas kernels: 8.59 us -> 10.2 us  [call(): pl.pallas_call(kernel, out_shape=outs, in_specs=[pl.BlockSpec(memory_spac...]
    ppermute x1, waiting for transfers between devices: 0.01 us -> 1.54 us  [body(): received = lax.ppermute(send, 'site', swaps(hours, distance))]
    ppermute x1, waiting for transfers between devices: 2.02 us -> 3.26 us  [body(): last = lax.ppermute(last, 'tm', swaps(blocks, 1))]
    ppermute x6, starting transfers between devices: 7.57 us -> 6.5 us  [the longest x1 2.66 us: body(): far = lax.ppermute(means, ('tm', 'site'), core_swaps(blocks, hours, 4, 6))]
    ppermute x1, waiting for transfers between devices: 0.98 us -> 0.11 us  [body(): other_merged = lax.ppermute(merged, 'site', swaps(hours, 1))]
  transfers between devices with their start and end apart: 13 -> 13, of which waited for: 11 -> 10; matrix products, arithmetic and copies ran while one was open for 0% -> 0% of each run, Pallas kernels for 7% -> 11%
where the time goes in v4:
time: 39.2 us; the launch traced here: 39 us
  starting transfers between devices  15.5 us (40%)
  waiting for transfers between devices  12 us (31%)
  Pallas kernels  11.3 us (29%)
    pallas_call x10, Pallas kernels, call(): pl.pallas_call(kernel, out_shape=outs, in_specs=[pl.BlockSpec(memory_spac...  10.2 us
    ppermute x1, waiting for transfers between devices, body(): last = lax.ppermute(last, 'tm', swaps(blocks, 1))  3.26 us
    ppermute x1, starting transfers between devices, body(): received = lax.ppermute(send, 'site', swaps(hours, distance))  2.92 us
    ppermute x1, starting transfers between devices, body(): received = lax.ppermute(shift, 'tm', swaps(blocks, distance))  2.66 us
    ppermute x1, starting transfers between devices, body(): far = lax.ppermute(means, ('tm', 'site'), core_swaps(blocks, hours, 4, 6))  2.66 us
    ppermute x1, starting transfers between devices, body(): last = lax.ppermute(last, 'tm', swaps(blocks, 1))  1.83 us
    ppermute x1, waiting for transfers between devices, body(): near = lax.ppermute(means, 'tm', swaps(blocks, 2))  1.73 us
    ppermute x1, starting transfers between devices, body(): far = lax.ppermute(own, ('tm', 'site'), core_swaps(blocks, hours, 2, 3))  1.64 us
  transfers between devices with their start and end apart: 13, of which 10 were waited for; matrix products, arithmetic and copies ran while one was open for 0% of the time, Pallas kernels for 11%

profile of v4, /device:TPU:0, one launch (start us, length us, event | category | flops | bytes accessed | tf_op | source)
XLA Modules:
  0.0 39.0 jit_solution(12700885570731255030)
XLA Ops:
  0.0 1.5 %local_grams.1 = (f32[1,264,256]{2,1,0:T(8,128)S(1)}, f32[1,264,256]{2,1,0:T(8,128)S(1)}) custom-call(bf16[512,256]{1,0:T(8,128)(2,1)} %rows_hbm.1, bf16[512]{0:T(512)(128)(2,1)} %values_hbm.1, s32[512]{0:T(512)} %codes_hbm.1), custom_call_target="tpu_custom_call" | custom-call | tf_op jit(solution)/shard_map/local_grams/pallas_call | solution.py:25
  1.5 0.5 %collective-permute-start = (f32[1,264,256]{2,1,0:T(8,128)S(1)}, f32[1,264,256]{2,1,0:T(8,128)S(1)}, u32[]{:S(2)}, u32[]{:S(2)}) collective-permute-start(f32[1,264,256]{2,1,0:T(8,128)S(1)} %get-tuple-element.21), channel_id=1, source_target_pairs={{0,1},{1,0},{2,3},{3,2},{4,5},{5,4},{6,7},{7,6},{8,9},{9,8},{10,11... | collective-permute-start | bytes 811016 | tf_op jit(solution)/shard_map/ppermute | solution.py:452
  2.0 1.2 %collective-permute-done.received_ref = f32[1,264,256]{2,1,0:T(8,128)S(1)} collective-permute-done((f32[1,264,256]{2,1,0:T(8,128)S(1)}, f32[1,264,256]{2,1,0:T(8,128)S(1)}, u32[]{:S(2)}, u32[]{:S(2)}) %collective-permute-start) | collective-permute-done | bytes 270368 | tf_op jit(solution)/shard_map/ppermute | solution.py:452
  3.2 2.9 %collective-permute-start.1 = (bf16[1,272,256]{2,1,0:T(8,128)(2,1)S(1)}, bf16[1,272,256]{2,1,0:T(8,128)(2,1)S(1)}, u32[]{:S(2)}, u32[]{:S(2)}) collective-permute-start(bf16[1,272,256]{2,1,0:T(8,128)(2,1)S(1)} %get-tuple-element.23), channel_id=1, source_target_pairs={{0,2},{1,3},{2,0},{3,1},{4,6},{5,7},{6,4},{7,5},{8,10},{9,11},{10,... | collective-permute-start | bytes 417800 | tf_op jit(solution)/shard_map/ppermute | solution.py:457
  6.1 2.4 %prepare.1 = (f32[256,256]{1,0:T(8,128)S(1)}, f32[256,256]{1,0:T(8,128)S(1)}, bf16[256,4096]{1,0:T(8,128)(2,1)S(1)}) custom-call(f32[256,256]{1,0:T(8,128)} %prior_hbm.1, f32[256,256]{1,0:T(8,128)} %transition_hbm.1, bf16[4096,256]{1,0:T(8,128)(2,1)} %basis_hbm.1), custom_call_target="tpu_custom_call" | custom-call | tf_op jit(solution)/shard_map/prepare/pallas_call | solution.py:25
  8.6 1.5 %collective-permute-done.1.received_ref = bf16[1,272,256]{2,1,0:T(8,128)(2,1)S(1)} collective-permute-done((bf16[1,272,256]{2,1,0:T(8,128)(2,1)S(1)}, bf16[1,272,256]{2,1,0:T(8,128)(2,1)S(1)}, u32[]{:S(2)}, u32[]{:S(2)}) %collective-permute-start.1) | collective-permute-done | bytes 139296 | tf_op jit(solution)/shard_map/ppermute | solution.py:457
  10.1 4.0 %hour_maps.1 = (f32[272,256]{1,0:T(8,128)S(1)}, f32[1,272,256]{2,1,0:T(8,128)S(1)}, bf16[272,256]{1,0:T(8,128)(2,1)S(1)}, bf16[1,272,256]{2,1,0:T(8,128)(2,1)S(1)}) custom-call(f32[1,264,256]{2,1,0:T(8,128)S(1)} %get-tuple-element.22.sum_ref, bf16[1,272,256]{2,1,0:T(8,128)(2,1)S(1)} %collective-permute-done.1.received_ref, ...), custom_call_target="tpu_custom_call" | custom-call | tf_op jit(solution)/shard_map/hour_maps/pallas_call | solution.py:25
  14.2 0.1 collective-permute-start.2
  14.2 1.8 %collective-permute-start.4 = (bf16[272,256]{1,0:T(8,128)(2,1)S(1)}, bf16[272,256]{1,0:T(8,128)(2,1)S(1)}, u32[]{:S(2)}, u32[]{:S(2)}) collective-permute-start(bf16[272,256]{1,0:T(8,128)(2,1)S(1)} %get-tuple-element.28), channel_id=1, source_target_pairs={{0,4},{4,0},{8,12},{12,8},{16,20},{20,16},{24,28},{28,24},{1,5},{5... | collective-permute-start | bytes 417800 | tf_op jit(solution)/shard_map/ppermute | solution.py:472
  16.1 0.0 collective-permute-done.2.received_ref.refs_1_
  16.1 0.3 block_map.1.own_ref.refs_7_
  16.4 1.6 %collective-permute-start.5 = (bf16[272,256]{1,0:T(8,128)(2,1)S(1)}, bf16[272,256]{1,0:T(8,128)(2,1)S(1)}, u32[]{:S(2)}, u32[]{:S(2)}) collective-permute-start(bf16[272,256]{1,0:T(8,128)(2,1)S(1)} %block_map.1.own_ref.refs_7_), channel_id=1, source_target_pairs={{0,8},{1,13},{2,10},{3,15},{4,12},{5,9},{6,14},{7,11},{8,0},{9,5},... | collective-permute-start | bytes 417800 | tf_op jit(solution)/shard_map/ppermute | solution.py:475
  18.1 3.3 %collective-permute-done.4.last_ref = bf16[272,256]{1,0:T(8,128)(2,1)S(1)} collective-permute-done((bf16[272,256]{1,0:T(8,128)(2,1)S(1)}, bf16[272,256]{1,0:T(8,128)(2,1)S(1)}, u32[]{:S(2)}, u32[]{:S(2)}) %collective-permute-start.4) | collective-permute-done | bytes 139296 | tf_op jit(solution)/shard_map/ppermute | solution.py:472
  21.3 1.6 %collective-permute-done.5.far_ref = bf16[272,256]{1,0:T(8,128)(2,1)S(1)} collective-permute-done((bf16[272,256]{1,0:T(8,128)(2,1)S(1)}, bf16[272,256]{1,0:T(8,128)(2,1)S(1)}, u32[]{:S(2)}, u32[]{:S(2)}) %collective-permute-start.5) | collective-permute-done | bytes 139296 | tf_op jit(solution)/shard_map/ppermute | solution.py:475
  23.0 0.1 collective-permute-start.6
  23.0 0.5 %collective-permute-start.3 = (f32[1,272,256]{2,1,0:T(8,128)S(1)}, f32[1,272,256]{2,1,0:T(8,128)S(1)}, u32[]{:S(2)}, u32[]{:S(2)}) collective-permute-start(f32[1,272,256]{2,1,0:T(8,128)S(1)} %get-tuple-element.27.refs_2_), channel_id=1, source_target_pairs={{0,1},{1,0},{2,3},{3,2},{4,5},{5,4},{6,7},{7,6},{8,9},{9,8},{10,11... | collective-permute-start | bytes 835592 | tf_op jit(solution)/shard_map/ppermute | solution.py:507
  23.5 0.9 %collective-permute-start.8 = (bf16[1,272,256]{2,1,0:T(8,128)(2,1)S(1)}, bf16[1,272,256]{2,1,0:T(8,128)(2,1)S(1)}, u32[]{:S(2)}, u32[]{:S(2)}) collective-permute-start(bf16[1,272,256]{2,1,0:T(8,128)(2,1)S(1)} %get-tuple-element.33), channel_id=1, source_target_pairs={{0,4},{4,0},{8,12},{12,8},{16,20},{20,16},{24,28},{28,24},{1,5},{5... | collective-permute-start | bytes 417800 | tf_op jit(solution)/shard_map/ppermute | solution.py:473
  24.5 0.1 collective-permute-done.6.other_ref.refs_5_
  24.6 0.6 %group_blocks.1 = (bf16[272,256]{1,0:T(8,128)(2,1)S(1)}, bf16[272,256]{1,0:T(8,128)(2,1)S(1)}, bf16[272,256]{1,0:T(8,128)(2,1)S(1)}, f32[8,256]{1,0:T(8,128)S(1)}) custom-call(bf16[272,256]{1,0:T(8,128)(2,1)S(1)} %block_map.1.own_ref.refs_7_, bf16[2,272,256]{2,1,0:T(8,128)(2,1)S(1)} %merge.1.merged_ref.refs_4_, ...), custom_call_target="tpu_custom_call" | custom-call | tf_op jit(solution)/shard_map/group_blocks/pallas_call | solution.py:25
  25.2 2.7 %collective-permute-start.7 = (f32[8,256]{1,0:T(8,128)S(1)}, f32[8,256]{1,0:T(8,128)S(1)}, u32[]{:S(2)}, u32[]{:S(2)}) collective-permute-start(f32[8,256]{1,0:T(8,128)S(1)} %get-tuple-element.29), channel_id=1, source_target_pairs={{0,16},{4,20},{8,24},{12,28},{16,0},{20,4},{24,8},{28,12},{1,17},{... | collective-permute-start | bytes 24584 | tf_op jit(solution)/shard_map/ppermute | solution.py:495
  27.9 1.3 %collective-permute-done.8.maps_ref = bf16[1,272,256]{2,1,0:T(8,128)(2,1)S(1)} collective-permute-done((bf16[1,272,256]{2,1,0:T(8,128)(2,1)S(1)}, bf16[1,272,256]{2,1,0:T(8,128)(2,1)S(1)}, u32[]{:S(2)}, u32[]{:S(2)}) %collective-permute-start.8) | collective-permute-done | bytes 139296 | tf_op jit(solution)/shard_map/ppermute | solution.py:473
  29.2 0.6 %collective-permute-done.7.refs_6_.received_ref = f32[8,256]{1,0:T(8,128)S(1)} collective-permute-done((f32[8,256]{1,0:T(8,128)S(1)}, f32[8,256]{1,0:T(8,128)S(1)}, u32[]{:S(2)}, u32[]{:S(2)}) %collective-permute-start.7) | collective-permute-done | bytes 8224 | tf_op jit(solution)/shard_map/ppermute | solution.py:495
  29.8 0.1 collective-permute-start.9
  29.9 0.0 collective-permute-done.3.refs_3_
  29.9 1.1 %pair_means.1.means_ref = f32[8,256]{1,0:T(8,128)S(1)} custom-call(f32[272,256]{1,0:T(8,128)S(1)} %get-tuple-element.26.own_ref.refs_0_, f32[272,256]{1,0:T(8,128)S(1)} %collective-permute-done.2.received_ref.refs_1_, f32[1,272,256]{2,1,0:T(8,128)S(1)} %get-tuple-element.27.refs_2_, f32[1,272,256]{2,1,0:T(8,128)S(1)} %collective-permute-done.3.refs_3_, ...), custom_call_target="tpu_custom_call" | custom-call | tf_op jit(solution)/shard_map/pair_means/pallas_call | solution.py:25
  31.0 0.3 collective-permute-done.9.other_ref
  31.3 0.2 rest_of_means.1.refs_0_
  31.4 2.7 %collective-permute-start.11 = (f32[8,256]{1,0:T(8,128)S(1)}, f32[8,256]{1,0:T(8,128)S(1)}, u32[]{:S(2)}, u32[]{:S(2)}) collective-permute-start(f32[8,256]{1,0:T(8,128)S(1)} %rest_of_means.1.refs_0_), channel_id=1, source_target_pairs={{0,16},{1,25},{2,18},{3,27},{4,20},{5,29},{6,22},{7,31},{8,24},{9,... | collective-permute-start | bytes 24584 | tf_op jit(solution)/shard_map/ppermute | solution.py:525
  34.1 1.6 %collective-permute-start.10 = (f32[8,256]{1,0:T(8,128)S(1)}, f32[8,256]{1,0:T(8,128)S(1)}, u32[]{:S(2)}, u32[]{:S(2)}) collective-permute-start(f32[8,256]{1,0:T(8,128)S(1)} %rest_of_means.1.refs_0_), channel_id=1, source_target_pairs={{0,8},{4,12},{8,0},{12,4},{16,24},{20,28},{24,16},{28,20},{1,9},{5... | collective-permute-start | bytes 24584 | tf_op jit(solution)/shard_map/ppermute | solution.py:526
  35.7 0.4 collective-permute-done.11.refs_2_
  36.1 0.1 collective-permute-start.12
  36.1 1.7 %collective-permute-done.10.refs_1_ = f32[8,256]{1,0:T(8,128)S(1)} collective-permute-done((f32[8,256]{1,0:T(8,128)S(1)}, f32[8,256]{1,0:T(8,128)S(1)}, u32[]{:S(2)}, u32[]{:S(2)}) %collective-permute-start.10) | collective-permute-done | bytes 8224 | tf_op jit(solution)/shard_map/ppermute | solution.py:526
  37.8 0.0 collective-permute-done.12.refs_3_
  37.8 1.1 %predict.1 = bf16[32,4096]{1,0:T(8,128)(2,1)} custom-call(f32[8,256]{1,0:T(8,128)S(1)} %rest_of_means.1.refs_0_, f32[8,256]{1,0:T(8,128)S(1)} %collective-permute-done.10.refs_1_, f32[8,256]{1,0:T(8,128)S(1)} %collective-permute-done.11.refs_2_, f32[8,256]{1,0:T(8,128)S(1)} %collective-permute-done.12.refs_3_, bf16[256,4096]{1,0:T(8,128)(2,1)S(1)} %get-tuple-element.34.refs_4_), custom_call_target="tpu_custom_call" | custom-call | tf_op jit(solution)/shard_map/predict/pallas_call | solution.py:533
  (3 shorter events, 0.1 us)
Async XLA Ops:
  1.5 1.7 %collective-permute-start = (f32[1,264,256]{2,1,0:T(8,128)S(1)}, f32[1,264,256]{2,1,0:T(8,128)S(1)}, u32[]{:S(2)}, u32[]{:S(2)}) collective-permute-start(f32[1,264,256]{2,1,0:T(8,128)S(1)} %get-tuple-element.21), channel_id=1, source_target_pairs={{0,1},{1,0},{2,3},{3,2},{4,5},{5,4},{6,7},{7,6},{8,9},{9,8},{10,11... | collective-permute-start | bytes 811016 | tf_op jit(solution)/shard_map/ppermute | solution.py:452
  3.2 6.9 %collective-permute-start.1 = (bf16[1,272,256]{2,1,0:T(8,128)(2,1)S(1)}, bf16[1,272,256]{2,1,0:T(8,128)(2,1)S(1)}, u32[]{:S(2)}, u32[]{:S(2)}) collective-permute-start(bf16[1,272,256]{2,1,0:T(8,128)(2,1)S(1)} %get-tuple-element.23), channel_id=1, source_target_pairs={{0,2},{1,3},{2,0},{3,1},{4,6},{5,7},{6,4},{7,5},{8,10},{9,11},{10,... | collective-permute-start | bytes 417800 | tf_op jit(solution)/shard_map/ppermute | solution.py:457
  14.2 1.9 %collective-permute-start.2 = (f32[272,256]{1,0:T(8,128)S(1)}, f32[272,256]{1,0:T(8,128)S(1)}, u32[]{:S(2)}, u32[]{:S(2)}) collective-permute-start(f32[272,256]{1,0:T(8,128)S(1)} %get-tuple-element.26.own_ref.refs_0_), channel_id=1, source_target_pairs={{0,1},{1,0},{2,3},{3,2},{4,5},{5,4},{6,7},{7,6},{8,9},{9,8},{10,11... | collective-permute-start | bytes 835592 | tf_op jit(solution)/shard_map/ppermute | solution.py:471
  14.2 7.1 %collective-permute-start.4 = (bf16[272,256]{1,0:T(8,128)(2,1)S(1)}, bf16[272,256]{1,0:T(8,128)(2,1)S(1)}, u32[]{:S(2)}, u32[]{:S(2)}) collective-permute-start(bf16[272,256]{1,0:T(8,128)(2,1)S(1)} %get-tuple-element.28), channel_id=1, source_target_pairs={{0,4},{4,0},{8,12},{12,8},{16,20},{20,16},{24,28},{28,24},{1,5},{5... | collective-permute-start | bytes 417800 | tf_op jit(solution)/shard_map/ppermute | solution.py:472
  16.4 6.5 %collective-permute-start.5 = (bf16[272,256]{1,0:T(8,128)(2,1)S(1)}, bf16[272,256]{1,0:T(8,128)(2,1)S(1)}, u32[]{:S(2)}, u32[]{:S(2)}) collective-permute-start(bf16[272,256]{1,0:T(8,128)(2,1)S(1)} %block_map.1.own_ref.refs_7_), channel_id=1, source_target_pairs={{0,8},{1,13},{2,10},{3,15},{4,12},{5,9},{6,14},{7,11},{8,0},{9,5},... | collective-permute-start | bytes 417800 | tf_op jit(solution)/shard_map/ppermute | solution.py:475
  23.0 1.6 %collective-permute-start.6 = (bf16[2,272,256]{2,1,0:T(8,128)(2,1)S(1)}, bf16[2,272,256]{2,1,0:T(8,128)(2,1)S(1)}, u32[]{:S(2)}, u32[]{:S(2)}) collective-permute-start(bf16[2,272,256]{2,1,0:T(8,128)(2,1)S(1)} %merge.1.merged_ref.refs_4_), channel_id=1, source_target_pairs={{0,1},{1,0},{2,3},{3,2},{4,5},{5,4},{6,7},{7,6},{8,9},{9,8},{10,11... | collective-permute-start | bytes 835592 | tf_op jit(solution)/shard_map/ppermute | solution.py:477
  23.0 6.9 %collective-permute-start.3 = (f32[1,272,256]{2,1,0:T(8,128)S(1)}, f32[1,272,256]{2,1,0:T(8,128)S(1)}, u32[]{:S(2)}, u32[]{:S(2)}) collective-permute-start(f32[1,272,256]{2,1,0:T(8,128)S(1)} %get-tuple-element.27.refs_2_), channel_id=1, source_target_pairs={{0,1},{1,0},{2,3},{3,2},{4,5},{5,4},{6,7},{7,6},{8,9},{9,8},{10,11... | collective-permute-start | bytes 835592 | tf_op jit(solution)/shard_map/ppermute | solution.py:507
  23.5 5.7 %collective-permute-start.8 = (bf16[1,272,256]{2,1,0:T(8,128)(2,1)S(1)}, bf16[1,272,256]{2,1,0:T(8,128)(2,1)S(1)}, u32[]{:S(2)}, u32[]{:S(2)}) collective-permute-start(bf16[1,272,256]{2,1,0:T(8,128)(2,1)S(1)} %get-tuple-element.33), channel_id=1, source_target_pairs={{0,4},{4,0},{8,12},{12,8},{16,20},{20,16},{24,28},{28,24},{1,5},{5... | collective-permute-start | bytes 417800 | tf_op jit(solution)/shard_map/ppermute | solution.py:473
  25.2 4.6 %collective-permute-start.7 = (f32[8,256]{1,0:T(8,128)S(1)}, f32[8,256]{1,0:T(8,128)S(1)}, u32[]{:S(2)}, u32[]{:S(2)}) collective-permute-start(f32[8,256]{1,0:T(8,128)S(1)} %get-tuple-element.29), channel_id=1, source_target_pairs={{0,16},{4,20},{8,24},{12,28},{16,0},{20,4},{24,8},{28,12},{1,17},{... | collective-permute-start | bytes 24584 | tf_op jit(solution)/shard_map/ppermute | solution.py:495
  29.8 1.4 %collective-permute-start.9 = (bf16[1,272,256]{2,1,0:T(8,128)(2,1)S(1)}, bf16[1,272,256]{2,1,0:T(8,128)(2,1)S(1)}, u32[]{:S(2)}, u32[]{:S(2)}) collective-permute-start(bf16[1,272,256]{2,1,0:T(8,128)(2,1)S(1)} %hold.1.firsts_ref), channel_id=1, source_target_pairs={{0,1},{1,0},{2,3},{3,2},{4,5},{5,4},{6,7},{7,6},{8,9},{9,8},{10,11... | collective-permute-start | bytes 417800 | tf_op jit(solution)/shard_map/ppermute | solution.py:517
  31.4 4.6 %collective-permute-start.11 = (f32[8,256]{1,0:T(8,128)S(1)}, f32[8,256]{1,0:T(8,128)S(1)}, u32[]{:S(2)}, u32[]{:S(2)}) collective-permute-start(f32[8,256]{1,0:T(8,128)S(1)} %rest_of_means.1.refs_0_), channel_id=1, source_target_pairs={{0,16},{1,25},{2,18},{3,27},{4,20},{5,29},{6,22},{7,31},{8,24},{9,... | collective-permute-start | bytes 24584 | tf_op jit(solution)/shard_map/ppermute | solution.py:525
  34.1 3.7 %collective-permute-start.10 = (f32[8,256]{1,0:T(8,128)S(1)}, f32[8,256]{1,0:T(8,128)S(1)}, u32[]{:S(2)}, u32[]{:S(2)}) collective-permute-start(f32[8,256]{1,0:T(8,128)S(1)} %rest_of_means.1.refs_0_), channel_id=1, source_target_pairs={{0,8},{4,12},{8,0},{12,4},{16,24},{20,28},{24,16},{28,20},{1,9},{5... | collective-permute-start | bytes 24584 | tf_op jit(solution)/shard_map/ppermute | solution.py:526
  36.1 1.8 %collective-permute-start.12 = (f32[8,256]{1,0:T(8,128)S(1)}, f32[8,256]{1,0:T(8,128)S(1)}, u32[]{:S(2)}, u32[]{:S(2)}) collective-permute-start(f32[8,256]{1,0:T(8,128)S(1)} %collective-permute-done.11.refs_2_), channel_id=1, source_target_pairs={{0,1},{1,0},{2,3},{3,2},{4,5},{5,4},{6,7},{7,6},{8,9},{9,8},{10,11... | collective-permute-start | bytes 24584 | tf_op jit(solution)/shard_map/ppermute | solution.py:527

commit v5 on v4

--- a/solution.py
+++ b/solution.py
@@ -110,16 +110,24 @@
     drives = dot(jnp.concatenate([weighted, pad], axis=0).astype(BF16), rows)
     row_id = lax.broadcasted_iota(jnp.int32, (states, states), 0)
     column_id = lax.broadcasted_iota(jnp.int32, (states, states), 1)
-    for out_ref, base in ((keep_ref, 0), (send_ref, half)):
+    for base in (0, half):
         for pair in range(half // 2):
             first = base + 2 * pair
             a = grams[first * states : (first + 1) * states]
             b = grams[(first + 1) * states : (first + 2) * states]
-            diagonal = jnp.sum(jnp.where(row_id == column_id, b, 0.0), axis=0, keepdims=True)
-            out_ref[pair, :states, :] = jnp.where(row_id <= column_id, a, b)
-            out_ref[pair, states:, :] = jnp.concatenate(
-                [diagonal, drives[first : first + 2], jnp.zeros((TAIL - 3, states), F32)], axis=0
+            diagonals = [
+                jnp.sum(jnp.where(row_id == column_id, gram, 0.0), axis=0, keepdims=True)
+                for gram in (a, b)
+            ]
+            square = jnp.where(row_id <= column_id, a, b)
+            tail = jnp.concatenate(
+                diagonals + [drives[first : first + 2], jnp.zeros((TAIL - 4, states), F32)], axis=0
             )
+            if base == 0:
+                keep_ref[pair, :states, :] = square
+                keep_ref[pair, states:, :] = tail
+            else:
+                store_rounded(send_ref, pair, square, tail)
 
 
 def prepare(
@@ -151,12 +159,16 @@
 def add_and_round(keep_ref, received_ref, sum_ref, send_ref):
     states = keep_ref.shape[2]
     for pair in range(keep_ref.shape[0]):
-        total = keep_ref[pair] + received_ref[pair]
+        total = sum_of(keep_ref, received_ref, pair, states)
         sum_ref[pair] = total
-        send_ref[pair, :states, :] = total[:states].astype(BF16)
-        tail = total[states:]
-        high = tail.astype(BF16).astype(F32)
-        send_ref[pair, states:, :] = jnp.concatenate([high, tail - high], axis=0).astype(BF16)
+        store_rounded(send_ref, pair, total[:states], total[states:])
+
+
+def store_rounded(out_ref, pair, square, tail):
+    states = square.shape[1]
+    out_ref[pair, :states, :] = square.astype(BF16)
+    high = tail.astype(BF16).astype(F32)
+    out_ref[pair, states:, :] = jnp.concatenate([high, tail - high], axis=0).astype(BF16)
 
 
 def add_received(sum_ref, received_ref, out_ref):
@@ -192,16 +204,14 @@
         square = total[:states]
         flipped = square.T
         upper, lower = row_id <= column_id, row_id > column_id
-        gram_a = jnp.where(upper, square, flipped)
-        gram_b = jnp.where(lower, square, flipped)
-        gram_b = jnp.where(row_id == column_id, total[states : states + 1], gram_b)
-        for gram, place in ((gram_a, states + 1), (gram_b, states + 2)):
+        grams = (jnp.where(upper, square, flipped), jnp.where(lower, square, flipped))
+        for place, gram in enumerate(grams):
+            diagonal, drive = [total[states + i : states + i + 1] for i in (place, place + 2)]
+            gram = jnp.where(row_id == column_id, diagonal, gram)
             precision = prior + gram
             bound = jnp.max(jnp.sum(jnp.abs(precision), axis=0, keepdims=True), axis=1, keepdims=True)
             scale = 1.0 / bound
-            offset = jnp.concatenate(
-                [total[place : place + 1], jnp.zeros((15, states), F32)], axis=0
-            )
+            offset = jnp.concatenate([drive, jnp.zeros((15, states), F32)], axis=0)
             running.append((precision * scale, turned * scale, offset * scale))
     stacked = [jnp.concatenate(parts, axis=0) for parts in running]
 
@@ -247,16 +257,11 @@
     out_ref[...] = rounded(append(early, late))
 
 
-def merge(last_ref, far_ref, out_ref):
-    out_ref[0] = last_ref[...]
-    out_ref[1] = far_ref[...]
-
-
-def group_blocks(own_ref, merged_ref, other_ref, *out_refs):
+def group_blocks(own_ref, last_ref, far_ref, other_last_ref, other_far_ref, *out_refs):
     shift_ref, out_refs = out_refs[-1], out_refs[:-1]
-    (early,), (late,) = in_order([merged_ref[0]], [other_ref[0]])
+    (early,), (late,) = in_order([last_ref[...]], [other_last_ref[...]])
     out_refs[0][...] = follow(early, late)
-    (near,), (far,) = in_order([merged_ref[1]], [other_ref[1]])
+    (near,), (far,) = in_order([far_ref[...]], [other_far_ref[...]])
     out_refs[1][...] = near
     out_refs[2][...] = far
     group_shift(own_ref, *out_refs, shift_ref)
@@ -323,7 +328,7 @@
 
 def pair_means(distances, *refs):
     out_ref = refs[-1]
-    own_last_ref, own_other_ref, own_firsts_ref, other_firsts_ref, merged_ref, other_merged_ref = refs[:6]
+    own_last_ref, own_other_ref, own_firsts_ref, other_firsts_ref, last_ref, other_last_ref = refs[:6]
     levels, gathered = refs[6 : 6 + len(distances)], refs[6 + len(distances) : -1]
     rows, states = own_last_ref.shape
     half = own_firsts_ref.shape[0] + 1
@@ -351,7 +356,7 @@
             own.append(row_times(start, *split(each[:states])) + each[states : states + 1])
     state = jnp.where(odd, mean, own[-1])
     partner = []
-    for maps in in_order([merged_ref[0]], [other_merged_ref[0]]):
+    for maps in in_order([last_ref[...]], [other_last_ref[...]]):
         partner += [state] * (half - 1)
         state = apply(maps[0], state)
         partner.append(state)
@@ -436,9 +441,10 @@
         in_hbm=True,
     )
     packed = sds((pairs, states + TAIL, states), F32)
+    rounded = sds((pairs, states + 2 * TAIL, states), BF16)
     keep, send = call(
         functools.partial(local_grams, hours),
-        (packed, packed),
+        (packed, rounded),
         (obs_rows, obs_values, obs_hours),
         "local_grams",
         [
@@ -450,7 +456,6 @@
         in_hbm=True,
     )
     received = lax.ppermute(send, "site", swaps(hours, 1))
-    rounded = sds((pairs, states + 2 * TAIL, states), BF16)
     distance = 2
     while distance < hours:
         total, send = call(add_and_round, (packed, rounded), (keep, received), "add_and_round")
@@ -458,7 +463,7 @@
         distance *= 2
         if distance < hours:
             keep = call(add_received, packed, (total, received), "add_received")
-            received = jnp.zeros_like(keep)
+            received = jnp.zeros_like(received)
     rows = states + 16
     block = sds((rows, states), BF16)
     firsts = sds((half - 1, rows, states), BF16)
@@ -473,13 +478,13 @@
     first_maps = lax.ppermute(first_maps, "tm", swaps(blocks, 1))
     own = call(block_map, block, (own_last, other_last), "block_map")
     far = lax.ppermute(own, ("tm", "site"), core_swaps(blocks, hours, 2, 3))
-    merged = call(merge, sds((2, rows, states), BF16), (last, far), "merge")
-    other_merged = lax.ppermute(merged, "site", swaps(hours, 1))
+    others_last = lax.ppermute(last, "site", swaps(hours, 1))
+    others_far = lax.ppermute(far, "site", swaps(hours, 1))
     radix = 4
     *gathered, shift = call(
         group_blocks,
         (block,) * 3 + (sds((8, states), F32),),
-        (own, merged, other_merged),
+        (own, last, far, others_last, others_far),
         "group_blocks",
     )
     gathered = (own, *gathered)
@@ -508,7 +513,7 @@
     means = call(
         functools.partial(pair_means, tuple(distances)),
         sds((2 * hours, states), F32),
-        [own_last, other_last, own_firsts, other_firsts, merged, other_merged]
+        [own_last, other_last, own_firsts, other_firsts, last, others_last]
         + levels
         + list(gathered),
         "pair_means",

time: 39.2 us -> 38.7 us (0.987)
    pallas_call x10 -> x9, Pallas kernels: 10.2 us -> 10.2 us  [call(): pl.pallas_call(kernel, out_shape=outs, in_specs=[pl.BlockSpec(memory_spac...]
  transfers between devices with their start and end apart: 13 -> 14, of which waited for: 10 -> 9; matrix products, arithmetic and copies ran while one was open for 0% -> 0% of each run, Pallas kernels for 11% -> 12%
where the time goes in v5:
time: 38.7 us; the launch traced here: 38.5 us
  starting transfers between devices  15.3 us (40%)
  waiting for transfers between devices  11.8 us (30%)
  Pallas kernels  11.3 us (29%)
    pallas_call x9, Pallas kernels, call(): pl.pallas_call(kernel, out_shape=outs, in_specs=[pl.BlockSpec(memory_spac...  10.2 us
    ppermute x1, waiting for transfers between devices, body(): last = lax.ppermute(last, 'tm', swaps(blocks, 1))  3.27 us
    ppermute x1, starting transfers between devices, body(): received = lax.ppermute(send, 'site', swaps(hours, distance))  2.91 us
    ppermute x1, starting transfers between devices, body(): received = lax.ppermute(shift, 'tm', swaps(blocks, distance))  2.66 us
    ppermute x1, starting transfers between devices, body(): far = lax.ppermute(means, ('tm', 'site'), core_swaps(blocks, hours, 4, 6))  2.66 us
    ppermute x1, starting transfers between devices, body(): last = lax.ppermute(last, 'tm', swaps(blocks, 1))  1.83 us
    ppermute x1, waiting for transfers between devices, body(): near = lax.ppermute(means, 'tm', swaps(blocks, 2))  1.73 us
    ppermute x1, starting transfers between devices, body(): far = lax.ppermute(own, ('tm', 'site'), core_swaps(blocks, hours, 2, 3))  1.64 us
  transfers between devices with their start and end apart: 14, of which 9 were waited for; matrix products, arithmetic and copies ran while one was open for 0% of the time, Pallas kernels for 12%

profile of v5, /device:TPU:0, one launch (start us, length us, event | category | flops | bytes accessed | tf_op | source)
XLA Modules:
  0.0 38.5 jit_solution(15643040091323275680)
XLA Ops:
  0.0 1.5 %local_grams.1 = (f32[1,264,256]{2,1,0:T(8,128)S(1)}, bf16[1,272,256]{2,1,0:T(8,128)(2,1)S(1)}) custom-call(bf16[512,256]{1,0:T(8,128)(2,1)} %rows_hbm.1, bf16[512]{0:T(512)(128)(2,1)} %values_hbm.1, s32[512]{0:T(512)} %codes_hbm.1), custom_call_target="tpu_custom_call" | custom-call | tf_op jit(solution)/shard_map/local_grams/pallas_call | solution.py:25
  1.5 0.5 %collective-permute-start = (bf16[1,272,256]{2,1,0:T(8,128)(2,1)S(1)}, bf16[1,272,256]{2,1,0:T(8,128)(2,1)S(1)}, u32[]{:S(2)}, u32[]{:S(2)}) collective-permute-start(bf16[1,272,256]{2,1,0:T(8,128)(2,1)S(1)} %get-tuple-element.21), channel_id=1, source_target_pairs={{0,1},{1,0},{2,3},{3,2},{4,5},{5,4},{6,7},{7,6},{8,9},{9,8},{10,11... | collective-permute-start | bytes 417800 | tf_op jit(solution)/shard_map/ppermute | solution.py:458
  2.0 1.0 %collective-permute-done.received_ref = bf16[1,272,256]{2,1,0:T(8,128)(2,1)S(1)} collective-permute-done((bf16[1,272,256]{2,1,0:T(8,128)(2,1)S(1)}, bf16[1,272,256]{2,1,0:T(8,128)(2,1)S(1)}, u32[]{:S(2)}, u32[]{:S(2)}) %collective-permute-start) | collective-permute-done | bytes 139296 | tf_op jit(solution)/shard_map/ppermute | solution.py:458
  3.0 2.9 %collective-permute-start.1 = (bf16[1,272,256]{2,1,0:T(8,128)(2,1)S(1)}, bf16[1,272,256]{2,1,0:T(8,128)(2,1)S(1)}, u32[]{:S(2)}, u32[]{:S(2)}) collective-permute-start(bf16[1,272,256]{2,1,0:T(8,128)(2,1)S(1)} %get-tuple-element.23), channel_id=1, source_target_pairs={{0,2},{1,3},{2,0},{3,1},{4,6},{5,7},{6,4},{7,5},{8,10},{9,11},{10,... | collective-permute-start | bytes 417800 | tf_op jit(solution)/shard_map/ppermute | solution.py:462
  6.0 2.4 %prepare.1 = (f32[256,256]{1,0:T(8,128)S(1)}, f32[256,256]{1,0:T(8,128)S(1)}, bf16[256,4096]{1,0:T(8,128)(2,1)S(1)}) custom-call(f32[256,256]{1,0:T(8,128)} %prior_hbm.1, f32[256,256]{1,0:T(8,128)} %transition_hbm.1, bf16[4096,256]{1,0:T(8,128)(2,1)} %basis_hbm.1), custom_call_target="tpu_custom_call" | custom-call | tf_op jit(solution)/shard_map/prepare/pallas_call | solution.py:25
  8.4 1.5 %collective-permute-done.1.received_ref = bf16[1,272,256]{2,1,0:T(8,128)(2,1)S(1)} collective-permute-done((bf16[1,272,256]{2,1,0:T(8,128)(2,1)S(1)}, bf16[1,272,256]{2,1,0:T(8,128)(2,1)S(1)}, u32[]{:S(2)}, u32[]{:S(2)}) %collective-permute-start.1) | collective-permute-done | bytes 139296 | tf_op jit(solution)/shard_map/ppermute | solution.py:462
  9.9 4.0 %hour_maps.1 = (f32[272,256]{1,0:T(8,128)S(1)}, f32[1,272,256]{2,1,0:T(8,128)S(1)}, bf16[272,256]{1,0:T(8,128)(2,1)S(1)}, bf16[1,272,256]{2,1,0:T(8,128)(2,1)S(1)}) custom-call(f32[1,264,256]{2,1,0:T(8,128)S(1)} %get-tuple-element.22.sum_ref, bf16[1,272,256]{2,1,0:T(8,128)(2,1)S(1)} %collective-permute-done.1.received_ref, ...), custom_call_target="tpu_custom_call" | custom-call | tf_op jit(solution)/shard_map/hour_maps/pallas_call | solution.py:25
  14.0 0.1 collective-permute-start.2
  14.1 1.8 %collective-permute-start.4 = (bf16[272,256]{1,0:T(8,128)(2,1)S(1)}, bf16[272,256]{1,0:T(8,128)(2,1)S(1)}, u32[]{:S(2)}, u32[]{:S(2)}) collective-permute-start(bf16[272,256]{1,0:T(8,128)(2,1)S(1)} %get-tuple-element.28), channel_id=1, source_target_pairs={{0,4},{4,0},{8,12},{12,8},{16,20},{20,16},{24,28},{28,24},{1,5},{5... | collective-permute-start | bytes 417800 | tf_op jit(solution)/shard_map/ppermute | solution.py:477
  15.9 0.0 collective-permute-done.2.received_ref.refs_1_
  15.9 0.3 block_map.1.own_ref.refs_7_
  16.2 1.6 %collective-permute-start.6 = (bf16[272,256]{1,0:T(8,128)(2,1)S(1)}, bf16[272,256]{1,0:T(8,128)(2,1)S(1)}, u32[]{:S(2)}, u32[]{:S(2)}) collective-permute-start(bf16[272,256]{1,0:T(8,128)(2,1)S(1)} %block_map.1.own_ref.refs_7_), channel_id=1, source_target_pairs={{0,8},{1,13},{2,10},{3,15},{4,12},{5,9},{6,14},{7,11},{8,0},{9,5},... | collective-permute-start | bytes 417800 | tf_op jit(solution)/shard_map/ppermute | solution.py:480
  17.9 3.3 %collective-permute-done.4.last_ref.refs_4_ = bf16[272,256]{1,0:T(8,128)(2,1)S(1)} collective-permute-done((bf16[272,256]{1,0:T(8,128)(2,1)S(1)}, bf16[272,256]{1,0:T(8,128)(2,1)S(1)}, u32[]{:S(2)}, u32[]{:S(2)}) %collective-permute-start.4) | collective-permute-done | bytes 139296 | tf_op jit(solution)/shard_map/ppermute | solution.py:477
  21.2 0.0 collective-permute-start.5
  21.2 1.6 %collective-permute-done.6.far_ref = bf16[272,256]{1,0:T(8,128)(2,1)S(1)} collective-permute-done((bf16[272,256]{1,0:T(8,128)(2,1)S(1)}, bf16[272,256]{1,0:T(8,128)(2,1)S(1)}, u32[]{:S(2)}, u32[]{:S(2)}) %collective-permute-start.6) | collective-permute-done | bytes 139296 | tf_op jit(solution)/shard_map/ppermute | solution.py:480
  22.8 0.0 collective-permute-start.7
  22.8 0.5 %collective-permute-start.3 = (f32[1,272,256]{2,1,0:T(8,128)S(1)}, f32[1,272,256]{2,1,0:T(8,128)S(1)}, u32[]{:S(2)}, u32[]{:S(2)}) collective-permute-start(f32[1,272,256]{2,1,0:T(8,128)S(1)} %get-tuple-element.27.refs_2_), channel_id=1, source_target_pairs={{0,1},{1,0},{2,3},{3,2},{4,5},{5,4},{6,7},{7,6},{8,9},{9,8},{10,11... | collective-permute-start | bytes 835592 | tf_op jit(solution)/shard_map/ppermute | solution.py:512
  23.3 0.9 %collective-permute-start.9 = (bf16[1,272,256]{2,1,0:T(8,128)(2,1)S(1)}, bf16[1,272,256]{2,1,0:T(8,128)(2,1)S(1)}, u32[]{:S(2)}, u32[]{:S(2)}) collective-permute-start(bf16[1,272,256]{2,1,0:T(8,128)(2,1)S(1)} %get-tuple-element.33), channel_id=1, source_target_pairs={{0,4},{4,0},{8,12},{12,8},{16,20},{20,16},{24,28},{28,24},{1,5},{5... | collective-permute-start | bytes 417800 | tf_op jit(solution)/shard_map/ppermute | solution.py:478
  24.1 0.0 collective-permute-done.5.other_last_ref.refs_5_
  24.1 0.0 collective-permute-done.7.other_far_ref
  24.1 0.6 %group_blocks.1 = (bf16[272,256]{1,0:T(8,128)(2,1)S(1)}, bf16[272,256]{1,0:T(8,128)(2,1)S(1)}, bf16[272,256]{1,0:T(8,128)(2,1)S(1)}, f32[8,256]{1,0:T(8,128)S(1)}) custom-call(bf16[272,256]{1,0:T(8,128)(2,1)S(1)} %block_map.1.own_ref.refs_7_, bf16[272,256]{1,0:T(8,128)(2,1)S(1)} %collective-permute-done.4.last_ref.refs_4_, ...), custom_call_target="tpu_custom_call" | custom-call | tf_op jit(solution)/shard_map/group_blocks/pallas_call | solution.py:25
  24.8 2.7 %collective-permute-start.8 = (f32[8,256]{1,0:T(8,128)S(1)}, f32[8,256]{1,0:T(8,128)S(1)}, u32[]{:S(2)}, u32[]{:S(2)}) collective-permute-start(f32[8,256]{1,0:T(8,128)S(1)} %get-tuple-element.29), channel_id=1, source_target_pairs={{0,16},{4,20},{8,24},{12,28},{16,0},{20,4},{24,8},{28,12},{1,17},{... | collective-permute-start | bytes 24584 | tf_op jit(solution)/shard_map/ppermute | solution.py:500
  27.4 1.4 %collective-permute-done.9.maps_ref = bf16[1,272,256]{2,1,0:T(8,128)(2,1)S(1)} collective-permute-done((bf16[1,272,256]{2,1,0:T(8,128)(2,1)S(1)}, bf16[1,272,256]{2,1,0:T(8,128)(2,1)S(1)}, u32[]{:S(2)}, u32[]{:S(2)}) %collective-permute-start.9) | collective-permute-done | bytes 139296 | tf_op jit(solution)/shard_map/ppermute | solution.py:478
  28.9 0.5 %collective-permute-done.8.refs_6_.received_ref = f32[8,256]{1,0:T(8,128)S(1)} collective-permute-done((f32[8,256]{1,0:T(8,128)S(1)}, f32[8,256]{1,0:T(8,128)S(1)}, u32[]{:S(2)}, u32[]{:S(2)}) %collective-permute-start.8) | collective-permute-done | bytes 8224 | tf_op jit(solution)/shard_map/ppermute | solution.py:500
  29.4 0.1 collective-permute-start.10
  29.5 0.0 collective-permute-done.3.refs_3_
  29.5 1.1 %pair_means.1.means_ref = f32[8,256]{1,0:T(8,128)S(1)} custom-call(f32[272,256]{1,0:T(8,128)S(1)} %get-tuple-element.26.own_ref.refs_0_, f32[272,256]{1,0:T(8,128)S(1)} %collective-permute-done.2.received_ref.refs_1_, f32[1,272,256]{2,1,0:T(8,128)S(1)} %get-tuple-element.27.refs_2_, f32[1,272,256]{2,1,0:T(8,128)S(1)} %collective-permute-done.3.refs_3_, ...), custom_call_target="tpu_custom_call" | custom-call | tf_op jit(solution)/shard_map/pair_means/pallas_call | solution.py:25
  30.6 0.3 collective-permute-done.10.other_ref
  30.8 0.2 rest_of_means.1.refs_0_
  31.0 2.7 %collective-permute-start.12 = (f32[8,256]{1,0:T(8,128)S(1)}, f32[8,256]{1,0:T(8,128)S(1)}, u32[]{:S(2)}, u32[]{:S(2)}) collective-permute-start(f32[8,256]{1,0:T(8,128)S(1)} %rest_of_means.1.refs_0_), channel_id=1, source_target_pairs={{0,16},{1,25},{2,18},{3,27},{4,20},{5,29},{6,22},{7,31},{8,24},{9,... | collective-permute-start | bytes 24584 | tf_op jit(solution)/shard_map/ppermute | solution.py:530
  33.7 1.6 %collective-permute-start.11 = (f32[8,256]{1,0:T(8,128)S(1)}, f32[8,256]{1,0:T(8,128)S(1)}, u32[]{:S(2)}, u32[]{:S(2)}) collective-permute-start(f32[8,256]{1,0:T(8,128)S(1)} %rest_of_means.1.refs_0_), channel_id=1, source_target_pairs={{0,8},{4,12},{8,0},{12,4},{16,24},{20,28},{24,16},{28,20},{1,9},{5... | collective-permute-start | bytes 24584 | tf_op jit(solution)/shard_map/ppermute | solution.py:531
  35.2 0.4 collective-permute-done.12.refs_2_
  35.6 0.0 collective-permute-start.13
  35.7 1.7 %collective-permute-done.11.refs_1_ = f32[8,256]{1,0:T(8,128)S(1)} collective-permute-done((f32[8,256]{1,0:T(8,128)S(1)}, f32[8,256]{1,0:T(8,128)S(1)}, u32[]{:S(2)}, u32[]{:S(2)}) %collective-permute-start.11) | collective-permute-done | bytes 8224 | tf_op jit(solution)/shard_map/ppermute | solution.py:531
  37.4 0.0 collective-permute-done.13.refs_3_
  37.4 1.1 %predict.1 = bf16[32,4096]{1,0:T(8,128)(2,1)} custom-call(f32[8,256]{1,0:T(8,128)S(1)} %rest_of_means.1.refs_0_, f32[8,256]{1,0:T(8,128)S(1)} %collective-permute-done.11.refs_1_, f32[8,256]{1,0:T(8,128)S(1)} %collective-permute-done.12.refs_2_, f32[8,256]{1,0:T(8,128)S(1)} %collective-permute-done.13.refs_3_, bf16[256,4096]{1,0:T(8,128)(2,1)S(1)} %get-tuple-element.34.refs_4_), custom_call_target="tpu_custom_call" | custom-call | tf_op jit(solution)/shard_map/predict/pallas_call | solution.py:538
  (2 shorter events, 0.0 us)
Async XLA Ops:
  1.5 1.5 %collective-permute-start = (bf16[1,272,256]{2,1,0:T(8,128)(2,1)S(1)}, bf16[1,272,256]{2,1,0:T(8,128)(2,1)S(1)}, u32[]{:S(2)}, u32[]{:S(2)}) collective-permute-start(bf16[1,272,256]{2,1,0:T(8,128)(2,1)S(1)} %get-tuple-element.21), channel_id=1, source_target_pairs={{0,1},{1,0},{2,3},{3,2},{4,5},{5,4},{6,7},{7,6},{8,9},{9,8},{10,11... | collective-permute-start | bytes 417800 | tf_op jit(solution)/shard_map/ppermute | solution.py:458
  3.0 6.9 %collective-permute-start.1 = (bf16[1,272,256]{2,1,0:T(8,128)(2,1)S(1)}, bf16[1,272,256]{2,1,0:T(8,128)(2,1)S(1)}, u32[]{:S(2)}, u32[]{:S(2)}) collective-permute-start(bf16[1,272,256]{2,1,0:T(8,128)(2,1)S(1)} %get-tuple-element.23), channel_id=1, source_target_pairs={{0,2},{1,3},{2,0},{3,1},{4,6},{5,7},{6,4},{7,5},{8,10},{9,11},{10,... | collective-permute-start | bytes 417800 | tf_op jit(solution)/shard_map/ppermute | solution.py:462
  14.0 1.9 %collective-permute-start.2 = (f32[272,256]{1,0:T(8,128)S(1)}, f32[272,256]{1,0:T(8,128)S(1)}, u32[]{:S(2)}, u32[]{:S(2)}) collective-permute-start(f32[272,256]{1,0:T(8,128)S(1)} %get-tuple-element.26.own_ref.refs_0_), channel_id=1, source_target_pairs={{0,1},{1,0},{2,3},{3,2},{4,5},{5,4},{6,7},{7,6},{8,9},{9,8},{10,11... | collective-permute-start | bytes 835592 | tf_op jit(solution)/shard_map/ppermute | solution.py:476
  14.1 7.1 %collective-permute-start.4 = (bf16[272,256]{1,0:T(8,128)(2,1)S(1)}, bf16[272,256]{1,0:T(8,128)(2,1)S(1)}, u32[]{:S(2)}, u32[]{:S(2)}) collective-permute-start(bf16[272,256]{1,0:T(8,128)(2,1)S(1)} %get-tuple-element.28), channel_id=1, source_target_pairs={{0,4},{4,0},{8,12},{12,8},{16,20},{20,16},{24,28},{28,24},{1,5},{5... | collective-permute-start | bytes 417800 | tf_op jit(solution)/shard_map/ppermute | solution.py:477
  16.2 6.5 %collective-permute-start.6 = (bf16[272,256]{1,0:T(8,128)(2,1)S(1)}, bf16[272,256]{1,0:T(8,128)(2,1)S(1)}, u32[]{:S(2)}, u32[]{:S(2)}) collective-permute-start(bf16[272,256]{1,0:T(8,128)(2,1)S(1)} %block_map.1.own_ref.refs_7_), channel_id=1, source_target_pairs={{0,8},{1,13},{2,10},{3,15},{4,12},{5,9},{6,14},{7,11},{8,0},{9,5},... | collective-permute-start | bytes 417800 | tf_op jit(solution)/shard_map/ppermute | solution.py:480
  21.2 3.0 %collective-permute-start.5 = (bf16[272,256]{1,0:T(8,128)(2,1)S(1)}, bf16[272,256]{1,0:T(8,128)(2,1)S(1)}, u32[]{:S(2)}, u32[]{:S(2)}) collective-permute-start(bf16[272,256]{1,0:T(8,128)(2,1)S(1)} %collective-permute-done.4.last_ref.refs_4_), channel_id=1, source_target_pairs={{0,1},{1,0},{2,3},{3,2},{4,5},{5,4},{6,7},{7,6},{8,9},{9,8},{10,11... | collective-permute-start | bytes 417800 | tf_op jit(solution)/shard_map/ppermute | solution.py:481
  22.8 1.4 %collective-permute-start.7 = (bf16[272,256]{1,0:T(8,128)(2,1)S(1)}, bf16[272,256]{1,0:T(8,128)(2,1)S(1)}, u32[]{:S(2)}, u32[]{:S(2)}) collective-permute-start(bf16[272,256]{1,0:T(8,128)(2,1)S(1)} %collective-permute-done.6.far_ref), channel_id=1, source_target_pairs={{0,1},{1,0},{2,3},{3,2},{4,5},{5,4},{6,7},{7,6},{8,9},{9,8},{10,11... | collective-permute-start | bytes 417800 | tf_op jit(solution)/shard_map/ppermute | solution.py:482
  22.8 6.7 %collective-permute-start.3 = (f32[1,272,256]{2,1,0:T(8,128)S(1)}, f32[1,272,256]{2,1,0:T(8,128)S(1)}, u32[]{:S(2)}, u32[]{:S(2)}) collective-permute-start(f32[1,272,256]{2,1,0:T(8,128)S(1)} %get-tuple-element.27.refs_2_), channel_id=1, source_target_pairs={{0,1},{1,0},{2,3},{3,2},{4,5},{5,4},{6,7},{7,6},{8,9},{9,8},{10,11... | collective-permute-start | bytes 835592 | tf_op jit(solution)/shard_map/ppermute | solution.py:512
  23.3 5.6 %collective-permute-start.9 = (bf16[1,272,256]{2,1,0:T(8,128)(2,1)S(1)}, bf16[1,272,256]{2,1,0:T(8,128)(2,1)S(1)}, u32[]{:S(2)}, u32[]{:S(2)}) collective-permute-start(bf16[1,272,256]{2,1,0:T(8,128)(2,1)S(1)} %get-tuple-element.33), channel_id=1, source_target_pairs={{0,4},{4,0},{8,12},{12,8},{16,20},{20,16},{24,28},{28,24},{1,5},{5... | collective-permute-start | bytes 417800 | tf_op jit(solution)/shard_map/ppermute | solution.py:478
  24.8 4.6 %collective-permute-start.8 = (f32[8,256]{1,0:T(8,128)S(1)}, f32[8,256]{1,0:T(8,128)S(1)}, u32[]{:S(2)}, u32[]{:S(2)}) collective-permute-start(f32[8,256]{1,0:T(8,128)S(1)} %get-tuple-element.29), channel_id=1, source_target_pairs={{0,16},{4,20},{8,24},{12,28},{16,0},{20,4},{24,8},{28,12},{1,17},{... | collective-permute-start | bytes 24584 | tf_op jit(solution)/shard_map/ppermute | solution.py:500
  29.4 1.4 %collective-permute-start.10 = (bf16[1,272,256]{2,1,0:T(8,128)(2,1)S(1)}, bf16[1,272,256]{2,1,0:T(8,128)(2,1)S(1)}, u32[]{:S(2)}, u32[]{:S(2)}) collective-permute-start(bf16[1,272,256]{2,1,0:T(8,128)(2,1)S(1)} %hold.1.firsts_ref), channel_id=1, source_target_pairs={{0,1},{1,0},{2,3},{3,2},{4,5},{5,4},{6,7},{7,6},{8,9},{9,8},{10,11... | collective-permute-start | bytes 417800 | tf_op jit(solution)/shard_map/ppermute | solution.py:522
  31.0 4.6 %collective-permute-start.12 = (f32[8,256]{1,0:T(8,128)S(1)}, f32[8,256]{1,0:T(8,128)S(1)}, u32[]{:S(2)}, u32[]{:S(2)}) collective-permute-start(f32[8,256]{1,0:T(8,128)S(1)} %rest_of_means.1.refs_0_), channel_id=1, source_target_pairs={{0,16},{1,25},{2,18},{3,27},{4,20},{5,29},{6,22},{7,31},{8,24},{9,... | collective-permute-start | bytes 24584 | tf_op jit(solution)/shard_map/ppermute | solution.py:530
  33.7 3.7 %collective-permute-start.11 = (f32[8,256]{1,0:T(8,128)S(1)}, f32[8,256]{1,0:T(8,128)S(1)}, u32[]{:S(2)}, u32[]{:S(2)}) collective-permute-start(f32[8,256]{1,0:T(8,128)S(1)} %rest_of_means.1.refs_0_), channel_id=1, source_target_pairs={{0,8},{4,12},{8,0},{12,4},{16,24},{20,28},{24,16},{28,20},{1,9},{5... | collective-permute-start | bytes 24584 | tf_op jit(solution)/shard_map/ppermute | solution.py:531
  35.6 1.8 %collective-permute-start.13 = (f32[8,256]{1,0:T(8,128)S(1)}, f32[8,256]{1,0:T(8,128)S(1)}, u32[]{:S(2)}, u32[]{:S(2)}) collective-permute-start(f32[8,256]{1,0:T(8,128)S(1)} %collective-permute-done.12.refs_2_), channel_id=1, source_target_pairs={{0,1},{1,0},{2,3},{3,2},{4,5},{5,4},{6,7},{7,6},{8,9},{9,8},{10,11... | collective-permute-start | bytes 24584 | tf_op jit(solution)/shard_map/ppermute | solution.py:532

commit v6 on v5

--- a/solution.py
+++ b/solution.py
@@ -183,6 +183,19 @@
     return sum_ref[pair] + jnp.concatenate([received[:states], tail], axis=0)
 
 
+def times_own(z):
+    states = z.shape[1]
+    high, low = split(z)
+    d_high, d_low = high[:states], low[:states]
+    mixed = dot(d_high, d_low)
+    square = dot(d_high, d_high) + (mixed + mixed.T)
+    rest = dot(
+        jnp.concatenate([high[states:], low[states:], high[states:]], axis=1),
+        jnp.concatenate([d_high, d_high, d_low], axis=0),
+    )
+    return jnp.concatenate([square, rest], axis=0)
+
+
 def hour_maps(
     sum_ref,
     received_ref,
@@ -216,7 +229,7 @@
     stacked = [jnp.concatenate(parts, axis=0) for parts in running]
 
     for _ in range(NS_ITERS - 2):
-        stacked = [2.0 * z - dot_wide(z, z[:states]) for z in stacked]
+        stacked = [2.0 * z - times_own(z) for z in stacked]
     maps = []
     for z in stacked:
         power = (jnp.where(row_id == column_id, 1.0, 0.0) - z[:states]).astype(BF16)

time: 38.7 us -> 38.1 us (0.984)
  Pallas kernels: 11.3 us -> 10.7 us
    pallas_call x9, Pallas kernels: 10.2 us -> 9.57 us  [call(): pl.pallas_call(kernel, out_shape=outs, in_specs=[pl.BlockSpec(memory_spac...]
where the time goes in v6:
time: 38.1 us; the launch traced here: 37.9 us
  starting transfers between devices  15.3 us (40%)
  waiting for transfers between devices  11.8 us (31%)
  Pallas kernels  10.7 us (28%)
    pallas_call x9, Pallas kernels, call(): pl.pallas_call(kernel, out_shape=outs, in_specs=[pl.BlockSpec(memory_spac...  9.57 us
    ppermute x1, waiting for transfers between devices, body(): last = lax.ppermute(last, 'tm', swaps(blocks, 1))  3.27 us
    ppermute x1, starting transfers between devices, body(): received = lax.ppermute(send, 'site', swaps(hours, distance))  2.91 us
    ppermute x1, starting transfers between devices, body(): received = lax.ppermute(shift, 'tm', swaps(blocks, distance))  2.66 us
    ppermute x1, starting transfers between devices, body(): far = lax.ppermute(means, ('tm', 'site'), core_swaps(blocks, hours, 4, 6))  2.66 us
    ppermute x1, starting transfers between devices, body(): last = lax.ppermute(last, 'tm', swaps(blocks, 1))  1.83 us
    ppermute x1, waiting for transfers between devices, body(): near = lax.ppermute(means, 'tm', swaps(blocks, 2))  1.73 us
    ppermute x1, starting transfers between devices, body(): far = lax.ppermute(own, ('tm', 'site'), core_swaps(blocks, hours, 2, 3))  1.64 us
  transfers between devices with their start and end apart: 14, of which 9 were waited for; matrix products, arithmetic and copies ran while one was open for 0% of the time, Pallas kernels for 12%

profile of v6, /device:TPU:0, one launch (start us, length us, event | category | flops | bytes accessed | tf_op | source)
XLA Modules:
  0.0 37.9 jit_solution(15028014831430360969)
XLA Ops:
  0.0 1.5 %local_grams.1 = (f32[1,264,256]{2,1,0:T(8,128)S(1)}, bf16[1,272,256]{2,1,0:T(8,128)(2,1)S(1)}) custom-call(bf16[512,256]{1,0:T(8,128)(2,1)} %rows_hbm.1, bf16[512]{0:T(512)(128)(2,1)} %values_hbm.1, s32[512]{0:T(512)} %codes_hbm.1), custom_call_target="tpu_custom_call" | custom-call | tf_op jit(solution)/shard_map/local_grams/pallas_call | solution.py:25
  1.5 0.5 %collective-permute-start = (bf16[1,272,256]{2,1,0:T(8,128)(2,1)S(1)}, bf16[1,272,256]{2,1,0:T(8,128)(2,1)S(1)}, u32[]{:S(2)}, u32[]{:S(2)}) collective-permute-start(bf16[1,272,256]{2,1,0:T(8,128)(2,1)S(1)} %get-tuple-element.21), channel_id=1, source_target_pairs={{0,1},{1,0},{2,3},{3,2},{4,5},{5,4},{6,7},{7,6},{8,9},{9,8},{10,11... | collective-permute-start | bytes 417800 | tf_op jit(solution)/shard_map/ppermute | solution.py:471
  2.0 1.0 %collective-permute-done.received_ref = bf16[1,272,256]{2,1,0:T(8,128)(2,1)S(1)} collective-permute-done((bf16[1,272,256]{2,1,0:T(8,128)(2,1)S(1)}, bf16[1,272,256]{2,1,0:T(8,128)(2,1)S(1)}, u32[]{:S(2)}, u32[]{:S(2)}) %collective-permute-start) | collective-permute-done | bytes 139296 | tf_op jit(solution)/shard_map/ppermute | solution.py:471
  3.0 2.9 %collective-permute-start.1 = (bf16[1,272,256]{2,1,0:T(8,128)(2,1)S(1)}, bf16[1,272,256]{2,1,0:T(8,128)(2,1)S(1)}, u32[]{:S(2)}, u32[]{:S(2)}) collective-permute-start(bf16[1,272,256]{2,1,0:T(8,128)(2,1)S(1)} %get-tuple-element.23), channel_id=1, source_target_pairs={{0,2},{1,3},{2,0},{3,1},{4,6},{5,7},{6,4},{7,5},{8,10},{9,11},{10,... | collective-permute-start | bytes 417800 | tf_op jit(solution)/shard_map/ppermute | solution.py:475
  6.0 2.4 %prepare.1 = (f32[256,256]{1,0:T(8,128)S(1)}, f32[256,256]{1,0:T(8,128)S(1)}, bf16[256,4096]{1,0:T(8,128)(2,1)S(1)}) custom-call(f32[256,256]{1,0:T(8,128)} %prior_hbm.1, f32[256,256]{1,0:T(8,128)} %transition_hbm.1, bf16[4096,256]{1,0:T(8,128)(2,1)} %basis_hbm.1), custom_call_target="tpu_custom_call" | custom-call | tf_op jit(solution)/shard_map/prepare/pallas_call | solution.py:25
  8.4 1.5 %collective-permute-done.1.received_ref = bf16[1,272,256]{2,1,0:T(8,128)(2,1)S(1)} collective-permute-done((bf16[1,272,256]{2,1,0:T(8,128)(2,1)S(1)}, bf16[1,272,256]{2,1,0:T(8,128)(2,1)S(1)}, u32[]{:S(2)}, u32[]{:S(2)}) %collective-permute-start.1) | collective-permute-done | bytes 139296 | tf_op jit(solution)/shard_map/ppermute | solution.py:475
  9.9 3.4 %hour_maps.1 = (f32[272,256]{1,0:T(8,128)S(1)}, f32[1,272,256]{2,1,0:T(8,128)S(1)}, bf16[272,256]{1,0:T(8,128)(2,1)S(1)}, bf16[1,272,256]{2,1,0:T(8,128)(2,1)S(1)}) custom-call(f32[1,264,256]{2,1,0:T(8,128)S(1)} %get-tuple-element.22.sum_ref, bf16[1,272,256]{2,1,0:T(8,128)(2,1)S(1)} %collective-permute-done.1.received_ref, ...), custom_call_target="tpu_custom_call" | custom-call | tf_op jit(solution)/shard_map/hour_maps/pallas_call | solution.py:25
  13.4 0.1 collective-permute-start.2
  13.5 1.8 %collective-permute-start.4 = (bf16[272,256]{1,0:T(8,128)(2,1)S(1)}, bf16[272,256]{1,0:T(8,128)(2,1)S(1)}, u32[]{:S(2)}, u32[]{:S(2)}) collective-permute-start(bf16[272,256]{1,0:T(8,128)(2,1)S(1)} %get-tuple-element.28), channel_id=1, source_target_pairs={{0,4},{4,0},{8,12},{12,8},{16,20},{20,16},{24,28},{28,24},{1,5},{5... | collective-permute-start | bytes 417800 | tf_op jit(solution)/shard_map/ppermute | solution.py:490
  15.3 0.0 collective-permute-done.2.received_ref.refs_1_
  15.3 0.3 block_map.1.own_ref.refs_7_
  15.6 1.6 %collective-permute-start.6 = (bf16[272,256]{1,0:T(8,128)(2,1)S(1)}, bf16[272,256]{1,0:T(8,128)(2,1)S(1)}, u32[]{:S(2)}, u32[]{:S(2)}) collective-permute-start(bf16[272,256]{1,0:T(8,128)(2,1)S(1)} %block_map.1.own_ref.refs_7_), channel_id=1, source_target_pairs={{0,8},{1,13},{2,10},{3,15},{4,12},{5,9},{6,14},{7,11},{8,0},{9,5},... | collective-permute-start | bytes 417800 | tf_op jit(solution)/shard_map/ppermute | solution.py:493
  17.3 3.3 %collective-permute-done.4.last_ref.refs_4_ = bf16[272,256]{1,0:T(8,128)(2,1)S(1)} collective-permute-done((bf16[272,256]{1,0:T(8,128)(2,1)S(1)}, bf16[272,256]{1,0:T(8,128)(2,1)S(1)}, u32[]{:S(2)}, u32[]{:S(2)}) %collective-permute-start.4) | collective-permute-done | bytes 139296 | tf_op jit(solution)/shard_map/ppermute | solution.py:490
  20.6 0.0 collective-permute-start.5
  20.6 1.6 %collective-permute-done.6.far_ref = bf16[272,256]{1,0:T(8,128)(2,1)S(1)} collective-permute-done((bf16[272,256]{1,0:T(8,128)(2,1)S(1)}, bf16[272,256]{1,0:T(8,128)(2,1)S(1)}, u32[]{:S(2)}, u32[]{:S(2)}) %collective-permute-start.6) | collective-permute-done | bytes 139296 | tf_op jit(solution)/shard_map/ppermute | solution.py:493
  22.2 0.0 collective-permute-start.7
  22.2 0.5 %collective-permute-start.3 = (f32[1,272,256]{2,1,0:T(8,128)S(1)}, f32[1,272,256]{2,1,0:T(8,128)S(1)}, u32[]{:S(2)}, u32[]{:S(2)}) collective-permute-start(f32[1,272,256]{2,1,0:T(8,128)S(1)} %get-tuple-element.27.refs_2_), channel_id=1, source_target_pairs={{0,1},{1,0},{2,3},{3,2},{4,5},{5,4},{6,7},{7,6},{8,9},{9,8},{10,11... | collective-permute-start | bytes 835592 | tf_op jit(solution)/shard_map/ppermute | solution.py:525
  22.7 0.9 %collective-permute-start.9 = (bf16[1,272,256]{2,1,0:T(8,128)(2,1)S(1)}, bf16[1,272,256]{2,1,0:T(8,128)(2,1)S(1)}, u32[]{:S(2)}, u32[]{:S(2)}) collective-permute-start(bf16[1,272,256]{2,1,0:T(8,128)(2,1)S(1)} %get-tuple-element.33), channel_id=1, source_target_pairs={{0,4},{4,0},{8,12},{12,8},{16,20},{20,16},{24,28},{28,24},{1,5},{5... | collective-permute-start | bytes 417800 | tf_op jit(solution)/shard_map/ppermute | solution.py:491
  23.5 0.0 collective-permute-done.5.other_last_ref.refs_5_
  23.5 0.0 collective-permute-done.7.other_far_ref
  23.6 0.6 %group_blocks.1 = (bf16[272,256]{1,0:T(8,128)(2,1)S(1)}, bf16[272,256]{1,0:T(8,128)(2,1)S(1)}, bf16[272,256]{1,0:T(8,128)(2,1)S(1)}, f32[8,256]{1,0:T(8,128)S(1)}) custom-call(bf16[272,256]{1,0:T(8,128)(2,1)S(1)} %block_map.1.own_ref.refs_7_, bf16[272,256]{1,0:T(8,128)(2,1)S(1)} %collective-permute-done.4.last_ref.refs_4_, ...), custom_call_target="tpu_custom_call" | custom-call | tf_op jit(solution)/shard_map/group_blocks/pallas_call | solution.py:25
  24.2 2.7 %collective-permute-start.8 = (f32[8,256]{1,0:T(8,128)S(1)}, f32[8,256]{1,0:T(8,128)S(1)}, u32[]{:S(2)}, u32[]{:S(2)}) collective-permute-start(f32[8,256]{1,0:T(8,128)S(1)} %get-tuple-element.29), channel_id=1, source_target_pairs={{0,16},{4,20},{8,24},{12,28},{16,0},{20,4},{24,8},{28,12},{1,17},{... | collective-permute-start | bytes 24584 | tf_op jit(solution)/shard_map/ppermute | solution.py:513
  26.8 1.4 %collective-permute-done.9.maps_ref = bf16[1,272,256]{2,1,0:T(8,128)(2,1)S(1)} collective-permute-done((bf16[1,272,256]{2,1,0:T(8,128)(2,1)S(1)}, bf16[1,272,256]{2,1,0:T(8,128)(2,1)S(1)}, u32[]{:S(2)}, u32[]{:S(2)}) %collective-permute-start.9) | collective-permute-done | bytes 139296 | tf_op jit(solution)/shard_map/ppermute | solution.py:491
  28.3 0.5 %collective-permute-done.8.refs_6_.received_ref = f32[8,256]{1,0:T(8,128)S(1)} collective-permute-done((f32[8,256]{1,0:T(8,128)S(1)}, f32[8,256]{1,0:T(8,128)S(1)}, u32[]{:S(2)}, u32[]{:S(2)}) %collective-permute-start.8) | collective-permute-done | bytes 8224 | tf_op jit(solution)/shard_map/ppermute | solution.py:513
  28.8 0.1 collective-permute-start.10
  28.9 0.0 collective-permute-done.3.refs_3_
  28.9 1.1 %pair_means.1.means_ref = f32[8,256]{1,0:T(8,128)S(1)} custom-call(f32[272,256]{1,0:T(8,128)S(1)} %get-tuple-element.26.own_ref.refs_0_, f32[272,256]{1,0:T(8,128)S(1)} %collective-permute-done.2.received_ref.refs_1_, f32[1,272,256]{2,1,0:T(8,128)S(1)} %get-tuple-element.27.refs_2_, f32[1,272,256]{2,1,0:T(8,128)S(1)} %collective-permute-done.3.refs_3_, ...), custom_call_target="tpu_custom_call" | custom-call | tf_op jit(solution)/shard_map/pair_means/pallas_call | solution.py:25
  30.0 0.3 collective-permute-done.10.other_ref
  30.2 0.2 rest_of_means.1.refs_0_
  30.4 2.7 %collective-permute-start.12 = (f32[8,256]{1,0:T(8,128)S(1)}, f32[8,256]{1,0:T(8,128)S(1)}, u32[]{:S(2)}, u32[]{:S(2)}) collective-permute-start(f32[8,256]{1,0:T(8,128)S(1)} %rest_of_means.1.refs_0_), channel_id=1, source_target_pairs={{0,16},{1,25},{2,18},{3,27},{4,20},{5,29},{6,22},{7,31},{8,24},{9,... | collective-permute-start | bytes 24584 | tf_op jit(solution)/shard_map/ppermute | solution.py:543
  33.1 1.6 %collective-permute-start.11 = (f32[8,256]{1,0:T(8,128)S(1)}, f32[8,256]{1,0:T(8,128)S(1)}, u32[]{:S(2)}, u32[]{:S(2)}) collective-permute-start(f32[8,256]{1,0:T(8,128)S(1)} %rest_of_means.1.refs_0_), channel_id=1, source_target_pairs={{0,8},{4,12},{8,0},{12,4},{16,24},{20,28},{24,16},{28,20},{1,9},{5... | collective-permute-start | bytes 24584 | tf_op jit(solution)/shard_map/ppermute | solution.py:544
  34.6 0.4 %collective-permute-done.12.refs_2_ = f32[8,256]{1,0:T(8,128)S(1)} collective-permute-done((f32[8,256]{1,0:T(8,128)S(1)}, f32[8,256]{1,0:T(8,128)S(1)}, u32[]{:S(2)}, u32[]{:S(2)}) %collective-permute-start.12) | collective-permute-done | bytes 8224 | tf_op jit(solution)/shard_map/ppermute | solution.py:543
  35.0 0.0 collective-permute-start.13
  35.1 1.7 %collective-permute-done.11.refs_1_ = f32[8,256]{1,0:T(8,128)S(1)} collective-permute-done((f32[8,256]{1,0:T(8,128)S(1)}, f32[8,256]{1,0:T(8,128)S(1)}, u32[]{:S(2)}, u32[]{:S(2)}) %collective-permute-start.11) | collective-permute-done | bytes 8224 | tf_op jit(solution)/shard_map/ppermute | solution.py:544
  36.8 0.0 collective-permute-done.13.refs_3_
  36.8 1.1 %predict.1 = bf16[32,4096]{1,0:T(8,128)(2,1)} custom-call(f32[8,256]{1,0:T(8,128)S(1)} %rest_of_means.1.refs_0_, f32[8,256]{1,0:T(8,128)S(1)} %collective-permute-done.11.refs_1_, f32[8,256]{1,0:T(8,128)S(1)} %collective-permute-done.12.refs_2_, f32[8,256]{1,0:T(8,128)S(1)} %collective-permute-done.13.refs_3_, bf16[256,4096]{1,0:T(8,128)(2,1)S(1)} %get-tuple-element.34.refs_4_), custom_call_target="tpu_custom_call" | custom-call | tf_op jit(solution)/shard_map/predict/pallas_call | solution.py:551
  (2 shorter events, 0.0 us)
Async XLA Ops:
  1.5 1.5 %collective-permute-start = (bf16[1,272,256]{2,1,0:T(8,128)(2,1)S(1)}, bf16[1,272,256]{2,1,0:T(8,128)(2,1)S(1)}, u32[]{:S(2)}, u32[]{:S(2)}) collective-permute-start(bf16[1,272,256]{2,1,0:T(8,128)(2,1)S(1)} %get-tuple-element.21), channel_id=1, source_target_pairs={{0,1},{1,0},{2,3},{3,2},{4,5},{5,4},{6,7},{7,6},{8,9},{9,8},{10,11... | collective-permute-start | bytes 417800 | tf_op jit(solution)/shard_map/ppermute | solution.py:471
  3.0 6.9 %collective-permute-start.1 = (bf16[1,272,256]{2,1,0:T(8,128)(2,1)S(1)}, bf16[1,272,256]{2,1,0:T(8,128)(2,1)S(1)}, u32[]{:S(2)}, u32[]{:S(2)}) collective-permute-start(bf16[1,272,256]{2,1,0:T(8,128)(2,1)S(1)} %get-tuple-element.23), channel_id=1, source_target_pairs={{0,2},{1,3},{2,0},{3,1},{4,6},{5,7},{6,4},{7,5},{8,10},{9,11},{10,... | collective-permute-start | bytes 417800 | tf_op jit(solution)/shard_map/ppermute | solution.py:475
  13.4 1.9 %collective-permute-start.2 = (f32[272,256]{1,0:T(8,128)S(1)}, f32[272,256]{1,0:T(8,128)S(1)}, u32[]{:S(2)}, u32[]{:S(2)}) collective-permute-start(f32[272,256]{1,0:T(8,128)S(1)} %get-tuple-element.26.own_ref.refs_0_), channel_id=1, source_target_pairs={{0,1},{1,0},{2,3},{3,2},{4,5},{5,4},{6,7},{7,6},{8,9},{9,8},{10,11... | collective-permute-start | bytes 835592 | tf_op jit(solution)/shard_map/ppermute | solution.py:489
  13.5 7.1 %collective-permute-start.4 = (bf16[272,256]{1,0:T(8,128)(2,1)S(1)}, bf16[272,256]{1,0:T(8,128)(2,1)S(1)}, u32[]{:S(2)}, u32[]{:S(2)}) collective-permute-start(bf16[272,256]{1,0:T(8,128)(2,1)S(1)} %get-tuple-element.28), channel_id=1, source_target_pairs={{0,4},{4,0},{8,12},{12,8},{16,20},{20,16},{24,28},{28,24},{1,5},{5... | collective-permute-start | bytes 417800 | tf_op jit(solution)/shard_map/ppermute | solution.py:490
  15.6 6.5 %collective-permute-start.6 = (bf16[272,256]{1,0:T(8,128)(2,1)S(1)}, bf16[272,256]{1,0:T(8,128)(2,1)S(1)}, u32[]{:S(2)}, u32[]{:S(2)}) collective-permute-start(bf16[272,256]{1,0:T(8,128)(2,1)S(1)} %block_map.1.own_ref.refs_7_), channel_id=1, source_target_pairs={{0,8},{1,13},{2,10},{3,15},{4,12},{5,9},{6,14},{7,11},{8,0},{9,5},... | collective-permute-start | bytes 417800 | tf_op jit(solution)/shard_map/ppermute | solution.py:493
  20.6 3.0 %collective-permute-start.5 = (bf16[272,256]{1,0:T(8,128)(2,1)S(1)}, bf16[272,256]{1,0:T(8,128)(2,1)S(1)}, u32[]{:S(2)}, u32[]{:S(2)}) collective-permute-start(bf16[272,256]{1,0:T(8,128)(2,1)S(1)} %collective-permute-done.4.last_ref.refs_4_), channel_id=1, source_target_pairs={{0,1},{1,0},{2,3},{3,2},{4,5},{5,4},{6,7},{7,6},{8,9},{9,8},{10,11... | collective-permute-start | bytes 417800 | tf_op jit(solution)/shard_map/ppermute | solution.py:494
  22.2 1.4 %collective-permute-start.7 = (bf16[272,256]{1,0:T(8,128)(2,1)S(1)}, bf16[272,256]{1,0:T(8,128)(2,1)S(1)}, u32[]{:S(2)}, u32[]{:S(2)}) collective-permute-start(bf16[272,256]{1,0:T(8,128)(2,1)S(1)} %collective-permute-done.6.far_ref), channel_id=1, source_target_pairs={{0,1},{1,0},{2,3},{3,2},{4,5},{5,4},{6,7},{7,6},{8,9},{9,8},{10,11... | collective-permute-start | bytes 417800 | tf_op jit(solution)/shard_map/ppermute | solution.py:495
  22.2 6.7 %collective-permute-start.3 = (f32[1,272,256]{2,1,0:T(8,128)S(1)}, f32[1,272,256]{2,1,0:T(8,128)S(1)}, u32[]{:S(2)}, u32[]{:S(2)}) collective-permute-start(f32[1,272,256]{2,1,0:T(8,128)S(1)} %get-tuple-element.27.refs_2_), channel_id=1, source_target_pairs={{0,1},{1,0},{2,3},{3,2},{4,5},{5,4},{6,7},{7,6},{8,9},{9,8},{10,11... | collective-permute-start | bytes 835592 | tf_op jit(solution)/shard_map/ppermute | solution.py:525
  22.7 5.6 %collective-permute-start.9 = (bf16[1,272,256]{2,1,0:T(8,128)(2,1)S(1)}, bf16[1,272,256]{2,1,0:T(8,128)(2,1)S(1)}, u32[]{:S(2)}, u32[]{:S(2)}) collective-permute-start(bf16[1,272,256]{2,1,0:T(8,128)(2,1)S(1)} %get-tuple-element.33), channel_id=1, source_target_pairs={{0,4},{4,0},{8,12},{12,8},{16,20},{20,16},{24,28},{28,24},{1,5},{5... | collective-permute-start | bytes 417800 | tf_op jit(solution)/shard_map/ppermute | solution.py:491
  24.2 4.6 %collective-permute-start.8 = (f32[8,256]{1,0:T(8,128)S(1)}, f32[8,256]{1,0:T(8,128)S(1)}, u32[]{:S(2)}, u32[]{:S(2)}) collective-permute-start(f32[8,256]{1,0:T(8,128)S(1)} %get-tuple-element.29), channel_id=1, source_target_pairs={{0,16},{4,20},{8,24},{12,28},{16,0},{20,4},{24,8},{28,12},{1,17},{... | collective-permute-start | bytes 24584 | tf_op jit(solution)/shard_map/ppermute | solution.py:513
  28.8 1.4 %collective-permute-start.10 = (bf16[1,272,256]{2,1,0:T(8,128)(2,1)S(1)}, bf16[1,272,256]{2,1,0:T(8,128)(2,1)S(1)}, u32[]{:S(2)}, u32[]{:S(2)}) collective-permute-start(bf16[1,272,256]{2,1,0:T(8,128)(2,1)S(1)} %hold.1.firsts_ref), channel_id=1, source_target_pairs={{0,1},{1,0},{2,3},{3,2},{4,5},{5,4},{6,7},{7,6},{8,9},{9,8},{10,11... | collective-permute-start | bytes 417800 | tf_op jit(solution)/shard_map/ppermute | solution.py:535
  30.4 4.6 %collective-permute-start.12 = (f32[8,256]{1,0:T(8,128)S(1)}, f32[8,256]{1,0:T(8,128)S(1)}, u32[]{:S(2)}, u32[]{:S(2)}) collective-permute-start(f32[8,256]{1,0:T(8,128)S(1)} %rest_of_means.1.refs_0_), channel_id=1, source_target_pairs={{0,16},{1,25},{2,18},{3,27},{4,20},{5,29},{6,22},{7,31},{8,24},{9,... | collective-permute-start | bytes 24584 | tf_op jit(solution)/shard_map/ppermute | solution.py:543
  33.1 3.7 %collective-permute-start.11 = (f32[8,256]{1,0:T(8,128)S(1)}, f32[8,256]{1,0:T(8,128)S(1)}, u32[]{:S(2)}, u32[]{:S(2)}) collective-permute-start(f32[8,256]{1,0:T(8,128)S(1)} %rest_of_means.1.refs_0_), channel_id=1, source_target_pairs={{0,8},{4,12},{8,0},{12,4},{16,24},{20,28},{24,16},{28,20},{1,9},{5... | collective-permute-start | bytes 24584 | tf_op jit(solution)/shard_map/ppermute | solution.py:544
  35.0 1.8 %collective-permute-start.13 = (f32[8,256]{1,0:T(8,128)S(1)}, f32[8,256]{1,0:T(8,128)S(1)}, u32[]{:S(2)}, u32[]{:S(2)}) collective-permute-start(f32[8,256]{1,0:T(8,128)S(1)} %collective-permute-done.12.refs_2_), channel_id=1, source_target_pairs={{0,1},{1,0},{2,3},{3,2},{4,5},{5,4},{6,7},{7,6},{8,9},{9,8},{10,11... | collective-permute-start | bytes 24584 | tf_op jit(solution)/shard_map/ppermute | solution.py:545

commit v7 on v6

--- a/solution.py
+++ b/solution.py
@@ -13,6 +13,9 @@
 BF16 = jnp.bfloat16
 F32 = jnp.float32
 VMEM_LIMIT = 40 * 2**20
+COSTS = {
+    "pair_block": pl.CostEstimate(flops=3000000000, bytes_accessed=0, transcendentals=0),
+}
 
 
 def whole():
@@ -29,6 +32,7 @@
         out_specs=jax.tree.map(lambda _: whole(), outs),
         scratch_shapes=scratch,
         compiler_params=pltpu.CompilerParams(vmem_limit_bytes=VMEM_LIMIT),
+        cost_estimate=COSTS.get(name),
         name=name,
     )(*args)
 
@@ -270,14 +274,36 @@
     out_ref[...] = rounded(append(early, late))
 
 
-def group_blocks(own_ref, last_ref, far_ref, other_last_ref, other_far_ref, *out_refs):
-    shift_ref, out_refs = out_refs[-1], out_refs[:-1]
+def pair_block(own_ref, last_ref, other_last_ref, next_ref, pair_ref):
     (early,), (late,) = in_order([last_ref[...]], [other_last_ref[...]])
-    out_refs[0][...] = follow(early, late)
+    own, following = own_ref[...], follow(early, late)
+    next_ref[...] = following
+    odd = lax.rem(lax.axis_index("tm"), 2) == 1
+    first, second = jnp.where(odd, following, own), jnp.where(odd, own, following)
+    states = own.shape[1]
+    pair_ref[:states, :] = dot(first[:states], second[:states])
+    pair_ref[states:, :] = jnp.broadcast_to(apply(second, shift_of(first)), (8, states))
+
+
+def group_blocks(own_ref, next_ref, pair_ref, far_ref, other_far_ref, out_ref, shift_ref):
     (near,), (far,) = in_order([far_ref[...]], [other_far_ref[...]])
-    out_refs[1][...] = near
-    out_refs[2][...] = far
-    group_shift(own_ref, *out_refs, shift_ref)
+    out_ref[0] = own_ref[...]
+    out_ref[1] = next_ref[...]
+    out_ref[2] = near
+    out_ref[3] = far
+    states = near.shape[1]
+    place = lax.rem(lax.axis_index("tm"), out_ref.shape[0])
+    odd, upper = lax.rem(place, 2) == 1, place >= 2
+    first, second = jnp.where(odd, far, near), jnp.where(odd, near, far)
+    pair = pair_ref[:states, :]
+    pair_shift = pair_ref[states : states + 1, :]
+    high, low = split(pair)
+    mean = jnp.where(upper, shift_of(first), pair_shift)
+    mean = apply(jnp.where(upper, second, first), mean)
+    high = jnp.where(upper, high, second[:states])
+    low = jnp.where(upper, low, jnp.zeros_like(low))
+    mean = row_times(mean, high, low) + jnp.where(upper, pair_shift, shift_of(second))
+    shift_ref[...] = jnp.broadcast_to(mean, shift_ref.shape)
 
 
 def shift_of(block):
@@ -292,10 +318,6 @@
     return value
 
 
-def pick(refs, slot):
-    return choose([ref[...] for ref in refs], slot)
-
-
 def apply(block, mean):
     return row_times(mean, block[: block.shape[1]]) + shift_of(block)
 
@@ -306,21 +328,11 @@
     return jnp.concatenate([product, thirds(apply(latter, shift_of(earlier)))], axis=0)
 
 
-def group_shift(*refs):
-    gathered, out_ref = refs[:-1], refs[-1]
-    place = lax.rem(lax.axis_index("tm"), len(gathered))
-    mean = shift_of(pick(gathered, place))
-    for i in range(1, len(gathered)):
-        mean = apply(pick(gathered, place ^ i), mean)
-    out_ref[...] = jnp.broadcast_to(mean, out_ref.shape)
-
-
-def group_map(*refs):
-    gathered, out_ref = refs[:-1], refs[-1]
-    place = lax.rem(lax.axis_index("tm"), len(gathered))
-    joined = pick(gathered, place)
-    for i in range(1, len(gathered)):
-        joined = follow(joined, pick(gathered, place ^ i))
+def group_map(gathered_ref, out_ref):
+    place = lax.rem(lax.axis_index("tm"), gathered_ref.shape[0])
+    joined = gathered_ref[place]
+    for i in range(1, gathered_ref.shape[0]):
+        joined = follow(joined, gathered_ref[place ^ i])
     out_ref[...] = joined
 
 
@@ -342,7 +354,7 @@
 def pair_means(distances, *refs):
     out_ref = refs[-1]
     own_last_ref, own_other_ref, own_firsts_ref, other_firsts_ref, last_ref, other_last_ref = refs[:6]
-    levels, gathered = refs[6 : 6 + len(distances)], refs[6 + len(distances) : -1]
+    levels, gathered_ref = refs[6:-2], refs[-2]
     rows, states = own_last_ref.shape
     half = own_firsts_ref.shape[0] + 1
     mean = jnp.zeros((1, states), F32)
@@ -352,11 +364,11 @@
         else:
             entered = apply(levels[level][...], mean)
         mean = jnp.where(is_upper(distances[level]), entered, mean)
-    place = lax.rem(lax.axis_index("tm"), len(gathered))
+    place = lax.rem(lax.axis_index("tm"), gathered_ref.shape[0])
     for i in range(2):
-        mean = jnp.where(place >= 2, apply(pick(gathered, place ^ i), mean), mean)
+        mean = jnp.where(place >= 2, apply(gathered_ref[place ^ i], mean), mean)
     odd = lax.rem(place, 2) == 1
-    between = apply(pick(gathered, place & 1), mean)
+    between = apply(gathered_ref[place & 1], mean)
     own_start = jnp.where(odd, between, mean)
     own = []
     sides = [
@@ -494,17 +506,22 @@
     others_last = lax.ppermute(last, "site", swaps(hours, 1))
     others_far = lax.ppermute(far, "site", swaps(hours, 1))
     radix = 4
-    *gathered, shift = call(
+    following, pair = call(
+        pair_block,
+        (block, sds((states + 8, states), F32)),
+        (own, last, others_last),
+        "pair_block",
+    )
+    gathered, shift = call(
         group_blocks,
-        (block,) * 3 + (sds((8, states), F32),),
-        (own, last, far, others_last, others_far),
+        (sds((radix, rows, states), BF16), sds((8, states), F32)),
+        (own, following, pair, far, others_far),
         "group_blocks",
     )
-    gathered = (own, *gathered)
     distances, levels = [], []
     distance = radix
     if 2 * distance < blocks:
-        joined = call(group_map, sds(own.shape, BF16), gathered, "group_map")
+        joined = call(group_map, sds(own.shape, BF16), (gathered,), "group_map")
     while distance < blocks:
         if 2 * distance == blocks:
             if levels:
@@ -528,7 +545,7 @@
         sds((2 * hours, states), F32),
         [own_last, other_last, own_firsts, other_firsts, last, others_last]
         + levels
-        + list(gathered),
+        + [gathered],
         "pair_means",
     )
     first_maps = call(hold, firsts, (first_maps, levels[-1]), "hold")

time: 38.1 us -> 37.9 us (level)
  waiting for transfers between devices: 11.8 us -> 11.1 us
    ppermute x1, waiting for transfers between devices: 1.62 us -> 0.12 us  [body(): far = lax.ppermute(own, ('tm', 'site'), core_swaps(blocks, hours, 2, 3))]
    ppermute x1, waiting for transfers between devices: 0.52 us -> 1.94 us  [body(): received = lax.ppermute(shift, 'tm', swaps(blocks, distance))]
    ppermute x1, waiting for transfers between devices: 1.43 us -> 0.02 us  [body(): first_maps = lax.ppermute(first_maps, 'tm', swaps(blocks, 1))]
    ppermute x1, waiting for transfers between devices: 0.01 us -> 0.82 us  [body(): others_far = lax.ppermute(far, 'site', swaps(hours, 1))]
    ppermute x1, starting transfers between devices: 0.85 us -> 1.28 us  [body(): first_maps = lax.ppermute(first_maps, 'tm', swaps(blocks, 1))]
    pallas_call x9 -> x10, Pallas kernels: 9.57 us -> 9.71 us  [call(): pl.pallas_call(kernel, out_shape=outs, in_specs=[pl.BlockSpec(memory_spac...]
where the time goes in v7:
time: 37.9 us; the launch traced here: 37.7 us
  starting transfers between devices  15.6 us (41%)
  waiting for transfers between devices  11.1 us (29%)
  Pallas kernels  10.9 us (29%)
    pallas_call x10, Pallas kernels, call(): pl.pallas_call(kernel, out_shape=outs, in_specs=[pl.BlockSpec(memory_spac...  9.71 us
    ppermute x1, waiting for transfers between devices, body(): last = lax.ppermute(last, 'tm', swaps(blocks, 1))  3.27 us
    ppermute x1, starting transfers between devices, body(): received = lax.ppermute(send, 'site', swaps(hours, distance))  2.91 us
    ppermute x1, starting transfers between devices, body(): received = lax.ppermute(shift, 'tm', swaps(blocks, distance))  2.66 us
    ppermute x1, starting transfers between devices, body(): far = lax.ppermute(means, ('tm', 'site'), core_swaps(blocks, hours, 4, 6))  2.66 us
    ppermute x1, waiting for transfers between devices, body(): received = lax.ppermute(shift, 'tm', swaps(blocks, distance))  1.94 us
    ppermute x1, starting transfers between devices, body(): last = lax.ppermute(last, 'tm', swaps(blocks, 1))  1.83 us
    ppermute x1, waiting for transfers between devices, body(): near = lax.ppermute(means, 'tm', swaps(blocks, 2))  1.73 us
  transfers between devices with their start and end apart: 14, of which 9 were waited for; matrix products, arithmetic and copies ran while one was open for 0% of the time, Pallas kernels for 12%

profile of v7, /device:TPU:0, one launch (start us, length us, event | category | flops | bytes accessed | tf_op | source)
XLA Modules:
  0.0 37.7 jit_solution(2102798945077566744)
XLA Ops:
  0.0 1.5 %local_grams.1 = (f32[1,264,256]{2,1,0:T(8,128)S(1)}, bf16[1,272,256]{2,1,0:T(8,128)(2,1)S(1)}) custom-call(bf16[512,256]{1,0:T(8,128)(2,1)} %rows_hbm.1, bf16[512]{0:T(512)(128)(2,1)} %values_hbm.1, s32[512]{0:T(512)} %codes_hbm.1), custom_call_target="tpu_custom_call" | custom-call | tf_op jit(solution)/shard_map/local_grams/pallas_call | solution.py:28
  1.5 0.5 %collective-permute-start = (bf16[1,272,256]{2,1,0:T(8,128)(2,1)S(1)}, bf16[1,272,256]{2,1,0:T(8,128)(2,1)S(1)}, u32[]{:S(2)}, u32[]{:S(2)}) collective-permute-start(bf16[1,272,256]{2,1,0:T(8,128)(2,1)S(1)} %get-tuple-element.21), channel_id=1, source_target_pairs={{0,1},{1,0},{2,3},{3,2},{4,5},{5,4},{6,7},{7,6},{8,9},{9,8},{10,11... | collective-permute-start | bytes 417800 | tf_op jit(solution)/shard_map/ppermute | solution.py:483
  2.0 1.0 %collective-permute-done.received_ref = bf16[1,272,256]{2,1,0:T(8,128)(2,1)S(1)} collective-permute-done((bf16[1,272,256]{2,1,0:T(8,128)(2,1)S(1)}, bf16[1,272,256]{2,1,0:T(8,128)(2,1)S(1)}, u32[]{:S(2)}, u32[]{:S(2)}) %collective-permute-start) | collective-permute-done | bytes 139296 | tf_op jit(solution)/shard_map/ppermute | solution.py:483
  3.0 2.9 %collective-permute-start.1 = (bf16[1,272,256]{2,1,0:T(8,128)(2,1)S(1)}, bf16[1,272,256]{2,1,0:T(8,128)(2,1)S(1)}, u32[]{:S(2)}, u32[]{:S(2)}) collective-permute-start(bf16[1,272,256]{2,1,0:T(8,128)(2,1)S(1)} %get-tuple-element.23), channel_id=1, source_target_pairs={{0,2},{1,3},{2,0},{3,1},{4,6},{5,7},{6,4},{7,5},{8,10},{9,11},{10,... | collective-permute-start | bytes 417800 | tf_op jit(solution)/shard_map/ppermute | solution.py:487
  6.0 2.4 %prepare.1 = (f32[256,256]{1,0:T(8,128)S(1)}, f32[256,256]{1,0:T(8,128)S(1)}, bf16[256,4096]{1,0:T(8,128)(2,1)S(1)}) custom-call(f32[256,256]{1,0:T(8,128)} %prior_hbm.1, f32[256,256]{1,0:T(8,128)} %transition_hbm.1, bf16[4096,256]{1,0:T(8,128)(2,1)} %basis_hbm.1), custom_call_target="tpu_custom_call" | custom-call | tf_op jit(solution)/shard_map/prepare/pallas_call | solution.py:28
  8.4 1.5 %collective-permute-done.1.received_ref = bf16[1,272,256]{2,1,0:T(8,128)(2,1)S(1)} collective-permute-done((bf16[1,272,256]{2,1,0:T(8,128)(2,1)S(1)}, bf16[1,272,256]{2,1,0:T(8,128)(2,1)S(1)}, u32[]{:S(2)}, u32[]{:S(2)}) %collective-permute-start.1) | collective-permute-done | bytes 139296 | tf_op jit(solution)/shard_map/ppermute | solution.py:487
  9.9 3.4 %hour_maps.1 = (f32[272,256]{1,0:T(8,128)S(1)}, f32[1,272,256]{2,1,0:T(8,128)S(1)}, bf16[272,256]{1,0:T(8,128)(2,1)S(1)}, bf16[1,272,256]{2,1,0:T(8,128)(2,1)S(1)}) custom-call(f32[1,264,256]{2,1,0:T(8,128)S(1)} %get-tuple-element.22.sum_ref, bf16[1,272,256]{2,1,0:T(8,128)(2,1)S(1)} %collective-permute-done.1.received_ref, ...), custom_call_target="tpu_custom_call" | custom-call | tf_op jit(solution)/shard_map/hour_maps/pallas_call | solution.py:28
  13.4 0.1 collective-permute-start.2
  13.5 1.8 %collective-permute-start.4 = (bf16[272,256]{1,0:T(8,128)(2,1)S(1)}, bf16[272,256]{1,0:T(8,128)(2,1)S(1)}, u32[]{:S(2)}, u32[]{:S(2)}) collective-permute-start(bf16[272,256]{1,0:T(8,128)(2,1)S(1)} %get-tuple-element.28), channel_id=1, source_target_pairs={{0,4},{4,0},{8,12},{12,8},{16,20},{20,16},{24,28},{28,24},{1,5},{5... | collective-permute-start | bytes 417800 | tf_op jit(solution)/shard_map/ppermute | solution.py:502
  15.3 0.0 collective-permute-done.2.received_ref.refs_1_
  15.3 0.3 block_map.1.own_ref
  15.6 1.6 %collective-permute-start.6 = (bf16[272,256]{1,0:T(8,128)(2,1)S(1)}, bf16[272,256]{1,0:T(8,128)(2,1)S(1)}, u32[]{:S(2)}, u32[]{:S(2)}) collective-permute-start(bf16[272,256]{1,0:T(8,128)(2,1)S(1)} %block_map.1.own_ref), channel_id=1, source_target_pairs={{0,8},{1,13},{2,10},{3,15},{4,12},{5,9},{6,14},{7,11},{8,0},{9,5},... | collective-permute-start | bytes 417800 | tf_op jit(solution)/shard_map/ppermute | solution.py:505
  17.3 3.3 %collective-permute-done.4.last_ref.refs_4_ = bf16[272,256]{1,0:T(8,128)(2,1)S(1)} collective-permute-done((bf16[272,256]{1,0:T(8,128)(2,1)S(1)}, bf16[272,256]{1,0:T(8,128)(2,1)S(1)}, u32[]{:S(2)}, u32[]{:S(2)}) %collective-permute-start.4) | collective-permute-done | bytes 139296 | tf_op jit(solution)/shard_map/ppermute | solution.py:502
  20.6 0.0 collective-permute-start.5
  20.6 1.3 %collective-permute-start.9 = (bf16[1,272,256]{2,1,0:T(8,128)(2,1)S(1)}, bf16[1,272,256]{2,1,0:T(8,128)(2,1)S(1)}, u32[]{:S(2)}, u32[]{:S(2)}) collective-permute-start(bf16[1,272,256]{2,1,0:T(8,128)(2,1)S(1)} %get-tuple-element.33), channel_id=1, source_target_pairs={{0,4},{4,0},{8,12},{12,8},{16,20},{20,16},{24,28},{28,24},{1,5},{5... | collective-permute-start | bytes 417800 | tf_op jit(solution)/shard_map/ppermute | solution.py:503
  21.8 0.2 collective-permute-start.3
  22.1 0.1 collective-permute-done.6.far_ref
  22.2 0.2 collective-permute-start.7
  22.4 0.0 collective-permute-done.5.other_last_ref.refs_5_
  22.4 0.4 %pair_block.1 = (bf16[272,256]{1,0:T(8,128)(2,1)S(1)}, f32[264,256]{1,0:T(8,128)S(1)}) custom-call(bf16[272,256]{1,0:T(8,128)(2,1)S(1)} %block_map.1.own_ref, bf16[272,256]{1,0:T(8,128)(2,1)S(1)} %collective-permute-done.4.last_ref.refs_4_, bf16[272,256]{1,0:T(8,128)(2,1)S(1)} %collective-permute-done.5.other_last_ref.refs_5_), custom_call_target="tpu_custom_call" | custom-call | flops 3000000000 | tf_op jit(solution)/shard_map/pair_block/pallas_call | solution.py:28
  22.8 0.8 %collective-permute-done.7.other_far_ref = bf16[272,256]{1,0:T(8,128)(2,1)S(1)} collective-permute-done((bf16[272,256]{1,0:T(8,128)(2,1)S(1)}, bf16[272,256]{1,0:T(8,128)(2,1)S(1)}, u32[]{:S(2)}, u32[]{:S(2)}) %collective-permute-start.7) | collective-permute-done | bytes 139296 | tf_op jit(solution)/shard_map/ppermute | solution.py:507
  23.6 0.4 group_blocks.1
  24.0 2.7 %collective-permute-start.8 = (f32[8,256]{1,0:T(8,128)S(1)}, f32[8,256]{1,0:T(8,128)S(1)}, u32[]{:S(2)}, u32[]{:S(2)}) collective-permute-start(f32[8,256]{1,0:T(8,128)S(1)} %get-tuple-element.31), channel_id=1, source_target_pairs={{0,16},{4,20},{8,24},{12,28},{16,0},{20,4},{24,8},{28,12},{1,17},{... | collective-permute-start | bytes 24584 | tf_op jit(solution)/shard_map/ppermute | solution.py:530
  26.6 0.0 collective-permute-done.9.maps_ref
  26.6 1.9 %collective-permute-done.8.refs_6_.received_ref = f32[8,256]{1,0:T(8,128)S(1)} collective-permute-done((f32[8,256]{1,0:T(8,128)S(1)}, f32[8,256]{1,0:T(8,128)S(1)}, u32[]{:S(2)}, u32[]{:S(2)}) %collective-permute-start.8) | collective-permute-done | bytes 8224 | tf_op jit(solution)/shard_map/ppermute | solution.py:530
  28.6 0.1 collective-permute-start.10
  28.7 0.0 collective-permute-done.3.refs_3_
  28.7 1.0 %pair_means.1.means_ref = f32[8,256]{1,0:T(8,128)S(1)} custom-call(f32[272,256]{1,0:T(8,128)S(1)} %get-tuple-element.26.own_ref.refs_0_, f32[272,256]{1,0:T(8,128)S(1)} %collective-permute-done.2.received_ref.refs_1_, f32[1,272,256]{2,1,0:T(8,128)S(1)} %get-tuple-element.27.refs_2_, f32[1,272,256]{2,1,0:T(8,128)S(1)} %collective-permute-done.3.refs_3_, ...), custom_call_target="tpu_custom_call" | custom-call | tf_op jit(solution)/shard_map/pair_means/pallas_call | solution.py:28
  29.7 0.3 collective-permute-done.10.other_ref
  30.0 0.2 rest_of_means.1.refs_0_
  30.2 2.7 %collective-permute-start.12 = (f32[8,256]{1,0:T(8,128)S(1)}, f32[8,256]{1,0:T(8,128)S(1)}, u32[]{:S(2)}, u32[]{:S(2)}) collective-permute-start(f32[8,256]{1,0:T(8,128)S(1)} %rest_of_means.1.refs_0_), channel_id=1, source_target_pairs={{0,16},{1,25},{2,18},{3,27},{4,20},{5,29},{6,22},{7,31},{8,24},{9,... | collective-permute-start | bytes 24584 | tf_op jit(solution)/shard_map/ppermute | solution.py:560
  32.8 1.6 %collective-permute-start.11 = (f32[8,256]{1,0:T(8,128)S(1)}, f32[8,256]{1,0:T(8,128)S(1)}, u32[]{:S(2)}, u32[]{:S(2)}) collective-permute-start(f32[8,256]{1,0:T(8,128)S(1)} %rest_of_means.1.refs_0_), channel_id=1, source_target_pairs={{0,8},{4,12},{8,0},{12,4},{16,24},{20,28},{24,16},{28,20},{1,9},{5... | collective-permute-start | bytes 24584 | tf_op jit(solution)/shard_map/ppermute | solution.py:561
  34.4 0.4 %collective-permute-done.12.refs_2_ = f32[8,256]{1,0:T(8,128)S(1)} collective-permute-done((f32[8,256]{1,0:T(8,128)S(1)}, f32[8,256]{1,0:T(8,128)S(1)}, u32[]{:S(2)}, u32[]{:S(2)}) %collective-permute-start.12) | collective-permute-done | bytes 8224 | tf_op jit(solution)/shard_map/ppermute | solution.py:560
  34.8 0.0 collective-permute-start.13
  34.8 1.7 %collective-permute-done.11.refs_1_ = f32[8,256]{1,0:T(8,128)S(1)} collective-permute-done((f32[8,256]{1,0:T(8,128)S(1)}, f32[8,256]{1,0:T(8,128)S(1)}, u32[]{:S(2)}, u32[]{:S(2)}) %collective-permute-start.11) | collective-permute-done | bytes 8224 | tf_op jit(solution)/shard_map/ppermute | solution.py:561
  36.5 0.0 collective-permute-done.13.refs_3_
  36.5 1.1 %predict.1 = bf16[32,4096]{1,0:T(8,128)(2,1)} custom-call(f32[8,256]{1,0:T(8,128)S(1)} %rest_of_means.1.refs_0_, f32[8,256]{1,0:T(8,128)S(1)} %collective-permute-done.11.refs_1_, f32[8,256]{1,0:T(8,128)S(1)} %collective-permute-done.12.refs_2_, f32[8,256]{1,0:T(8,128)S(1)} %collective-permute-done.13.refs_3_, bf16[256,4096]{1,0:T(8,128)(2,1)S(1)} %get-tuple-element.34.refs_4_), custom_call_target="tpu_custom_call" | custom-call | tf_op jit(solution)/shard_map/predict/pallas_call | solution.py:568
  (2 shorter events, 0.0 us)
Async XLA Ops:
  1.5 1.5 %collective-permute-start = (bf16[1,272,256]{2,1,0:T(8,128)(2,1)S(1)}, bf16[1,272,256]{2,1,0:T(8,128)(2,1)S(1)}, u32[]{:S(2)}, u32[]{:S(2)}) collective-permute-start(bf16[1,272,256]{2,1,0:T(8,128)(2,1)S(1)} %get-tuple-element.21), channel_id=1, source_target_pairs={{0,1},{1,0},{2,3},{3,2},{4,5},{5,4},{6,7},{7,6},{8,9},{9,8},{10,11... | collective-permute-start | bytes 417800 | tf_op jit(solution)/shard_map/ppermute | solution.py:483
  3.0 6.9 %collective-permute-start.1 = (bf16[1,272,256]{2,1,0:T(8,128)(2,1)S(1)}, bf16[1,272,256]{2,1,0:T(8,128)(2,1)S(1)}, u32[]{:S(2)}, u32[]{:S(2)}) collective-permute-start(bf16[1,272,256]{2,1,0:T(8,128)(2,1)S(1)} %get-tuple-element.23), channel_id=1, source_target_pairs={{0,2},{1,3},{2,0},{3,1},{4,6},{5,7},{6,4},{7,5},{8,10},{9,11},{10,... | collective-permute-start | bytes 417800 | tf_op jit(solution)/shard_map/ppermute | solution.py:487
  13.4 1.9 %collective-permute-start.2 = (f32[272,256]{1,0:T(8,128)S(1)}, f32[272,256]{1,0:T(8,128)S(1)}, u32[]{:S(2)}, u32[]{:S(2)}) collective-permute-start(f32[272,256]{1,0:T(8,128)S(1)} %get-tuple-element.26.own_ref.refs_0_), channel_id=1, source_target_pairs={{0,1},{1,0},{2,3},{3,2},{4,5},{5,4},{6,7},{7,6},{8,9},{9,8},{10,11... | collective-permute-start | bytes 835592 | tf_op jit(solution)/shard_map/ppermute | solution.py:501
  13.5 7.1 %collective-permute-start.4 = (bf16[272,256]{1,0:T(8,128)(2,1)S(1)}, bf16[272,256]{1,0:T(8,128)(2,1)S(1)}, u32[]{:S(2)}, u32[]{:S(2)}) collective-permute-start(bf16[272,256]{1,0:T(8,128)(2,1)S(1)} %get-tuple-element.28), channel_id=1, source_target_pairs={{0,4},{4,0},{8,12},{12,8},{16,20},{20,16},{24,28},{28,24},{1,5},{5... | collective-permute-start | bytes 417800 | tf_op jit(solution)/shard_map/ppermute | solution.py:502
  15.6 6.5 %collective-permute-start.6 = (bf16[272,256]{1,0:T(8,128)(2,1)S(1)}, bf16[272,256]{1,0:T(8,128)(2,1)S(1)}, u32[]{:S(2)}, u32[]{:S(2)}) collective-permute-start(bf16[272,256]{1,0:T(8,128)(2,1)S(1)} %block_map.1.own_ref), channel_id=1, source_target_pairs={{0,8},{1,13},{2,10},{3,15},{4,12},{5,9},{6,14},{7,11},{8,0},{9,5},... | collective-permute-start | bytes 417800 | tf_op jit(solution)/shard_map/ppermute | solution.py:505
  20.6 1.8 %collective-permute-start.5 = (bf16[272,256]{1,0:T(8,128)(2,1)S(1)}, bf16[272,256]{1,0:T(8,128)(2,1)S(1)}, u32[]{:S(2)}, u32[]{:S(2)}) collective-permute-start(bf16[272,256]{1,0:T(8,128)(2,1)S(1)} %collective-permute-done.4.last_ref.refs_4_), channel_id=1, source_target_pairs={{0,1},{1,0},{2,3},{3,2},{4,5},{5,4},{6,7},{7,6},{8,9},{9,8},{10,11... | collective-permute-start | bytes 417800 | tf_op jit(solution)/shard_map/ppermute | solution.py:506
  20.6 6.1 %collective-permute-start.9 = (bf16[1,272,256]{2,1,0:T(8,128)(2,1)S(1)}, bf16[1,272,256]{2,1,0:T(8,128)(2,1)S(1)}, u32[]{:S(2)}, u32[]{:S(2)}) collective-permute-start(bf16[1,272,256]{2,1,0:T(8,128)(2,1)S(1)} %get-tuple-element.33), channel_id=1, source_target_pairs={{0,4},{4,0},{8,12},{12,8},{16,20},{20,16},{24,28},{28,24},{1,5},{5... | collective-permute-start | bytes 417800 | tf_op jit(solution)/shard_map/ppermute | solution.py:503
  21.8 6.8 %collective-permute-start.3 = (f32[1,272,256]{2,1,0:T(8,128)S(1)}, f32[1,272,256]{2,1,0:T(8,128)S(1)}, u32[]{:S(2)}, u32[]{:S(2)}) collective-permute-start(f32[1,272,256]{2,1,0:T(8,128)S(1)} %get-tuple-element.27.refs_2_), channel_id=1, source_target_pairs={{0,1},{1,0},{2,3},{3,2},{4,5},{5,4},{6,7},{7,6},{8,9},{9,8},{10,11... | collective-permute-start | bytes 835592 | tf_op jit(solution)/shard_map/ppermute | solution.py:542
  22.2 1.4 %collective-permute-start.7 = (bf16[272,256]{1,0:T(8,128)(2,1)S(1)}, bf16[272,256]{1,0:T(8,128)(2,1)S(1)}, u32[]{:S(2)}, u32[]{:S(2)}) collective-permute-start(bf16[272,256]{1,0:T(8,128)(2,1)S(1)} %collective-permute-done.6.far_ref), channel_id=1, source_target_pairs={{0,1},{1,0},{2,3},{3,2},{4,5},{5,4},{6,7},{7,6},{8,9},{9,8},{10,11... | collective-permute-start | bytes 417800 | tf_op jit(solution)/shard_map/ppermute | solution.py:507
  24.0 4.6 %collective-permute-start.8 = (f32[8,256]{1,0:T(8,128)S(1)}, f32[8,256]{1,0:T(8,128)S(1)}, u32[]{:S(2)}, u32[]{:S(2)}) collective-permute-start(f32[8,256]{1,0:T(8,128)S(1)} %get-tuple-element.31), channel_id=1, source_target_pairs={{0,16},{4,20},{8,24},{12,28},{16,0},{20,4},{24,8},{28,12},{1,17},{... | collective-permute-start | bytes 24584 | tf_op jit(solution)/shard_map/ppermute | solution.py:530
  28.6 1.4 %collective-permute-start.10 = (bf16[1,272,256]{2,1,0:T(8,128)(2,1)S(1)}, bf16[1,272,256]{2,1,0:T(8,128)(2,1)S(1)}, u32[]{:S(2)}, u32[]{:S(2)}) collective-permute-start(bf16[1,272,256]{2,1,0:T(8,128)(2,1)S(1)} %hold.1.firsts_ref), channel_id=1, source_target_pairs={{0,1},{1,0},{2,3},{3,2},{4,5},{5,4},{6,7},{7,6},{8,9},{9,8},{10,11... | collective-permute-start | bytes 417800 | tf_op jit(solution)/shard_map/ppermute | solution.py:552
  30.2 4.6 %collective-permute-start.12 = (f32[8,256]{1,0:T(8,128)S(1)}, f32[8,256]{1,0:T(8,128)S(1)}, u32[]{:S(2)}, u32[]{:S(2)}) collective-permute-start(f32[8,256]{1,0:T(8,128)S(1)} %rest_of_means.1.refs_0_), channel_id=1, source_target_pairs={{0,16},{1,25},{2,18},{3,27},{4,20},{5,29},{6,22},{7,31},{8,24},{9,... | collective-permute-start | bytes 24584 | tf_op jit(solution)/shard_map/ppermute | solution.py:560
  32.8 3.7 %collective-permute-start.11 = (f32[8,256]{1,0:T(8,128)S(1)}, f32[8,256]{1,0:T(8,128)S(1)}, u32[]{:S(2)}, u32[]{:S(2)}) collective-permute-start(f32[8,256]{1,0:T(8,128)S(1)} %rest_of_means.1.refs_0_), channel_id=1, source_target_pairs={{0,8},{4,12},{8,0},{12,4},{16,24},{20,28},{24,16},{28,20},{1,9},{5... | collective-permute-start | bytes 24584 | tf_op jit(solution)/shard_map/ppermute | solution.py:561
  34.8 1.7 %collective-permute-start.13 = (f32[8,256]{1,0:T(8,128)S(1)}, f32[8,256]{1,0:T(8,128)S(1)}, u32[]{:S(2)}, u32[]{:S(2)}) collective-permute-start(f32[8,256]{1,0:T(8,128)S(1)} %collective-permute-done.12.refs_2_), channel_id=1, source_target_pairs={{0,1},{1,0},{2,3},{3,2},{4,5},{5,4},{6,7},{7,6},{8,9},{9,8},{10,11... | collective-permute-start | bytes 24584 | tf_op jit(solution)/shard_map/ppermute | solution.py:562

commit v8 on v7

--- a/solution.py
+++ b/solution.py
@@ -187,16 +187,16 @@
     return sum_ref[pair] + jnp.concatenate([received[:states], tail], axis=0)
 
 
-def times_own(z):
+def times_own(z, coarse):
     states = z.shape[1]
     high, low = split(z)
     d_high, d_low = high[:states], low[:states]
     mixed = dot(d_high, d_low)
     square = dot(d_high, d_high) + (mixed + mixed.T)
-    rest = dot(
-        jnp.concatenate([high[states:], low[states:], high[states:]], axis=1),
-        jnp.concatenate([d_high, d_high, d_low], axis=0),
-    )
+    left, right = [high[states:], high[states:]], [d_high, d_low]
+    if not coarse:
+        left, right = left + [low[states:]], right + [d_high]
+    rest = dot(jnp.concatenate(left, axis=1), jnp.concatenate(right, axis=0))
     return jnp.concatenate([square, rest], axis=0)
 
 
@@ -232,8 +232,8 @@
             running.append((precision * scale, turned * scale, offset * scale))
     stacked = [jnp.concatenate(parts, axis=0) for parts in running]
 
-    for _ in range(NS_ITERS - 2):
-        stacked = [2.0 * z - times_own(z) for z in stacked]
+    for step in range(NS_ITERS - 2):
+        stacked = [2.0 * z - times_own(z, step < 2) for z in stacked]
     maps = []
     for z in stacked:
         power = (jnp.where(row_id == column_id, 1.0, 0.0) - z[:states]).astype(BF16)

time: 37.9 us -> 37.7 us (level)
  no operation moved by 1% of the time
where the time goes in v8:
time: 37.7 us; the launch traced here: 37.5 us
  starting transfers between devices  15.6 us (41%)
  waiting for transfers between devices  11.1 us (29%)
  Pallas kernels  10.7 us (28%)
    pallas_call x10, Pallas kernels, call(): pl.pallas_call(kernel, out_shape=outs, in_specs=[pl.BlockSpec(memory_spac...  9.53 us
    ppermute x1, waiting for transfers between devices, body(): last = lax.ppermute(last, 'tm', swaps(blocks, 1))  3.27 us
    ppermute x1, starting transfers between devices, body(): received = lax.ppermute(send, 'site', swaps(hours, distance))  2.91 us
    ppermute x1, starting transfers between devices, body(): received = lax.ppermute(shift, 'tm', swaps(blocks, distance))  2.66 us
    ppermute x1, starting transfers between devices, body(): far = lax.ppermute(means, ('tm', 'site'), core_swaps(blocks, hours, 4, 6))  2.66 us
    ppermute x1, waiting for transfers between devices, body(): received = lax.ppermute(shift, 'tm', swaps(blocks, distance))  1.93 us
    ppermute x1, starting transfers between devices, body(): last = lax.ppermute(last, 'tm', swaps(blocks, 1))  1.84 us
    ppermute x1, waiting for transfers between devices, body(): near = lax.ppermute(means, 'tm', swaps(blocks, 2))  1.73 us
  transfers between devices with their start and end apart: 14, of which 9 were waited for; matrix products, arithmetic and copies ran while one was open for 0% of the time, Pallas kernels for 12%

profile of v8, /device:TPU:0, one launch (start us, length us, event | category | flops | bytes accessed | tf_op | source)
XLA Modules:
  0.0 37.5 jit_solution(2929440586444910814)
XLA Ops:
  0.0 1.5 %local_grams.1 = (f32[1,264,256]{2,1,0:T(8,128)S(1)}, bf16[1,272,256]{2,1,0:T(8,128)(2,1)S(1)}) custom-call(bf16[512,256]{1,0:T(8,128)(2,1)} %rows_hbm.1, bf16[512]{0:T(512)(128)(2,1)} %values_hbm.1, s32[512]{0:T(512)} %codes_hbm.1), custom_call_target="tpu_custom_call" | custom-call | tf_op jit(solution)/shard_map/local_grams/pallas_call | solution.py:28
  1.5 0.5 %collective-permute-start = (bf16[1,272,256]{2,1,0:T(8,128)(2,1)S(1)}, bf16[1,272,256]{2,1,0:T(8,128)(2,1)S(1)}, u32[]{:S(2)}, u32[]{:S(2)}) collective-permute-start(bf16[1,272,256]{2,1,0:T(8,128)(2,1)S(1)} %get-tuple-element.21), channel_id=1, source_target_pairs={{0,1},{1,0},{2,3},{3,2},{4,5},{5,4},{6,7},{7,6},{8,9},{9,8},{10,11... | collective-permute-start | bytes 417800 | tf_op jit(solution)/shard_map/ppermute | solution.py:483
  2.0 1.0 %collective-permute-done.received_ref = bf16[1,272,256]{2,1,0:T(8,128)(2,1)S(1)} collective-permute-done((bf16[1,272,256]{2,1,0:T(8,128)(2,1)S(1)}, bf16[1,272,256]{2,1,0:T(8,128)(2,1)S(1)}, u32[]{:S(2)}, u32[]{:S(2)}) %collective-permute-start) | collective-permute-done | bytes 139296 | tf_op jit(solution)/shard_map/ppermute | solution.py:483
  3.0 2.9 %collective-permute-start.1 = (bf16[1,272,256]{2,1,0:T(8,128)(2,1)S(1)}, bf16[1,272,256]{2,1,0:T(8,128)(2,1)S(1)}, u32[]{:S(2)}, u32[]{:S(2)}) collective-permute-start(bf16[1,272,256]{2,1,0:T(8,128)(2,1)S(1)} %get-tuple-element.23), channel_id=1, source_target_pairs={{0,2},{1,3},{2,0},{3,1},{4,6},{5,7},{6,4},{7,5},{8,10},{9,11},{10,... | collective-permute-start | bytes 417800 | tf_op jit(solution)/shard_map/ppermute | solution.py:487
  6.0 2.4 %prepare.1 = (f32[256,256]{1,0:T(8,128)S(1)}, f32[256,256]{1,0:T(8,128)S(1)}, bf16[256,4096]{1,0:T(8,128)(2,1)S(1)}) custom-call(f32[256,256]{1,0:T(8,128)} %prior_hbm.1, f32[256,256]{1,0:T(8,128)} %transition_hbm.1, bf16[4096,256]{1,0:T(8,128)(2,1)} %basis_hbm.1), custom_call_target="tpu_custom_call" | custom-call | tf_op jit(solution)/shard_map/prepare/pallas_call | solution.py:28
  8.4 1.5 %collective-permute-done.1.received_ref = bf16[1,272,256]{2,1,0:T(8,128)(2,1)S(1)} collective-permute-done((bf16[1,272,256]{2,1,0:T(8,128)(2,1)S(1)}, bf16[1,272,256]{2,1,0:T(8,128)(2,1)S(1)}, u32[]{:S(2)}, u32[]{:S(2)}) %collective-permute-start.1) | collective-permute-done | bytes 139296 | tf_op jit(solution)/shard_map/ppermute | solution.py:487
  9.9 3.3 %hour_maps.1 = (f32[272,256]{1,0:T(8,128)S(1)}, f32[1,272,256]{2,1,0:T(8,128)S(1)}, bf16[272,256]{1,0:T(8,128)(2,1)S(1)}, bf16[1,272,256]{2,1,0:T(8,128)(2,1)S(1)}) custom-call(f32[1,264,256]{2,1,0:T(8,128)S(1)} %get-tuple-element.22.sum_ref, bf16[1,272,256]{2,1,0:T(8,128)(2,1)S(1)} %collective-permute-done.1.received_ref, ...), custom_call_target="tpu_custom_call" | custom-call | tf_op jit(solution)/shard_map/hour_maps/pallas_call | solution.py:28
  13.2 0.1 collective-permute-start.2
  13.3 1.8 %collective-permute-start.4 = (bf16[272,256]{1,0:T(8,128)(2,1)S(1)}, bf16[272,256]{1,0:T(8,128)(2,1)S(1)}, u32[]{:S(2)}, u32[]{:S(2)}) collective-permute-start(bf16[272,256]{1,0:T(8,128)(2,1)S(1)} %get-tuple-element.28), channel_id=1, source_target_pairs={{0,4},{4,0},{8,12},{12,8},{16,20},{20,16},{24,28},{28,24},{1,5},{5... | collective-permute-start | bytes 417800 | tf_op jit(solution)/shard_map/ppermute | solution.py:502
  15.1 0.0 collective-permute-done.2.received_ref.refs_1_
  15.1 0.3 block_map.1.own_ref
  15.5 1.6 %collective-permute-start.6 = (bf16[272,256]{1,0:T(8,128)(2,1)S(1)}, bf16[272,256]{1,0:T(8,128)(2,1)S(1)}, u32[]{:S(2)}, u32[]{:S(2)}) collective-permute-start(bf16[272,256]{1,0:T(8,128)(2,1)S(1)} %block_map.1.own_ref), channel_id=1, source_target_pairs={{0,8},{1,13},{2,10},{3,15},{4,12},{5,9},{6,14},{7,11},{8,0},{9,5},... | collective-permute-start | bytes 417800 | tf_op jit(solution)/shard_map/ppermute | solution.py:505
  17.1 3.3 %collective-permute-done.4.last_ref.refs_4_ = bf16[272,256]{1,0:T(8,128)(2,1)S(1)} collective-permute-done((bf16[272,256]{1,0:T(8,128)(2,1)S(1)}, bf16[272,256]{1,0:T(8,128)(2,1)S(1)}, u32[]{:S(2)}, u32[]{:S(2)}) %collective-permute-start.4) | collective-permute-done | bytes 139296 | tf_op jit(solution)/shard_map/ppermute | solution.py:502
  20.4 0.0 collective-permute-start.5
  20.4 1.3 %collective-permute-start.9 = (bf16[1,272,256]{2,1,0:T(8,128)(2,1)S(1)}, bf16[1,272,256]{2,1,0:T(8,128)(2,1)S(1)}, u32[]{:S(2)}, u32[]{:S(2)}) collective-permute-start(bf16[1,272,256]{2,1,0:T(8,128)(2,1)S(1)} %get-tuple-element.33), channel_id=1, source_target_pairs={{0,4},{4,0},{8,12},{12,8},{16,20},{20,16},{24,28},{28,24},{1,5},{5... | collective-permute-start | bytes 417800 | tf_op jit(solution)/shard_map/ppermute | solution.py:503
  21.7 0.2 collective-permute-start.3
  21.9 0.1 collective-permute-done.6.far_ref
  22.0 0.2 collective-permute-start.7
  22.2 0.0 collective-permute-done.5.other_last_ref.refs_5_
  22.2 0.4 %pair_block.1 = (bf16[272,256]{1,0:T(8,128)(2,1)S(1)}, f32[264,256]{1,0:T(8,128)S(1)}) custom-call(bf16[272,256]{1,0:T(8,128)(2,1)S(1)} %block_map.1.own_ref, bf16[272,256]{1,0:T(8,128)(2,1)S(1)} %collective-permute-done.4.last_ref.refs_4_, bf16[272,256]{1,0:T(8,128)(2,1)S(1)} %collective-permute-done.5.other_last_ref.refs_5_), custom_call_target="tpu_custom_call" | custom-call | flops 3000000000 | tf_op jit(solution)/shard_map/pair_block/pallas_call | solution.py:28
  22.6 0.8 %collective-permute-done.7.other_far_ref = bf16[272,256]{1,0:T(8,128)(2,1)S(1)} collective-permute-done((bf16[272,256]{1,0:T(8,128)(2,1)S(1)}, bf16[272,256]{1,0:T(8,128)(2,1)S(1)}, u32[]{:S(2)}, u32[]{:S(2)}) %collective-permute-start.7) | collective-permute-done | bytes 139296 | tf_op jit(solution)/shard_map/ppermute | solution.py:507
  23.4 0.4 group_blocks.1
  23.8 2.7 %collective-permute-start.8 = (f32[8,256]{1,0:T(8,128)S(1)}, f32[8,256]{1,0:T(8,128)S(1)}, u32[]{:S(2)}, u32[]{:S(2)}) collective-permute-start(f32[8,256]{1,0:T(8,128)S(1)} %get-tuple-element.31), channel_id=1, source_target_pairs={{0,16},{4,20},{8,24},{12,28},{16,0},{20,4},{24,8},{28,12},{1,17},{... | collective-permute-start | bytes 24584 | tf_op jit(solution)/shard_map/ppermute | solution.py:530
  26.4 0.0 collective-permute-done.9.maps_ref
  26.5 1.9 %collective-permute-done.8.refs_6_.received_ref = f32[8,256]{1,0:T(8,128)S(1)} collective-permute-done((f32[8,256]{1,0:T(8,128)S(1)}, f32[8,256]{1,0:T(8,128)S(1)}, u32[]{:S(2)}, u32[]{:S(2)}) %collective-permute-start.8) | collective-permute-done | bytes 8224 | tf_op jit(solution)/shard_map/ppermute | solution.py:530
  28.4 0.1 collective-permute-start.10
  28.5 0.0 collective-permute-done.3.refs_3_
  28.5 1.0 %pair_means.1.means_ref = f32[8,256]{1,0:T(8,128)S(1)} custom-call(f32[272,256]{1,0:T(8,128)S(1)} %get-tuple-element.26.own_ref.refs_0_, f32[272,256]{1,0:T(8,128)S(1)} %collective-permute-done.2.received_ref.refs_1_, f32[1,272,256]{2,1,0:T(8,128)S(1)} %get-tuple-element.27.refs_2_, f32[1,272,256]{2,1,0:T(8,128)S(1)} %collective-permute-done.3.refs_3_, ...), custom_call_target="tpu_custom_call" | custom-call | tf_op jit(solution)/shard_map/pair_means/pallas_call | solution.py:28
  29.5 0.3 collective-permute-done.10.other_ref
  29.8 0.2 rest_of_means.1.refs_0_
  30.0 2.7 %collective-permute-start.12 = (f32[8,256]{1,0:T(8,128)S(1)}, f32[8,256]{1,0:T(8,128)S(1)}, u32[]{:S(2)}, u32[]{:S(2)}) collective-permute-start(f32[8,256]{1,0:T(8,128)S(1)} %rest_of_means.1.refs_0_), channel_id=1, source_target_pairs={{0,16},{1,25},{2,18},{3,27},{4,20},{5,29},{6,22},{7,31},{8,24},{9,... | collective-permute-start | bytes 24584 | tf_op jit(solution)/shard_map/ppermute | solution.py:560
  32.7 1.6 %collective-permute-start.11 = (f32[8,256]{1,0:T(8,128)S(1)}, f32[8,256]{1,0:T(8,128)S(1)}, u32[]{:S(2)}, u32[]{:S(2)}) collective-permute-start(f32[8,256]{1,0:T(8,128)S(1)} %rest_of_means.1.refs_0_), channel_id=1, source_target_pairs={{0,8},{4,12},{8,0},{12,4},{16,24},{20,28},{24,16},{28,20},{1,9},{5... | collective-permute-start | bytes 24584 | tf_op jit(solution)/shard_map/ppermute | solution.py:561
  34.2 0.4 %collective-permute-done.12.refs_2_ = f32[8,256]{1,0:T(8,128)S(1)} collective-permute-done((f32[8,256]{1,0:T(8,128)S(1)}, f32[8,256]{1,0:T(8,128)S(1)}, u32[]{:S(2)}, u32[]{:S(2)}) %collective-permute-start.12) | collective-permute-done | bytes 8224 | tf_op jit(solution)/shard_map/ppermute | solution.py:560
  34.6 0.0 collective-permute-start.13
  34.6 1.7 %collective-permute-done.11.refs_1_ = f32[8,256]{1,0:T(8,128)S(1)} collective-permute-done((f32[8,256]{1,0:T(8,128)S(1)}, f32[8,256]{1,0:T(8,128)S(1)}, u32[]{:S(2)}, u32[]{:S(2)}) %collective-permute-start.11) | collective-permute-done | bytes 8224 | tf_op jit(solution)/shard_map/ppermute | solution.py:561
  36.4 0.0 collective-permute-done.13.refs_3_
  36.4 1.1 %predict.1 = bf16[32,4096]{1,0:T(8,128)(2,1)} custom-call(f32[8,256]{1,0:T(8,128)S(1)} %rest_of_means.1.refs_0_, f32[8,256]{1,0:T(8,128)S(1)} %collective-permute-done.11.refs_1_, f32[8,256]{1,0:T(8,128)S(1)} %collective-permute-done.12.refs_2_, f32[8,256]{1,0:T(8,128)S(1)} %collective-permute-done.13.refs_3_, bf16[256,4096]{1,0:T(8,128)(2,1)S(1)} %get-tuple-element.34.refs_4_), custom_call_target="tpu_custom_call" | custom-call | tf_op jit(solution)/shard_map/predict/pallas_call | solution.py:568
  (2 shorter events, 0.0 us)
Async XLA Ops:
  1.5 1.5 %collective-permute-start = (bf16[1,272,256]{2,1,0:T(8,128)(2,1)S(1)}, bf16[1,272,256]{2,1,0:T(8,128)(2,1)S(1)}, u32[]{:S(2)}, u32[]{:S(2)}) collective-permute-start(bf16[1,272,256]{2,1,0:T(8,128)(2,1)S(1)} %get-tuple-element.21), channel_id=1, source_target_pairs={{0,1},{1,0},{2,3},{3,2},{4,5},{5,4},{6,7},{7,6},{8,9},{9,8},{10,11... | collective-permute-start | bytes 417800 | tf_op jit(solution)/shard_map/ppermute | solution.py:483
  3.0 6.9 %collective-permute-start.1 = (bf16[1,272,256]{2,1,0:T(8,128)(2,1)S(1)}, bf16[1,272,256]{2,1,0:T(8,128)(2,1)S(1)}, u32[]{:S(2)}, u32[]{:S(2)}) collective-permute-start(bf16[1,272,256]{2,1,0:T(8,128)(2,1)S(1)} %get-tuple-element.23), channel_id=1, source_target_pairs={{0,2},{1,3},{2,0},{3,1},{4,6},{5,7},{6,4},{7,5},{8,10},{9,11},{10,... | collective-permute-start | bytes 417800 | tf_op jit(solution)/shard_map/ppermute | solution.py:487
  13.2 1.9 %collective-permute-start.2 = (f32[272,256]{1,0:T(8,128)S(1)}, f32[272,256]{1,0:T(8,128)S(1)}, u32[]{:S(2)}, u32[]{:S(2)}) collective-permute-start(f32[272,256]{1,0:T(8,128)S(1)} %get-tuple-element.26.own_ref.refs_0_), channel_id=1, source_target_pairs={{0,1},{1,0},{2,3},{3,2},{4,5},{5,4},{6,7},{7,6},{8,9},{9,8},{10,11... | collective-permute-start | bytes 835592 | tf_op jit(solution)/shard_map/ppermute | solution.py:501
  13.3 7.1 %collective-permute-start.4 = (bf16[272,256]{1,0:T(8,128)(2,1)S(1)}, bf16[272,256]{1,0:T(8,128)(2,1)S(1)}, u32[]{:S(2)}, u32[]{:S(2)}) collective-permute-start(bf16[272,256]{1,0:T(8,128)(2,1)S(1)} %get-tuple-element.28), channel_id=1, source_target_pairs={{0,4},{4,0},{8,12},{12,8},{16,20},{20,16},{24,28},{28,24},{1,5},{5... | collective-permute-start | bytes 417800 | tf_op jit(solution)/shard_map/ppermute | solution.py:502
  15.5 6.5 %collective-permute-start.6 = (bf16[272,256]{1,0:T(8,128)(2,1)S(1)}, bf16[272,256]{1,0:T(8,128)(2,1)S(1)}, u32[]{:S(2)}, u32[]{:S(2)}) collective-permute-start(bf16[272,256]{1,0:T(8,128)(2,1)S(1)} %block_map.1.own_ref), channel_id=1, source_target_pairs={{0,8},{1,13},{2,10},{3,15},{4,12},{5,9},{6,14},{7,11},{8,0},{9,5},... | collective-permute-start | bytes 417800 | tf_op jit(solution)/shard_map/ppermute | solution.py:505
  20.4 1.8 %collective-permute-start.5 = (bf16[272,256]{1,0:T(8,128)(2,1)S(1)}, bf16[272,256]{1,0:T(8,128)(2,1)S(1)}, u32[]{:S(2)}, u32[]{:S(2)}) collective-permute-start(bf16[272,256]{1,0:T(8,128)(2,1)S(1)} %collective-permute-done.4.last_ref.refs_4_), channel_id=1, source_target_pairs={{0,1},{1,0},{2,3},{3,2},{4,5},{5,4},{6,7},{7,6},{8,9},{9,8},{10,11... | collective-permute-start | bytes 417800 | tf_op jit(solution)/shard_map/ppermute | solution.py:506
  20.4 6.1 %collective-permute-start.9 = (bf16[1,272,256]{2,1,0:T(8,128)(2,1)S(1)}, bf16[1,272,256]{2,1,0:T(8,128)(2,1)S(1)}, u32[]{:S(2)}, u32[]{:S(2)}) collective-permute-start(bf16[1,272,256]{2,1,0:T(8,128)(2,1)S(1)} %get-tuple-element.33), channel_id=1, source_target_pairs={{0,4},{4,0},{8,12},{12,8},{16,20},{20,16},{24,28},{28,24},{1,5},{5... | collective-permute-start | bytes 417800 | tf_op jit(solution)/shard_map/ppermute | solution.py:503
  21.7 6.8 %collective-permute-start.3 = (f32[1,272,256]{2,1,0:T(8,128)S(1)}, f32[1,272,256]{2,1,0:T(8,128)S(1)}, u32[]{:S(2)}, u32[]{:S(2)}) collective-permute-start(f32[1,272,256]{2,1,0:T(8,128)S(1)} %get-tuple-element.27.refs_2_), channel_id=1, source_target_pairs={{0,1},{1,0},{2,3},{3,2},{4,5},{5,4},{6,7},{7,6},{8,9},{9,8},{10,11... | collective-permute-start | bytes 835592 | tf_op jit(solution)/shard_map/ppermute | solution.py:542
  22.0 1.4 %collective-permute-start.7 = (bf16[272,256]{1,0:T(8,128)(2,1)S(1)}, bf16[272,256]{1,0:T(8,128)(2,1)S(1)}, u32[]{:S(2)}, u32[]{:S(2)}) collective-permute-start(bf16[272,256]{1,0:T(8,128)(2,1)S(1)} %collective-permute-done.6.far_ref), channel_id=1, source_target_pairs={{0,1},{1,0},{2,3},{3,2},{4,5},{5,4},{6,7},{7,6},{8,9},{9,8},{10,11... | collective-permute-start | bytes 417800 | tf_op jit(solution)/shard_map/ppermute | solution.py:507
  23.8 4.6 %collective-permute-start.8 = (f32[8,256]{1,0:T(8,128)S(1)}, f32[8,256]{1,0:T(8,128)S(1)}, u32[]{:S(2)}, u32[]{:S(2)}) collective-permute-start(f32[8,256]{1,0:T(8,128)S(1)} %get-tuple-element.31), channel_id=1, source_target_pairs={{0,16},{4,20},{8,24},{12,28},{16,0},{20,4},{24,8},{28,12},{1,17},{... | collective-permute-start | bytes 24584 | tf_op jit(solution)/shard_map/ppermute | solution.py:530
  28.4 1.4 %collective-permute-start.10 = (bf16[1,272,256]{2,1,0:T(8,128)(2,1)S(1)}, bf16[1,272,256]{2,1,0:T(8,128)(2,1)S(1)}, u32[]{:S(2)}, u32[]{:S(2)}) collective-permute-start(bf16[1,272,256]{2,1,0:T(8,128)(2,1)S(1)} %hold.1.firsts_ref), channel_id=1, source_target_pairs={{0,1},{1,0},{2,3},{3,2},{4,5},{5,4},{6,7},{7,6},{8,9},{9,8},{10,11... | collective-permute-start | bytes 417800 | tf_op jit(solution)/shard_map/ppermute | solution.py:552
  30.0 4.6 %collective-permute-start.12 = (f32[8,256]{1,0:T(8,128)S(1)}, f32[8,256]{1,0:T(8,128)S(1)}, u32[]{:S(2)}, u32[]{:S(2)}) collective-permute-start(f32[8,256]{1,0:T(8,128)S(1)} %rest_of_means.1.refs_0_), channel_id=1, source_target_pairs={{0,16},{1,25},{2,18},{3,27},{4,20},{5,29},{6,22},{7,31},{8,24},{9,... | collective-permute-start | bytes 24584 | tf_op jit(solution)/shard_map/ppermute | solution.py:560
  32.7 3.7 %collective-permute-start.11 = (f32[8,256]{1,0:T(8,128)S(1)}, f32[8,256]{1,0:T(8,128)S(1)}, u32[]{:S(2)}, u32[]{:S(2)}) collective-permute-start(f32[8,256]{1,0:T(8,128)S(1)} %rest_of_means.1.refs_0_), channel_id=1, source_target_pairs={{0,8},{4,12},{8,0},{12,4},{16,24},{20,28},{24,16},{28,20},{1,9},{5... | collective-permute-start | bytes 24584 | tf_op jit(solution)/shard_map/ppermute | solution.py:561
  34.6 1.7 %collective-permute-start.13 = (f32[8,256]{1,0:T(8,128)S(1)}, f32[8,256]{1,0:T(8,128)S(1)}, u32[]{:S(2)}, u32[]{:S(2)}) collective-permute-start(f32[8,256]{1,0:T(8,128)S(1)} %collective-permute-done.12.refs_2_), channel_id=1, source_target_pairs={{0,1},{1,0},{2,3},{3,2},{4,5},{5,4},{6,7},{7,6},{8,9},{9,8},{10,11... | collective-permute-start | bytes 24584 | tf_op jit(solution)/shard_map/ppermute | solution.py:562

commit v9 on v8

--- a/solution.py
+++ b/solution.py
@@ -269,8 +269,14 @@
     return early, late
 
 
+def widened(block):
+    states = block.shape[1]
+    pad = jnp.zeros((15, states), F32)
+    return jnp.concatenate([block[:states].astype(F32), shift_of(block), pad], axis=0)
+
+
 def block_map(own_ref, received_ref, out_ref):
-    (early,), (late,) = in_order([own_ref[...]], [received_ref[...]])
+    (early,), (late,) = in_order([own_ref[...]], [widened(received_ref[...])])
     out_ref[...] = rounded(append(early, late))
 
 
@@ -372,8 +378,8 @@
     own_start = jnp.where(odd, between, mean)
     own = []
     sides = [
-        [firsts[i] for i in range(half - 1)] + [last[...]]
-        for firsts, last in ((own_firsts_ref, own_last_ref), (other_firsts_ref, own_other_ref))
+        [own_firsts_ref[i] for i in range(half - 1)] + [own_last_ref[...]],
+        [widened(other_firsts_ref[i]) for i in range(half - 1)] + [widened(own_other_ref[...])],
     ]
     for maps in in_order(*sides):
         start = own_start if not own else own[-1]
@@ -492,15 +498,15 @@
     rows = states + 16
     block = sds((rows, states), BF16)
     firsts = sds((half - 1, rows, states), BF16)
-    own_last, own_firsts, last, first_maps = call(
+    own_last, own_firsts, last, own_rounded = call(
         hour_maps,
         (sds((rows, states), F32), sds((half - 1, rows, states), F32), block, firsts),
         (total, received, prior, turned),
         "hour_maps",
     )
-    other_last = lax.ppermute(own_last, "site", swaps(hours, 1))
+    other_last = lax.ppermute(last, "site", swaps(hours, 1))
     last = lax.ppermute(last, "tm", swaps(blocks, 1))
-    first_maps = lax.ppermute(first_maps, "tm", swaps(blocks, 1))
+    first_maps = lax.ppermute(own_rounded, "tm", swaps(blocks, 1))
     own = call(block_map, block, (own_last, other_last), "block_map")
     far = lax.ppermute(own, ("tm", "site"), core_swaps(blocks, hours, 2, 3))
     others_last = lax.ppermute(last, "site", swaps(hours, 1))
@@ -539,7 +545,7 @@
         distances.append(distance)
         levels.append(received)
         distance *= 2
-    other_firsts = lax.ppermute(own_firsts, "site", swaps(hours, 1))
+    other_firsts = lax.ppermute(own_rounded, "site", swaps(hours, 1))
     means = call(
         functools.partial(pair_means, tuple(distances)),
         sds((2 * hours, states), F32),

time: 37.7 us -> 37.6 us (level)
  starting transfers between devices: 15.6 us -> 16 us
  waiting for transfers between devices: 11.1 us -> 10.7 us
  transfers between devices with their start and end apart: 14 -> 14, of which waited for: 9 -> 8; matrix products, arithmetic and copies ran while one was open for 0% -> 0% of each run, Pallas kernels for 12% -> 12%
where the time goes in v9:
time: 37.6 us; the launch traced here: 37.4 us
  starting transfers between devices  16 us (43%)
  Pallas kernels  10.7 us (28%)
  waiting for transfers between devices  10.7 us (28%)
    pallas_call x10, Pallas kernels, call(): pl.pallas_call(kernel, out_shape=outs, in_specs=[pl.BlockSpec(memory_spac...  9.53 us
    ppermute x1, waiting for transfers between devices, body(): last = lax.ppermute(last, 'tm', swaps(blocks, 1))  3.07 us
    ppermute x1, starting transfers between devices, body(): received = lax.ppermute(send, 'site', swaps(hours, distance))  2.91 us
    ppermute x1, starting transfers between devices, body(): received = lax.ppermute(shift, 'tm', swaps(blocks, distance))  2.65 us
    ppermute x1, starting transfers between devices, body(): far = lax.ppermute(means, ('tm', 'site'), core_swaps(blocks, hours, 4, 6))  2.65 us
    ppermute x1, waiting for transfers between devices, body(): received = lax.ppermute(shift, 'tm', swaps(blocks, distance))  1.96 us
    ppermute x1, starting transfers between devices, body(): last = lax.ppermute(last, 'tm', swaps(blocks, 1))  1.83 us
    ppermute x1, starting transfers between devices, body(): first_maps = lax.ppermute(own_rounded, 'tm', swaps(blocks, 1))  1.8 us
  transfers between devices with their start and end apart: 14, of which 8 were waited for; matrix products, arithmetic and copies ran while one was open for 0% of the time, Pallas kernels for 12%

profile of v9, /device:TPU:0, one launch (start us, length us, event | category | flops | bytes accessed | tf_op | source)
XLA Modules:
  0.0 37.4 jit_solution(10332950787353382296)
XLA Ops:
  0.0 1.5 %local_grams.1 = (f32[1,264,256]{2,1,0:T(8,128)S(1)}, bf16[1,272,256]{2,1,0:T(8,128)(2,1)S(1)}) custom-call(bf16[512,256]{1,0:T(8,128)(2,1)} %rows_hbm.1, bf16[512]{0:T(512)(128)(2,1)} %values_hbm.1, s32[512]{0:T(512)} %codes_hbm.1), custom_call_target="tpu_custom_call" | custom-call | tf_op jit(solution)/shard_map/local_grams/pallas_call | solution.py:28
  1.5 0.5 %collective-permute-start = (bf16[1,272,256]{2,1,0:T(8,128)(2,1)S(1)}, bf16[1,272,256]{2,1,0:T(8,128)(2,1)S(1)}, u32[]{:S(2)}, u32[]{:S(2)}) collective-permute-start(bf16[1,272,256]{2,1,0:T(8,128)(2,1)S(1)} %get-tuple-element.21), channel_id=1, source_target_pairs={{0,1},{1,0},{2,3},{3,2},{4,5},{5,4},{6,7},{7,6},{8,9},{9,8},{10,11... | collective-permute-start | bytes 417800 | tf_op jit(solution)/shard_map/ppermute | solution.py:489
  2.0 1.0 %collective-permute-done.received_ref = bf16[1,272,256]{2,1,0:T(8,128)(2,1)S(1)} collective-permute-done((bf16[1,272,256]{2,1,0:T(8,128)(2,1)S(1)}, bf16[1,272,256]{2,1,0:T(8,128)(2,1)S(1)}, u32[]{:S(2)}, u32[]{:S(2)}) %collective-permute-start) | collective-permute-done | bytes 139296 | tf_op jit(solution)/shard_map/ppermute | solution.py:489
  3.0 2.9 %collective-permute-start.1 = (bf16[1,272,256]{2,1,0:T(8,128)(2,1)S(1)}, bf16[1,272,256]{2,1,0:T(8,128)(2,1)S(1)}, u32[]{:S(2)}, u32[]{:S(2)}) collective-permute-start(bf16[1,272,256]{2,1,0:T(8,128)(2,1)S(1)} %get-tuple-element.23), channel_id=1, source_target_pairs={{0,2},{1,3},{2,0},{3,1},{4,6},{5,7},{6,4},{7,5},{8,10},{9,11},{10,... | collective-permute-start | bytes 417800 | tf_op jit(solution)/shard_map/ppermute | solution.py:493
  6.0 2.4 %prepare.1 = (f32[256,256]{1,0:T(8,128)S(1)}, f32[256,256]{1,0:T(8,128)S(1)}, bf16[256,4096]{1,0:T(8,128)(2,1)S(1)}) custom-call(f32[256,256]{1,0:T(8,128)} %prior_hbm.1, f32[256,256]{1,0:T(8,128)} %transition_hbm.1, bf16[4096,256]{1,0:T(8,128)(2,1)} %basis_hbm.1), custom_call_target="tpu_custom_call" | custom-call | tf_op jit(solution)/shard_map/prepare/pallas_call | solution.py:28
  8.4 1.5 %collective-permute-done.1.received_ref = bf16[1,272,256]{2,1,0:T(8,128)(2,1)S(1)} collective-permute-done((bf16[1,272,256]{2,1,0:T(8,128)(2,1)S(1)}, bf16[1,272,256]{2,1,0:T(8,128)(2,1)S(1)}, u32[]{:S(2)}, u32[]{:S(2)}) %collective-permute-start.1) | collective-permute-done | bytes 139296 | tf_op jit(solution)/shard_map/ppermute | solution.py:493
  9.9 3.3 %hour_maps.1 = (f32[272,256]{1,0:T(8,128)S(1)}, f32[1,272,256]{2,1,0:T(8,128)S(1)}, bf16[272,256]{1,0:T(8,128)(2,1)S(1)}, bf16[1,272,256]{2,1,0:T(8,128)(2,1)S(1)}) custom-call(f32[1,264,256]{2,1,0:T(8,128)S(1)} %get-tuple-element.22.sum_ref, bf16[1,272,256]{2,1,0:T(8,128)(2,1)S(1)} %collective-permute-done.1.received_ref, ...), custom_call_target="tpu_custom_call" | custom-call | tf_op jit(solution)/shard_map/hour_maps/pallas_call | solution.py:28
  13.2 0.1 collective-permute-start.2
  13.3 1.8 %collective-permute-start.4 = (bf16[272,256]{1,0:T(8,128)(2,1)S(1)}, bf16[272,256]{1,0:T(8,128)(2,1)S(1)}, u32[]{:S(2)}, u32[]{:S(2)}) collective-permute-start(bf16[272,256]{1,0:T(8,128)(2,1)S(1)} %get-tuple-element.27), channel_id=1, source_target_pairs={{0,4},{4,0},{8,12},{12,8},{16,20},{20,16},{24,28},{28,24},{1,5},{5... | collective-permute-start | bytes 417800 | tf_op jit(solution)/shard_map/ppermute | solution.py:508
  15.1 0.0 collective-permute-done.2.received_ref.refs_1_
  15.1 0.3 block_map.1.own_ref
  15.5 1.6 %collective-permute-start.6 = (bf16[272,256]{1,0:T(8,128)(2,1)S(1)}, bf16[272,256]{1,0:T(8,128)(2,1)S(1)}, u32[]{:S(2)}, u32[]{:S(2)}) collective-permute-start(bf16[272,256]{1,0:T(8,128)(2,1)S(1)} %block_map.1.own_ref), channel_id=1, source_target_pairs={{0,8},{1,13},{2,10},{3,15},{4,12},{5,9},{6,14},{7,11},{8,0},{9,5},... | collective-permute-start | bytes 417800 | tf_op jit(solution)/shard_map/ppermute | solution.py:511
  17.1 3.1 %collective-permute-done.4.last_ref.refs_4_ = bf16[272,256]{1,0:T(8,128)(2,1)S(1)} collective-permute-done((bf16[272,256]{1,0:T(8,128)(2,1)S(1)}, bf16[272,256]{1,0:T(8,128)(2,1)S(1)}, u32[]{:S(2)}, u32[]{:S(2)}) %collective-permute-start.4) | collective-permute-done | bytes 139296 | tf_op jit(solution)/shard_map/ppermute | solution.py:508
  20.2 0.0 collective-permute-start.5
  20.2 1.8 %collective-permute-start.9 = (bf16[1,272,256]{2,1,0:T(8,128)(2,1)S(1)}, bf16[1,272,256]{2,1,0:T(8,128)(2,1)S(1)}, u32[]{:S(2)}, u32[]{:S(2)}) collective-permute-start(bf16[1,272,256]{2,1,0:T(8,128)(2,1)S(1)} %get-tuple-element.29), channel_id=1, source_target_pairs={{0,4},{4,0},{8,12},{12,8},{16,20},{20,16},{24,28},{28,24},{1,5},{5... | collective-permute-start | bytes 417800 | tf_op jit(solution)/shard_map/ppermute | solution.py:509
  22.0 0.0 collective-permute-done.6.far_ref
  22.0 0.2 collective-permute-start.7
  22.2 0.0 collective-permute-done.5.other_last_ref.refs_5_
  22.2 0.4 %pair_block.1 = (bf16[272,256]{1,0:T(8,128)(2,1)S(1)}, f32[264,256]{1,0:T(8,128)S(1)}) custom-call(bf16[272,256]{1,0:T(8,128)(2,1)S(1)} %block_map.1.own_ref, bf16[272,256]{1,0:T(8,128)(2,1)S(1)} %collective-permute-done.4.last_ref.refs_4_, bf16[272,256]{1,0:T(8,128)(2,1)S(1)} %collective-permute-done.5.other_last_ref.refs_5_), custom_call_target="tpu_custom_call" | custom-call | flops 3000000000 | tf_op jit(solution)/shard_map/pair_block/pallas_call | solution.py:28
  22.6 0.7 %collective-permute-done.7.other_far_ref = bf16[272,256]{1,0:T(8,128)(2,1)S(1)} collective-permute-done((bf16[272,256]{1,0:T(8,128)(2,1)S(1)}, bf16[272,256]{1,0:T(8,128)(2,1)S(1)}, u32[]{:S(2)}, u32[]{:S(2)}) %collective-permute-start.7) | collective-permute-done | bytes 139296 | tf_op jit(solution)/shard_map/ppermute | solution.py:513
  23.3 0.4 group_blocks.1
  23.7 2.7 %collective-permute-start.8 = (f32[8,256]{1,0:T(8,128)S(1)}, f32[8,256]{1,0:T(8,128)S(1)}, u32[]{:S(2)}, u32[]{:S(2)}) collective-permute-start(f32[8,256]{1,0:T(8,128)S(1)} %get-tuple-element.32), channel_id=1, source_target_pairs={{0,16},{4,20},{8,24},{12,28},{16,0},{20,4},{24,8},{28,12},{1,17},{... | collective-permute-start | bytes 24584 | tf_op jit(solution)/shard_map/ppermute | solution.py:536
  26.4 0.0 collective-permute-start.3
  26.4 0.0 collective-permute-done.9.maps_ref
  26.4 2.0 %collective-permute-done.8.refs_6_.received_ref = f32[8,256]{1,0:T(8,128)S(1)} collective-permute-done((f32[8,256]{1,0:T(8,128)S(1)}, f32[8,256]{1,0:T(8,128)S(1)}, u32[]{:S(2)}, u32[]{:S(2)}) %collective-permute-start.8) | collective-permute-done | bytes 8224 | tf_op jit(solution)/shard_map/ppermute | solution.py:536
  28.3 0.1 collective-permute-start.10
  28.4 0.0 collective-permute-done.3.refs_3_
  28.4 1.0 %pair_means.1.means_ref = f32[8,256]{1,0:T(8,128)S(1)} custom-call(f32[272,256]{1,0:T(8,128)S(1)} %get-tuple-element.26.own_ref.refs_0_, bf16[272,256]{1,0:T(8,128)(2,1)S(1)} %collective-permute-done.2.received_ref.refs_1_, f32[1,272,256]{2,1,0:T(8,128)S(1)} %get-tuple-element.28.refs_2_, bf16[1,272,256]{2,1,0:T(8,128)(2,1)S(1)} %collective-permute-done.3.refs_3_, ...), custom_call_target="tpu_custom_call" | custom-call | tf_op jit(solution)/shard_map/pair_means/pallas_call | solution.py:28
  29.5 0.3 collective-permute-done.10.other_ref
  29.8 0.2 rest_of_means.1.refs_0_
  29.9 2.7 %collective-permute-start.12 = (f32[8,256]{1,0:T(8,128)S(1)}, f32[8,256]{1,0:T(8,128)S(1)}, u32[]{:S(2)}, u32[]{:S(2)}) collective-permute-start(f32[8,256]{1,0:T(8,128)S(1)} %rest_of_means.1.refs_0_), channel_id=1, source_target_pairs={{0,16},{1,25},{2,18},{3,27},{4,20},{5,29},{6,22},{7,31},{8,24},{9,... | collective-permute-start | bytes 24584 | tf_op jit(solution)/shard_map/ppermute | solution.py:566
  32.6 1.6 %collective-permute-start.11 = (f32[8,256]{1,0:T(8,128)S(1)}, f32[8,256]{1,0:T(8,128)S(1)}, u32[]{:S(2)}, u32[]{:S(2)}) collective-permute-start(f32[8,256]{1,0:T(8,128)S(1)} %rest_of_means.1.refs_0_), channel_id=1, source_target_pairs={{0,8},{4,12},{8,0},{12,4},{16,24},{20,28},{24,16},{28,20},{1,9},{5... | collective-permute-start | bytes 24584 | tf_op jit(solution)/shard_map/ppermute | solution.py:567
  34.2 0.4 %collective-permute-done.12.refs_2_ = f32[8,256]{1,0:T(8,128)S(1)} collective-permute-done((f32[8,256]{1,0:T(8,128)S(1)}, f32[8,256]{1,0:T(8,128)S(1)}, u32[]{:S(2)}, u32[]{:S(2)}) %collective-permute-start.12) | collective-permute-done | bytes 8224 | tf_op jit(solution)/shard_map/ppermute | solution.py:566
  34.6 0.0 collective-permute-start.13
  34.6 1.7 %collective-permute-done.11.refs_1_ = f32[8,256]{1,0:T(8,128)S(1)} collective-permute-done((f32[8,256]{1,0:T(8,128)S(1)}, f32[8,256]{1,0:T(8,128)S(1)}, u32[]{:S(2)}, u32[]{:S(2)}) %collective-permute-start.11) | collective-permute-done | bytes 8224 | tf_op jit(solution)/shard_map/ppermute | solution.py:567
  36.3 0.0 collective-permute-done.13.refs_3_
  36.3 1.1 %predict.1 = bf16[32,4096]{1,0:T(8,128)(2,1)} custom-call(f32[8,256]{1,0:T(8,128)S(1)} %rest_of_means.1.refs_0_, f32[8,256]{1,0:T(8,128)S(1)} %collective-permute-done.11.refs_1_, f32[8,256]{1,0:T(8,128)S(1)} %collective-permute-done.12.refs_2_, f32[8,256]{1,0:T(8,128)S(1)} %collective-permute-done.13.refs_3_, bf16[256,4096]{1,0:T(8,128)(2,1)S(1)} %get-tuple-element.34.refs_4_), custom_call_target="tpu_custom_call" | custom-call | tf_op jit(solution)/shard_map/predict/pallas_call | solution.py:574
  (2 shorter events, 0.0 us)
Async XLA Ops:
  1.5 1.5 %collective-permute-start = (bf16[1,272,256]{2,1,0:T(8,128)(2,1)S(1)}, bf16[1,272,256]{2,1,0:T(8,128)(2,1)S(1)}, u32[]{:S(2)}, u32[]{:S(2)}) collective-permute-start(bf16[1,272,256]{2,1,0:T(8,128)(2,1)S(1)} %get-tuple-element.21), channel_id=1, source_target_pairs={{0,1},{1,0},{2,3},{3,2},{4,5},{5,4},{6,7},{7,6},{8,9},{9,8},{10,11... | collective-permute-start | bytes 417800 | tf_op jit(solution)/shard_map/ppermute | solution.py:489
  3.0 6.9 %collective-permute-start.1 = (bf16[1,272,256]{2,1,0:T(8,128)(2,1)S(1)}, bf16[1,272,256]{2,1,0:T(8,128)(2,1)S(1)}, u32[]{:S(2)}, u32[]{:S(2)}) collective-permute-start(bf16[1,272,256]{2,1,0:T(8,128)(2,1)S(1)} %get-tuple-element.23), channel_id=1, source_target_pairs={{0,2},{1,3},{2,0},{3,1},{4,6},{5,7},{6,4},{7,5},{8,10},{9,11},{10,... | collective-permute-start | bytes 417800 | tf_op jit(solution)/shard_map/ppermute | solution.py:493
  13.2 1.9 %collective-permute-start.2 = (bf16[272,256]{1,0:T(8,128)(2,1)S(1)}, bf16[272,256]{1,0:T(8,128)(2,1)S(1)}, u32[]{:S(2)}, u32[]{:S(2)}) collective-permute-start(bf16[272,256]{1,0:T(8,128)(2,1)S(1)} %get-tuple-element.27), channel_id=1, source_target_pairs={{0,1},{1,0},{2,3},{3,2},{4,5},{5,4},{6,7},{7,6},{8,9},{9,8},{10,11... | collective-permute-start | bytes 417800 | tf_op jit(solution)/shard_map/ppermute | solution.py:507
  13.3 6.9 %collective-permute-start.4 = (bf16[272,256]{1,0:T(8,128)(2,1)S(1)}, bf16[272,256]{1,0:T(8,128)(2,1)S(1)}, u32[]{:S(2)}, u32[]{:S(2)}) collective-permute-start(bf16[272,256]{1,0:T(8,128)(2,1)S(1)} %get-tuple-element.27), channel_id=1, source_target_pairs={{0,4},{4,0},{8,12},{12,8},{16,20},{20,16},{24,28},{28,24},{1,5},{5... | collective-permute-start | bytes 417800 | tf_op jit(solution)/shard_map/ppermute | solution.py:508
  15.5 6.5 %collective-permute-start.6 = (bf16[272,256]{1,0:T(8,128)(2,1)S(1)}, bf16[272,256]{1,0:T(8,128)(2,1)S(1)}, u32[]{:S(2)}, u32[]{:S(2)}) collective-permute-start(bf16[272,256]{1,0:T(8,128)(2,1)S(1)} %block_map.1.own_ref), channel_id=1, source_target_pairs={{0,8},{1,13},{2,10},{3,15},{4,12},{5,9},{6,14},{7,11},{8,0},{9,5},... | collective-permute-start | bytes 417800 | tf_op jit(solution)/shard_map/ppermute | solution.py:511
  20.2 2.0 %collective-permute-start.5 = (bf16[272,256]{1,0:T(8,128)(2,1)S(1)}, bf16[272,256]{1,0:T(8,128)(2,1)S(1)}, u32[]{:S(2)}, u32[]{:S(2)}) collective-permute-start(bf16[272,256]{1,0:T(8,128)(2,1)S(1)} %collective-permute-done.4.last_ref.refs_4_), channel_id=1, source_target_pairs={{0,1},{1,0},{2,3},{3,2},{4,5},{5,4},{6,7},{7,6},{8,9},{9,8},{10,11... | collective-permute-start | bytes 417800 | tf_op jit(solution)/shard_map/ppermute | solution.py:512
  20.2 6.2 %collective-permute-start.9 = (bf16[1,272,256]{2,1,0:T(8,128)(2,1)S(1)}, bf16[1,272,256]{2,1,0:T(8,128)(2,1)S(1)}, u32[]{:S(2)}, u32[]{:S(2)}) collective-permute-start(bf16[1,272,256]{2,1,0:T(8,128)(2,1)S(1)} %get-tuple-element.29), channel_id=1, source_target_pairs={{0,4},{4,0},{8,12},{12,8},{16,20},{20,16},{24,28},{28,24},{1,5},{5... | collective-permute-start | bytes 417800 | tf_op jit(solution)/shard_map/ppermute | solution.py:509
  22.0 1.4 %collective-permute-start.7 = (bf16[272,256]{1,0:T(8,128)(2,1)S(1)}, bf16[272,256]{1,0:T(8,128)(2,1)S(1)}, u32[]{:S(2)}, u32[]{:S(2)}) collective-permute-start(bf16[272,256]{1,0:T(8,128)(2,1)S(1)} %collective-permute-done.6.far_ref), channel_id=1, source_target_pairs={{0,1},{1,0},{2,3},{3,2},{4,5},{5,4},{6,7},{7,6},{8,9},{9,8},{10,11... | collective-permute-start | bytes 417800 | tf_op jit(solution)/shard_map/ppermute | solution.py:513
  23.7 4.6 %collective-permute-start.8 = (f32[8,256]{1,0:T(8,128)S(1)}, f32[8,256]{1,0:T(8,128)S(1)}, u32[]{:S(2)}, u32[]{:S(2)}) collective-permute-start(f32[8,256]{1,0:T(8,128)S(1)} %get-tuple-element.32), channel_id=1, source_target_pairs={{0,16},{4,20},{8,24},{12,28},{16,0},{20,4},{24,8},{28,12},{1,17},{... | collective-permute-start | bytes 24584 | tf_op jit(solution)/shard_map/ppermute | solution.py:536
  26.4 2.1 %collective-permute-start.3 = (bf16[1,272,256]{2,1,0:T(8,128)(2,1)S(1)}, bf16[1,272,256]{2,1,0:T(8,128)(2,1)S(1)}, u32[]{:S(2)}, u32[]{:S(2)}) collective-permute-start(bf16[1,272,256]{2,1,0:T(8,128)(2,1)S(1)} %get-tuple-element.29), channel_id=1, source_target_pairs={{0,1},{1,0},{2,3},{3,2},{4,5},{5,4},{6,7},{7,6},{8,9},{9,8},{10,11... | collective-permute-start | bytes 417800 | tf_op jit(solution)/shard_map/ppermute | solution.py:548
  28.3 1.4 %collective-permute-start.10 = (bf16[1,272,256]{2,1,0:T(8,128)(2,1)S(1)}, bf16[1,272,256]{2,1,0:T(8,128)(2,1)S(1)}, u32[]{:S(2)}, u32[]{:S(2)}) collective-permute-start(bf16[1,272,256]{2,1,0:T(8,128)(2,1)S(1)} %hold.1.firsts_ref), channel_id=1, source_target_pairs={{0,1},{1,0},{2,3},{3,2},{4,5},{5,4},{6,7},{7,6},{8,9},{9,8},{10,11... | collective-permute-start | bytes 417800 | tf_op jit(solution)/shard_map/ppermute | solution.py:558
  29.9 4.6 %collective-permute-start.12 = (f32[8,256]{1,0:T(8,128)S(1)}, f32[8,256]{1,0:T(8,128)S(1)}, u32[]{:S(2)}, u32[]{:S(2)}) collective-permute-start(f32[8,256]{1,0:T(8,128)S(1)} %rest_of_means.1.refs_0_), channel_id=1, source_target_pairs={{0,16},{1,25},{2,18},{3,27},{4,20},{5,29},{6,22},{7,31},{8,24},{9,... | collective-permute-start | bytes 24584 | tf_op jit(solution)/shard_map/ppermute | solution.py:566
  32.6 3.7 %collective-permute-start.11 = (f32[8,256]{1,0:T(8,128)S(1)}, f32[8,256]{1,0:T(8,128)S(1)}, u32[]{:S(2)}, u32[]{:S(2)}) collective-permute-start(f32[8,256]{1,0:T(8,128)S(1)} %rest_of_means.1.refs_0_), channel_id=1, source_target_pairs={{0,8},{4,12},{8,0},{12,4},{16,24},{20,28},{24,16},{28,20},{1,9},{5... | collective-permute-start | bytes 24584 | tf_op jit(solution)/shard_map/ppermute | solution.py:567
  34.6 1.7 %collective-permute-start.13 = (f32[8,256]{1,0:T(8,128)S(1)}, f32[8,256]{1,0:T(8,128)S(1)}, u32[]{:S(2)}, u32[]{:S(2)}) collective-permute-start(f32[8,256]{1,0:T(8,128)S(1)} %collective-permute-done.12.refs_2_), channel_id=1, source_target_pairs={{0,1},{1,0},{2,3},{3,2},{4,5},{5,4},{6,7},{7,6},{8,9},{9,8},{10,11... | collective-permute-start | bytes 24584 | tf_op jit(solution)/shard_map/ppermute | solution.py:568

commit v10 on v9

--- a/solution.py
+++ b/solution.py
@@ -276,7 +276,7 @@
 
 
 def block_map(own_ref, received_ref, out_ref):
-    (early,), (late,) = in_order([own_ref[...]], [widened(received_ref[...])])
+    (early,), (late,) = in_order([own_ref[...]], [received_ref[...]])
     out_ref[...] = rounded(append(early, late))
 
 
@@ -379,7 +379,7 @@
     own = []
     sides = [
         [own_firsts_ref[i] for i in range(half - 1)] + [own_last_ref[...]],
-        [widened(other_firsts_ref[i]) for i in range(half - 1)] + [widened(own_other_ref[...])],
+        [widened(other_firsts_ref[i]) for i in range(half - 1)] + [own_other_ref[...]],
     ]
     for maps in in_order(*sides):
         start = own_start if not own else own[-1]
@@ -504,7 +504,7 @@
         (total, received, prior, turned),
         "hour_maps",
     )
-    other_last = lax.ppermute(last, "site", swaps(hours, 1))
+    other_last = lax.ppermute(own_last, "site", swaps(hours, 1))
     last = lax.ppermute(last, "tm", swaps(blocks, 1))
     first_maps = lax.ppermute(own_rounded, "tm", swaps(blocks, 1))
     own = call(block_map, block, (own_last, other_last), "block_map")

time: 37.6 us -> 37.6 us (level)
  starting transfers between devices: 16 us -> 15.2 us
  waiting for transfers between devices: 10.7 us -> 11.4 us
    ppermute x1, starting transfers between devices: 1.8 us -> 1.27 us  [body(): first_maps = lax.ppermute(own_rounded, 'tm', swaps(blocks, 1))]
  transfers between devices with their start and end apart: 14 -> 14, of which waited for: 8 -> 10; matrix products, arithmetic and copies ran while one was open for 0% -> 0% of each run, Pallas kernels for 12% -> 12%
where the time goes in v10:
time: 37.6 us; the launch traced here: 37.5 us
  starting transfers between devices  15.2 us (40%)
  waiting for transfers between devices  11.4 us (30%)
  Pallas kernels  10.7 us (28%)
    pallas_call x10, Pallas kernels, call(): pl.pallas_call(kernel, out_shape=outs, in_specs=[pl.BlockSpec(memory_spac...  9.55 us
    ppermute x1, waiting for transfers between devices, body(): last = lax.ppermute(last, 'tm', swaps(blocks, 1))  3.26 us
    ppermute x1, starting transfers between devices, body(): received = lax.ppermute(send, 'site', swaps(hours, distance))  2.91 us
    ppermute x1, starting transfers between devices, body(): received = lax.ppermute(shift, 'tm', swaps(blocks, distance))  2.66 us
    ppermute x1, starting transfers between devices, body(): far = lax.ppermute(means, ('tm', 'site'), core_swaps(blocks, hours, 4, 6))  2.66 us
    ppermute x1, waiting for transfers between devices, body(): received = lax.ppermute(shift, 'tm', swaps(blocks, distance))  1.89 us
    ppermute x1, starting transfers between devices, body(): last = lax.ppermute(last, 'tm', swaps(blocks, 1))  1.84 us
    ppermute x1, waiting for transfers between devices, body(): near = lax.ppermute(means, 'tm', swaps(blocks, 2))  1.73 us
  transfers between devices with their start and end apart: 14, of which 10 were waited for; matrix products, arithmetic and copies ran while one was open for 0% of the time, Pallas kernels for 12%

profile of v10, /device:TPU:0, one launch (start us, length us, event | category | flops | bytes accessed | tf_op | source)
XLA Modules:
  0.0 37.5 jit_solution(10768639711465157564)
XLA Ops:
  0.0 1.5 %local_grams.1 = (f32[1,264,256]{2,1,0:T(8,128)S(1)}, bf16[1,272,256]{2,1,0:T(8,128)(2,1)S(1)}) custom-call(bf16[512,256]{1,0:T(8,128)(2,1)} %rows_hbm.1, bf16[512]{0:T(512)(128)(2,1)} %values_hbm.1, s32[512]{0:T(512)} %codes_hbm.1), custom_call_target="tpu_custom_call" | custom-call | tf_op jit(solution)/shard_map/local_grams/pallas_call | solution.py:28
  1.5 0.5 %collective-permute-start = (bf16[1,272,256]{2,1,0:T(8,128)(2,1)S(1)}, bf16[1,272,256]{2,1,0:T(8,128)(2,1)S(1)}, u32[]{:S(2)}, u32[]{:S(2)}) collective-permute-start(bf16[1,272,256]{2,1,0:T(8,128)(2,1)S(1)} %get-tuple-element.21), channel_id=1, source_target_pairs={{0,1},{1,0},{2,3},{3,2},{4,5},{5,4},{6,7},{7,6},{8,9},{9,8},{10,11... | collective-permute-start | bytes 417800 | tf_op jit(solution)/shard_map/ppermute | solution.py:489
  2.0 1.0 %collective-permute-done.received_ref = bf16[1,272,256]{2,1,0:T(8,128)(2,1)S(1)} collective-permute-done((bf16[1,272,256]{2,1,0:T(8,128)(2,1)S(1)}, bf16[1,272,256]{2,1,0:T(8,128)(2,1)S(1)}, u32[]{:S(2)}, u32[]{:S(2)}) %collective-permute-start) | collective-permute-done | bytes 139296 | tf_op jit(solution)/shard_map/ppermute | solution.py:489
  3.0 2.9 %collective-permute-start.1 = (bf16[1,272,256]{2,1,0:T(8,128)(2,1)S(1)}, bf16[1,272,256]{2,1,0:T(8,128)(2,1)S(1)}, u32[]{:S(2)}, u32[]{:S(2)}) collective-permute-start(bf16[1,272,256]{2,1,0:T(8,128)(2,1)S(1)} %get-tuple-element.23), channel_id=1, source_target_pairs={{0,2},{1,3},{2,0},{3,1},{4,6},{5,7},{6,4},{7,5},{8,10},{9,11},{10,... | collective-permute-start | bytes 417800 | tf_op jit(solution)/shard_map/ppermute | solution.py:493
  6.0 2.4 %prepare.1 = (f32[256,256]{1,0:T(8,128)S(1)}, f32[256,256]{1,0:T(8,128)S(1)}, bf16[256,4096]{1,0:T(8,128)(2,1)S(1)}) custom-call(f32[256,256]{1,0:T(8,128)} %prior_hbm.1, f32[256,256]{1,0:T(8,128)} %transition_hbm.1, bf16[4096,256]{1,0:T(8,128)(2,1)} %basis_hbm.1), custom_call_target="tpu_custom_call" | custom-call | tf_op jit(solution)/shard_map/prepare/pallas_call | solution.py:28
  8.4 1.5 %collective-permute-done.1.received_ref = bf16[1,272,256]{2,1,0:T(8,128)(2,1)S(1)} collective-permute-done((bf16[1,272,256]{2,1,0:T(8,128)(2,1)S(1)}, bf16[1,272,256]{2,1,0:T(8,128)(2,1)S(1)}, u32[]{:S(2)}, u32[]{:S(2)}) %collective-permute-start.1) | collective-permute-done | bytes 139296 | tf_op jit(solution)/shard_map/ppermute | solution.py:493
  9.9 3.3 %hour_maps.1 = (f32[272,256]{1,0:T(8,128)S(1)}, f32[1,272,256]{2,1,0:T(8,128)S(1)}, bf16[272,256]{1,0:T(8,128)(2,1)S(1)}, bf16[1,272,256]{2,1,0:T(8,128)(2,1)S(1)}) custom-call(f32[1,264,256]{2,1,0:T(8,128)S(1)} %get-tuple-element.22.sum_ref, bf16[1,272,256]{2,1,0:T(8,128)(2,1)S(1)} %collective-permute-done.1.received_ref, ...), custom_call_target="tpu_custom_call" | custom-call | tf_op jit(solution)/shard_map/hour_maps/pallas_call | solution.py:28
  13.2 0.1 collective-permute-start.2
  13.3 1.8 %collective-permute-start.4 = (bf16[272,256]{1,0:T(8,128)(2,1)S(1)}, bf16[272,256]{1,0:T(8,128)(2,1)S(1)}, u32[]{:S(2)}, u32[]{:S(2)}) collective-permute-start(bf16[272,256]{1,0:T(8,128)(2,1)S(1)} %get-tuple-element.29), channel_id=1, source_target_pairs={{0,4},{4,0},{8,12},{12,8},{16,20},{20,16},{24,28},{28,24},{1,5},{5... | collective-permute-start | bytes 417800 | tf_op jit(solution)/shard_map/ppermute | solution.py:508
  15.1 0.0 collective-permute-done.2.received_ref.refs_1_
  15.1 0.3 block_map.1.own_ref
  15.5 1.6 %collective-permute-start.6 = (bf16[272,256]{1,0:T(8,128)(2,1)S(1)}, bf16[272,256]{1,0:T(8,128)(2,1)S(1)}, u32[]{:S(2)}, u32[]{:S(2)}) collective-permute-start(bf16[272,256]{1,0:T(8,128)(2,1)S(1)} %block_map.1.own_ref), channel_id=1, source_target_pairs={{0,8},{1,13},{2,10},{3,15},{4,12},{5,9},{6,14},{7,11},{8,0},{9,5},... | collective-permute-start | bytes 417800 | tf_op jit(solution)/shard_map/ppermute | solution.py:511
  17.1 3.3 %collective-permute-done.4.last_ref.refs_4_ = bf16[272,256]{1,0:T(8,128)(2,1)S(1)} collective-permute-done((bf16[272,256]{1,0:T(8,128)(2,1)S(1)}, bf16[272,256]{1,0:T(8,128)(2,1)S(1)}, u32[]{:S(2)}, u32[]{:S(2)}) %collective-permute-start.4) | collective-permute-done | bytes 139296 | tf_op jit(solution)/shard_map/ppermute | solution.py:508
  20.4 0.0 collective-permute-start.5
  20.4 1.3 %collective-permute-start.9 = (bf16[1,272,256]{2,1,0:T(8,128)(2,1)S(1)}, bf16[1,272,256]{2,1,0:T(8,128)(2,1)S(1)}, u32[]{:S(2)}, u32[]{:S(2)}) collective-permute-start(bf16[1,272,256]{2,1,0:T(8,128)(2,1)S(1)} %get-tuple-element.28), channel_id=1, source_target_pairs={{0,4},{4,0},{8,12},{12,8},{16,20},{20,16},{24,28},{28,24},{1,5},{5... | collective-permute-start | bytes 417800 | tf_op jit(solution)/shard_map/ppermute | solution.py:509
  21.7 0.4 collective-permute-done.6.far_ref
  22.0 0.0 collective-permute-start.7
  22.0 0.0 collective-permute-done.5.other_last_ref.refs_5_
  22.0 0.4 %pair_block.1 = (bf16[272,256]{1,0:T(8,128)(2,1)S(1)}, f32[264,256]{1,0:T(8,128)S(1)}) custom-call(bf16[272,256]{1,0:T(8,128)(2,1)S(1)} %block_map.1.own_ref, bf16[272,256]{1,0:T(8,128)(2,1)S(1)} %collective-permute-done.4.last_ref.refs_4_, bf16[272,256]{1,0:T(8,128)(2,1)S(1)} %collective-permute-done.5.other_last_ref.refs_5_), custom_call_target="tpu_custom_call" | custom-call | flops 3000000000 | tf_op jit(solution)/shard_map/pair_block/pallas_call | solution.py:28
  22.4 0.9 %collective-permute-done.7.other_far_ref = bf16[272,256]{1,0:T(8,128)(2,1)S(1)} collective-permute-done((bf16[272,256]{1,0:T(8,128)(2,1)S(1)}, bf16[272,256]{1,0:T(8,128)(2,1)S(1)}, u32[]{:S(2)}, u32[]{:S(2)}) %collective-permute-start.7) | collective-permute-done | bytes 139296 | tf_op jit(solution)/shard_map/ppermute | solution.py:513
  23.4 0.4 group_blocks.1
  23.7 2.7 %collective-permute-start.8 = (f32[8,256]{1,0:T(8,128)S(1)}, f32[8,256]{1,0:T(8,128)S(1)}, u32[]{:S(2)}, u32[]{:S(2)}) collective-permute-start(f32[8,256]{1,0:T(8,128)S(1)} %get-tuple-element.32), channel_id=1, source_target_pairs={{0,16},{4,20},{8,24},{12,28},{16,0},{20,4},{24,8},{28,12},{1,17},{... | collective-permute-start | bytes 24584 | tf_op jit(solution)/shard_map/ppermute | solution.py:536
  26.4 0.0 collective-permute-start.3
  26.4 0.1 collective-permute-done.9.maps_ref
  26.5 1.9 %collective-permute-done.8.refs_6_.received_ref = f32[8,256]{1,0:T(8,128)S(1)} collective-permute-done((f32[8,256]{1,0:T(8,128)S(1)}, f32[8,256]{1,0:T(8,128)S(1)}, u32[]{:S(2)}, u32[]{:S(2)}) %collective-permute-start.8) | collective-permute-done | bytes 8224 | tf_op jit(solution)/shard_map/ppermute | solution.py:536
  28.4 0.1 collective-permute-start.10
  28.4 0.0 collective-permute-done.3.refs_3_
  28.5 1.0 %pair_means.1.means_ref = f32[8,256]{1,0:T(8,128)S(1)} custom-call(f32[272,256]{1,0:T(8,128)S(1)} %get-tuple-element.26.own_ref.refs_0_, f32[272,256]{1,0:T(8,128)S(1)} %collective-permute-done.2.received_ref.refs_1_, f32[1,272,256]{2,1,0:T(8,128)S(1)} %get-tuple-element.27.refs_2_, bf16[1,272,256]{2,1,0:T(8,128)(2,1)S(1)} %collective-permute-done.3.refs_3_, ...), custom_call_target="tpu_custom_call" | custom-call | tf_op jit(solution)/shard_map/pair_means/pallas_call | solution.py:28
  29.5 0.3 collective-permute-done.10.other_ref
  29.8 0.2 rest_of_means.1.refs_0_
  30.0 2.7 %collective-permute-start.12 = (f32[8,256]{1,0:T(8,128)S(1)}, f32[8,256]{1,0:T(8,128)S(1)}, u32[]{:S(2)}, u32[]{:S(2)}) collective-permute-start(f32[8,256]{1,0:T(8,128)S(1)} %rest_of_means.1.refs_0_), channel_id=1, source_target_pairs={{0,16},{1,25},{2,18},{3,27},{4,20},{5,29},{6,22},{7,31},{8,24},{9,... | collective-permute-start | bytes 24584 | tf_op jit(solution)/shard_map/ppermute | solution.py:566
  32.6 1.6 %collective-permute-start.11 = (f32[8,256]{1,0:T(8,128)S(1)}, f32[8,256]{1,0:T(8,128)S(1)}, u32[]{:S(2)}, u32[]{:S(2)}) collective-permute-start(f32[8,256]{1,0:T(8,128)S(1)} %rest_of_means.1.refs_0_), channel_id=1, source_target_pairs={{0,8},{4,12},{8,0},{12,4},{16,24},{20,28},{24,16},{28,20},{1,9},{5... | collective-permute-start | bytes 24584 | tf_op jit(solution)/shard_map/ppermute | solution.py:567
  34.2 0.4 %collective-permute-done.12.refs_2_ = f32[8,256]{1,0:T(8,128)S(1)} collective-permute-done((f32[8,256]{1,0:T(8,128)S(1)}, f32[8,256]{1,0:T(8,128)S(1)}, u32[]{:S(2)}, u32[]{:S(2)}) %collective-permute-start.12) | collective-permute-done | bytes 8224 | tf_op jit(solution)/shard_map/ppermute | solution.py:566
  34.6 0.0 collective-permute-start.13
  34.6 1.7 %collective-permute-done.11.refs_1_ = f32[8,256]{1,0:T(8,128)S(1)} collective-permute-done((f32[8,256]{1,0:T(8,128)S(1)}, f32[8,256]{1,0:T(8,128)S(1)}, u32[]{:S(2)}, u32[]{:S(2)}) %collective-permute-start.11) | collective-permute-done | bytes 8224 | tf_op jit(solution)/shard_map/ppermute | solution.py:567
  36.3 0.0 collective-permute-done.13.refs_3_
  36.3 1.1 %predict.1 = bf16[32,4096]{1,0:T(8,128)(2,1)} custom-call(f32[8,256]{1,0:T(8,128)S(1)} %rest_of_means.1.refs_0_, f32[8,256]{1,0:T(8,128)S(1)} %collective-permute-done.11.refs_1_, f32[8,256]{1,0:T(8,128)S(1)} %collective-permute-done.12.refs_2_, f32[8,256]{1,0:T(8,128)S(1)} %collective-permute-done.13.refs_3_, bf16[256,4096]{1,0:T(8,128)(2,1)S(1)} %get-tuple-element.34.refs_4_), custom_call_target="tpu_custom_call" | custom-call | tf_op jit(solution)/shard_map/predict/pallas_call | solution.py:574
  (2 shorter events, 0.0 us)
Async XLA Ops:
  1.5 1.5 %collective-permute-start = (bf16[1,272,256]{2,1,0:T(8,128)(2,1)S(1)}, bf16[1,272,256]{2,1,0:T(8,128)(2,1)S(1)}, u32[]{:S(2)}, u32[]{:S(2)}) collective-permute-start(bf16[1,272,256]{2,1,0:T(8,128)(2,1)S(1)} %get-tuple-element.21), channel_id=1, source_target_pairs={{0,1},{1,0},{2,3},{3,2},{4,5},{5,4},{6,7},{7,6},{8,9},{9,8},{10,11... | collective-permute-start | bytes 417800 | tf_op jit(solution)/shard_map/ppermute | solution.py:489
  3.0 6.9 %collective-permute-start.1 = (bf16[1,272,256]{2,1,0:T(8,128)(2,1)S(1)}, bf16[1,272,256]{2,1,0:T(8,128)(2,1)S(1)}, u32[]{:S(2)}, u32[]{:S(2)}) collective-permute-start(bf16[1,272,256]{2,1,0:T(8,128)(2,1)S(1)} %get-tuple-element.23), channel_id=1, source_target_pairs={{0,2},{1,3},{2,0},{3,1},{4,6},{5,7},{6,4},{7,5},{8,10},{9,11},{10,... | collective-permute-start | bytes 417800 | tf_op jit(solution)/shard_map/ppermute | solution.py:493
  13.2 1.9 %collective-permute-start.2 = (f32[272,256]{1,0:T(8,128)S(1)}, f32[272,256]{1,0:T(8,128)S(1)}, u32[]{:S(2)}, u32[]{:S(2)}) collective-permute-start(f32[272,256]{1,0:T(8,128)S(1)} %get-tuple-element.26.own_ref.refs_0_), channel_id=1, source_target_pairs={{0,1},{1,0},{2,3},{3,2},{4,5},{5,4},{6,7},{7,6},{8,9},{9,8},{10,11... | collective-permute-start | bytes 835592 | tf_op jit(solution)/shard_map/ppermute | solution.py:507
  13.3 7.1 %collective-permute-start.4 = (bf16[272,256]{1,0:T(8,128)(2,1)S(1)}, bf16[272,256]{1,0:T(8,128)(2,1)S(1)}, u32[]{:S(2)}, u32[]{:S(2)}) collective-permute-start(bf16[272,256]{1,0:T(8,128)(2,1)S(1)} %get-tuple-element.29), channel_id=1, source_target_pairs={{0,4},{4,0},{8,12},{12,8},{16,20},{20,16},{24,28},{28,24},{1,5},{5... | collective-permute-start | bytes 417800 | tf_op jit(solution)/shard_map/ppermute | solution.py:508
  15.5 6.5 %collective-permute-start.6 = (bf16[272,256]{1,0:T(8,128)(2,1)S(1)}, bf16[272,256]{1,0:T(8,128)(2,1)S(1)}, u32[]{:S(2)}, u32[]{:S(2)}) collective-permute-start(bf16[272,256]{1,0:T(8,128)(2,1)S(1)} %block_map.1.own_ref), channel_id=1, source_target_pairs={{0,8},{1,13},{2,10},{3,15},{4,12},{5,9},{6,14},{7,11},{8,0},{9,5},... | collective-permute-start | bytes 417800 | tf_op jit(solution)/shard_map/ppermute | solution.py:511
  20.4 1.6 %collective-permute-start.5 = (bf16[272,256]{1,0:T(8,128)(2,1)S(1)}, bf16[272,256]{1,0:T(8,128)(2,1)S(1)}, u32[]{:S(2)}, u32[]{:S(2)}) collective-permute-start(bf16[272,256]{1,0:T(8,128)(2,1)S(1)} %collective-permute-done.4.last_ref.refs_4_), channel_id=1, source_target_pairs={{0,1},{1,0},{2,3},{3,2},{4,5},{5,4},{6,7},{7,6},{8,9},{9,8},{10,11... | collective-permute-start | bytes 417800 | tf_op jit(solution)/shard_map/ppermute | solution.py:512
  20.4 6.1 %collective-permute-start.9 = (bf16[1,272,256]{2,1,0:T(8,128)(2,1)S(1)}, bf16[1,272,256]{2,1,0:T(8,128)(2,1)S(1)}, u32[]{:S(2)}, u32[]{:S(2)}) collective-permute-start(bf16[1,272,256]{2,1,0:T(8,128)(2,1)S(1)} %get-tuple-element.28), channel_id=1, source_target_pairs={{0,4},{4,0},{8,12},{12,8},{16,20},{20,16},{24,28},{28,24},{1,5},{5... | collective-permute-start | bytes 417800 | tf_op jit(solution)/shard_map/ppermute | solution.py:509
  22.0 1.4 %collective-permute-start.7 = (bf16[272,256]{1,0:T(8,128)(2,1)S(1)}, bf16[272,256]{1,0:T(8,128)(2,1)S(1)}, u32[]{:S(2)}, u32[]{:S(2)}) collective-permute-start(bf16[272,256]{1,0:T(8,128)(2,1)S(1)} %collective-permute-done.6.far_ref), channel_id=1, source_target_pairs={{0,1},{1,0},{2,3},{3,2},{4,5},{5,4},{6,7},{7,6},{8,9},{9,8},{10,11... | collective-permute-start | bytes 417800 | tf_op jit(solution)/shard_map/ppermute | solution.py:513
  23.7 4.6 %collective-permute-start.8 = (f32[8,256]{1,0:T(8,128)S(1)}, f32[8,256]{1,0:T(8,128)S(1)}, u32[]{:S(2)}, u32[]{:S(2)}) collective-permute-start(f32[8,256]{1,0:T(8,128)S(1)} %get-tuple-element.32), channel_id=1, source_target_pairs={{0,16},{4,20},{8,24},{12,28},{16,0},{20,4},{24,8},{28,12},{1,17},{... | collective-permute-start | bytes 24584 | tf_op jit(solution)/shard_map/ppermute | solution.py:536
  26.4 2.1 %collective-permute-start.3 = (bf16[1,272,256]{2,1,0:T(8,128)(2,1)S(1)}, bf16[1,272,256]{2,1,0:T(8,128)(2,1)S(1)}, u32[]{:S(2)}, u32[]{:S(2)}) collective-permute-start(bf16[1,272,256]{2,1,0:T(8,128)(2,1)S(1)} %get-tuple-element.28), channel_id=1, source_target_pairs={{0,1},{1,0},{2,3},{3,2},{4,5},{5,4},{6,7},{7,6},{8,9},{9,8},{10,11... | collective-permute-start | bytes 417800 | tf_op jit(solution)/shard_map/ppermute | solution.py:548
  28.4 1.4 %collective-permute-start.10 = (bf16[1,272,256]{2,1,0:T(8,128)(2,1)S(1)}, bf16[1,272,256]{2,1,0:T(8,128)(2,1)S(1)}, u32[]{:S(2)}, u32[]{:S(2)}) collective-permute-start(bf16[1,272,256]{2,1,0:T(8,128)(2,1)S(1)} %hold.1.firsts_ref), channel_id=1, source_target_pairs={{0,1},{1,0},{2,3},{3,2},{4,5},{5,4},{6,7},{7,6},{8,9},{9,8},{10,11... | collective-permute-start | bytes 417800 | tf_op jit(solution)/shard_map/ppermute | solution.py:558
  30.0 4.6 %collective-permute-start.12 = (f32[8,256]{1,0:T(8,128)S(1)}, f32[8,256]{1,0:T(8,128)S(1)}, u32[]{:S(2)}, u32[]{:S(2)}) collective-permute-start(f32[8,256]{1,0:T(8,128)S(1)} %rest_of_means.1.refs_0_), channel_id=1, source_target_pairs={{0,16},{1,25},{2,18},{3,27},{4,20},{5,29},{6,22},{7,31},{8,24},{9,... | collective-permute-start | bytes 24584 | tf_op jit(solution)/shard_map/ppermute | solution.py:566
  32.6 3.7 %collective-permute-start.11 = (f32[8,256]{1,0:T(8,128)S(1)}, f32[8,256]{1,0:T(8,128)S(1)}, u32[]{:S(2)}, u32[]{:S(2)}) collective-permute-start(f32[8,256]{1,0:T(8,128)S(1)} %rest_of_means.1.refs_0_), channel_id=1, source_target_pairs={{0,8},{4,12},{8,0},{12,4},{16,24},{20,28},{24,16},{28,20},{1,9},{5... | collective-permute-start | bytes 24584 | tf_op jit(solution)/shard_map/ppermute | solution.py:567
  34.6 1.8 %collective-permute-start.13 = (f32[8,256]{1,0:T(8,128)S(1)}, f32[8,256]{1,0:T(8,128)S(1)}, u32[]{:S(2)}, u32[]{:S(2)}) collective-permute-start(f32[8,256]{1,0:T(8,128)S(1)} %collective-permute-done.12.refs_2_), channel_id=1, source_target_pairs={{0,1},{1,0},{2,3},{3,2},{4,5},{5,4},{6,7},{7,6},{8,9},{9,8},{10,11... | collective-permute-start | bytes 24584 | tf_op jit(solution)/shard_map/ppermute | solution.py:568
